TPU v7x, 32 devices: a whole 2x2x4 slice. The times are simulated.
32 devices in a mesh: dp: 8 (over z, x), rep: 4 (over y, core).
Axes of the slice: x: 2, y: 2, z: 4, core: 2. Of those that a mesh axis runs over, the one named last changes fastest.
Arguments:
- page_pool: bfloat16 [3584, 64, 576], P(('rep', 'dp')), parts along dimension 0, may hold values from -12 to 12
- move_source: int32 [768, 1], P('rep'), parts along dimension 0, may hold values from 0 to 7; in each aligned block of 24 rows (0 to 23, 24 to 47, ...) at most 5 rows name the same one
- move_page: int32 [768], P('rep'), parts along dimension 0, may hold values from 0 to 111
- move_slot: int32 [768], P('rep'), parts along dimension 0, may hold values from 0 to 111, as said below
- row_count: int32 [32], P(('rep', 'dp')), parts along dimension 0, may hold values from 1 to 16, as said below
- lengths: int32 [512], P(('rep', 'dp')), parts along dimension 0, may hold values from 1 to 2048, as said below
- page_table: int32 [512, 32], P(('rep', 'dp')), parts along dimension 0, may hold values from 0 to 111
- queries: bfloat16 [512, 64, 576], P(('rep', 'dp')), parts along dimension 0, may hold values from -32 to 32
- value_up: bfloat16 [64, 512, 128], P('dp'), may hold values from -0.25 to 0.25
- out_proj: bfloat16 [8192, 7168], P('dp'), may hold values from -0.375 to 0.375
- residual: bfloat16 [512, 7168], P(('rep', 'dp')), parts along dimension 0, may hold values from -6 to 6
- norm_gain: float32 [7168], replicated, may hold values from 0.1 to 1.9
- gate_proj: bfloat16 [7168, 9216], P(None, 'dp'), may hold values from -0.0625 to 0.0625
- up_proj: bfloat16 [7168, 9216], P(None, 'dp'), may hold values from -0.0625 to 0.0625
- down_proj: bfloat16 [9216, 7168], P('dp'), may hold values from -0.0625 to 0.0625
Outputs:
- layer_out: bfloat16 [512, 7168], P(('rep', 'dp')), parts along dimension 0
There are 4 independent parts, one for each index of `rep`. A program takes and returns all parts, laid end to end along the dimension named above; an argument that names none is the same for every part. Nothing has to cross between parts.
Inputs may be any that keep to these rules, and one draw needn't show every extreme that they name: `move_source`: within the 24 moves of one destination rank, no source rank appears more than 5 times, and some source appears exactly 5 times. `move_slot`: the 24 slots of one destination rank are distinct. `row_count`: some rank has exactly 16 live rows. `lengths`: some row has exactly 2048 tokens.
All inputs are finite; a program needn't handle non-finite values.
Results may differ from a plain program's by a relative error of at most 0.02.
Values may be sent and summed in bfloat16 or wider, within the bound.
No kernel may reach another device: no remote copies, remote signals or barrier semaphores. Data moves between devices by JAX's collectives and lax.ppermute only.
A program may use at most 128 MiB of HBM per device.

v0:
```python
import jax
import jax.numpy as jnp
from jax import lax
from jax.sharding import PartitionSpec as P

LATENT = 512


SOFTMAX_SCALE = 192 ** (-0.5)


def rms_scale(values, gain_row):
    factor = lax.rsqrt(jnp.mean(values * values, axis=-1, keepdims=True) + 1e-06)
    return (values * factor * gain_row).astype(jnp.bfloat16)


def attend_rows(cache_pages, tables, row_lens, queries, valid_rows):

    def one_row(inputs):
        table_row, row_len, query_row = inputs
        tokens = cache_pages[table_row].reshape(-1, cache_pages.shape[2])
        scores = (
            jnp.einsum("hk,tk->ht", query_row, tokens, preferred_element_type=jnp.float32)
            * SOFTMAX_SCALE
        )
        live_mask = jnp.arange(tokens.shape[0]) < row_len
        scores = jnp.where(live_mask[None, :], scores, -jnp.inf)
        top_score = jnp.max(scores, axis=1, keepdims=True)
        exponent = jnp.exp(scores - top_score)
        weights = (exponent / jnp.sum(exponent, axis=1, keepdims=True)).astype(jnp.bfloat16)
        return jnp.einsum(
            "ht,tl->hl", weights, tokens[:, :LATENT], preferred_element_type=jnp.float32
        ).astype(jnp.bfloat16)

    outputs = lax.map(one_row, (tables, row_lens, queries))
    return jnp.where(valid_rows[:, None, None], outputs, jnp.zeros_like(outputs))


def body(
    page_pool,
    move_source,
    move_page,
    move_slot,
    row_count,
    lengths,
    page_table,
    queries,
    value_up,
    out_proj,
    residual,
    norm_gain,
    gate_proj,
    up_proj,
    down_proj,
):
    rank_count = lax.axis_size("dp")
    own_rank = lax.axis_index("dp")
    move_count = move_page.shape[0] // rank_count
    capacity = max(2, (3 * move_count + 2 * rank_count - 1) // (2 * rank_count))
    sources = move_source.reshape(rank_count, move_count)
    page_ids = move_page.reshape(rank_count, move_count)
    slot_ids = move_slot.reshape(rank_count, move_count)
    move_order = jnp.arange(move_count)
    earlier = (sources[:, :, None] == sources[:, None, :]) & (
        move_order[None, None, :] < move_order[None, :, None]
    )
    arrival = jnp.sum(earlier.astype(jnp.int32), axis=2)
    chosen = (sources == own_rank)[:, :, None] & (
        arrival[:, :, None] == jnp.arange(capacity)[None, None, :]
    )
    send_ids = jnp.sum(jnp.where(chosen, page_ids[:, :, None], 0), axis=1)
    page_size = page_pool.shape[1]
    feature_width = page_pool.shape[2]
    outgoing = page_pool[send_ids.reshape(-1)].reshape(
        rank_count, capacity, page_size, feature_width
    )
    incoming = lax.all_to_all(outgoing, "dp", split_axis=0, concat_axis=0, tiled=True)
    own_sources = lax.dynamic_index_in_dim(sources, own_rank, 0, keepdims=False)
    own_arrival = lax.dynamic_index_in_dim(arrival, own_rank, 0, keepdims=False)
    own_slots = lax.dynamic_index_in_dim(slot_ids, own_rank, 0, keepdims=False)
    picked = incoming.reshape(rank_count * capacity, page_size, feature_width)[
        own_sources * capacity + own_arrival
    ]
    local_pool = page_pool.at[own_slots].set(picked)
    rows_local = residual.shape[0]
    valid_rows = jnp.arange(rows_local) < row_count[0]
    latent_out = attend_rows(local_pool, page_table, lengths, queries, valid_rows)
    by_head = lax.all_to_all(latent_out, "dp", split_axis=1, concat_axis=0, tiled=True)
    head_out = jnp.einsum(
        "rhl,hlv->rhv", by_head, value_up, preferred_element_type=jnp.float32
    ).astype(jnp.bfloat16)
    head_out = head_out.reshape(head_out.shape[0], -1)
    rows_slice = head_out
    attention = lax.psum_scatter(
        jnp.dot(rows_slice, out_proj, preferred_element_type=jnp.float32).astype(jnp.bfloat16),
        "dp",
        scatter_dimension=0,
        tiled=True,
    ).astype(jnp.float32)
    middle = residual.astype(jnp.float32) + attention
    normed = rms_scale(middle, norm_gain)
    row_piece = lax.all_gather(normed, "dp", axis=0, tiled=True)
    gate_part = jnp.dot(row_piece, gate_proj, preferred_element_type=jnp.float32)
    up_part = jnp.dot(row_piece, up_proj, preferred_element_type=jnp.float32)
    hidden = (jax.nn.silu(gate_part) * up_part).astype(jnp.bfloat16)
    rows_slice = hidden
    mlp_out = lax.psum_scatter(
        jnp.dot(rows_slice, down_proj, preferred_element_type=jnp.float32).astype(jnp.bfloat16),
        "dp",
        scatter_dimension=0,
        tiled=True,
    ).astype(jnp.float32)
    return (middle + mlp_out).astype(jnp.bfloat16)


def solution(mesh):
    in_specs = (
        P(("rep", "dp"), None, None),
        P("rep", None),
        P("rep"),
        P("rep"),
        P(("rep", "dp")),
        P(("rep", "dp")),
        P(("rep", "dp"), None),
        P(("rep", "dp"), None, None),
        P("dp", None, None),
        P("dp", None),
        P(("rep", "dp"), None),
        P(),
        P(None, "dp"),
        P(None, "dp"),
        P("dp", None),
    )
    out_specs = P(("rep", "dp"), None)
    return jax.shard_map(body, mesh=mesh, in_specs=in_specs, out_specs=out_specs, check_vma=False)
```

profile of v0, /device:TPU:0, one launch (start us, length us, event | category | flops | bytes accessed | tf_op | source)
XLA Modules:
  0.0 558.8 jit_solution(5294071896678537733)
XLA Ops:
  6.5 8.1 %copy.40 = bf16[112,64,576]{2,1,0:T(8,128)(2,1)} copy(bf16[112,64,576]{2,1,0:T(8,128)(2,1)} %param.17) | data formatting | bytes 16515072
  16.8 6.5 %gather_fusion.1 = bf16[40,64,576]{2,1,0:T(8,128)(2,1)} fusion(bf16[112,64,576]{2,1,0:T(8,128)(2,1)} %copy.40, s32[1024]{0:T(1024)S(1)} %pad_clamp_fusion.2), kind=kCustom, calls=%fused_computation.1 | custom fusion | bytes 5898400 | tf_op jit(solution)/shard_map/gather | solution.py:74
  23.3 7.4 %all-to-all-start = ((bf16[8,5,64,576]{3,2,1,0:T(8,128)(2,1)}), bf16[8,5,64,576]{3,2,1,0:T(8,128)(2,1)}, u32[]{:S(2)}, u32[]{:S(2)}) async-start(bf16[8,5,64,576]{3,2,1,0:T(8,128)(2,1)} %bitcast.74), calls=%async_computation | async-start | bytes 6553600 | tf_op jit(solution)/shard_map/all_to_all | solution.py:77
  31.5 72.8 %all-to-all-done = bf16[8,5,64,576]{3,2,1,0:T(8,128)(2,1)} async-done(((bf16[8,5,64,576]{3,2,1,0:T(8,128)(2,1)}), bf16[8,5,64,576]{3,2,1,0:T(8,128)(2,1)}, u32[]{:S(2)}, u32[]{:S(2)}) %all-to-all-start) | async-done | bytes 2949152 | tf_op jit(solution)/shard_map/all_to_all | solution.py:77
  104.3 2.8 gather_fusion.2
  107.2 5.6 %scatter_fusion = bf16[112,64,576]{2,1,0:T(8,128)(2,1)} fusion(bf16[112,64,576]{2,1,0:T(8,128)(2,1)} %copy.40, s32[24]{0:T(128)S(1)} %get-tuple-element.65, bf16[24,64,576]{2,1,0:T(8,128)(2,1)S(1)} %gather_fusion.2), kind=kCustom, calls=%fused_computation.3 | custom fusion | bytes 5308512 | tf_op jit(solution)/shard_map/scatter | solution.py:84
  112.8 196.8 %while.10 = (s32[]{:T(128)}, bf16[16,64,512]{2,1,0:T(8,128)(2,1)}, s32[16]{0:T(128)S(1)}, bf16[16,64,576]{2,1,0:T(8,128)(2,1)}, s32[16,32]{1,0:T(8,128)}, /*index=5*/bf16[112,64,576]{2,1,0:T(8,128)(2,1)}, s32[]{:T(128)}) while((s32[]{:T(128)}, bf16[16,64,512]{2,1,0:T(8,128)(2,1)}, s32[16]{0:T(128)S(1)}, bf16[16,64,576]{2,1,0:T(8,128)(2,1)}, ...), condition=%wide.region_6.7_spmd, body=%wide.region_3.6_spmd.sunk | while | flops 286297056 | bytes 20606332 | solution.py:35
  113.5 5.9 %gather_fusion = bf16[32,64,576]{2,1,0:T(8,128)(2,1)} fusion(bf16[112,64,576]{2,1,0:T(8,128)(2,1)} %get-tuple-element.126, s32[1024]{0:T(1024)S(1)} %pad_clamp_fusion.4), kind=kCustom, calls=%fused_computation.clone.1 | custom fusion | bytes 4718720 | tf_op jit(solution)/shard_map/while/body/eval_jaxpr/gather | solution.py:21
  120.9 2.8 fusion.50
  124.0 1.2 fusion.52
  125.8 5.9 %gather_fusion = bf16[32,64,576]{2,1,0:T(8,128)(2,1)} fusion(bf16[112,64,576]{2,1,0:T(8,128)(2,1)} %get-tuple-element.126, s32[1024]{0:T(1024)S(1)} %pad_clamp_fusion.4), kind=kCustom, calls=%fused_computation.clone.1 | custom fusion | bytes 4718720 | tf_op jit(solution)/shard_map/while/body/eval_jaxpr/gather | solution.py:21
  133.2 2.8 fusion.50
  136.3 1.2 fusion.52
  138.1 5.9 %gather_fusion = bf16[32,64,576]{2,1,0:T(8,128)(2,1)} fusion(bf16[112,64,576]{2,1,0:T(8,128)(2,1)} %get-tuple-element.126, s32[1024]{0:T(1024)S(1)} %pad_clamp_fusion.4), kind=kCustom, calls=%fused_computation.clone.1 | custom fusion | bytes 4718720 | tf_op jit(solution)/shard_map/while/body/eval_jaxpr/gather | solution.py:21
  145.5 2.8 fusion.50
  148.6 1.2 fusion.52
  150.4 5.9 %gather_fusion = bf16[32,64,576]{2,1,0:T(8,128)(2,1)} fusion(bf16[112,64,576]{2,1,0:T(8,128)(2,1)} %get-tuple-element.126, s32[1024]{0:T(1024)S(1)} %pad_clamp_fusion.4), kind=kCustom, calls=%fused_computation.clone.1 | custom fusion | bytes 4718720 | tf_op jit(solution)/shard_map/while/body/eval_jaxpr/gather | solution.py:21
  157.8 2.8 fusion.50
  160.9 1.2 fusion.52
  162.7 5.9 %gather_fusion = bf16[32,64,576]{2,1,0:T(8,128)(2,1)} fusion(bf16[112,64,576]{2,1,0:T(8,128)(2,1)} %get-tuple-element.126, s32[1024]{0:T(1024)S(1)} %pad_clamp_fusion.4), kind=kCustom, calls=%fused_computation.clone.1 | custom fusion | bytes 4718720 | tf_op jit(solution)/shard_map/while/body/eval_jaxpr/gather | solution.py:21
  170.1 2.8 fusion.50
  175.0 5.9 %gather_fusion = bf16[32,64,576]{2,1,0:T(8,128)(2,1)} fusion(bf16[112,64,576]{2,1,0:T(8,128)(2,1)} %get-tuple-element.126, s32[1024]{0:T(1024)S(1)} %pad_clamp_fusion.4), kind=kCustom, calls=%fused_computation.clone.1 | custom fusion | bytes 4718720 | tf_op jit(solution)/shard_map/while/body/eval_jaxpr/gather | solution.py:21
  182.4 2.8 fusion.50
  185.4 1.2 fusion.52
  187.3 5.9 %gather_fusion = bf16[32,64,576]{2,1,0:T(8,128)(2,1)} fusion(bf16[112,64,576]{2,1,0:T(8,128)(2,1)} %get-tuple-element.126, s32[1024]{0:T(1024)S(1)} %pad_clamp_fusion.4), kind=kCustom, calls=%fused_computation.clone.1 | custom fusion | bytes 4718720 | tf_op jit(solution)/shard_map/while/body/eval_jaxpr/gather | solution.py:21
  194.7 2.8 fusion.50
  197.7 1.2 fusion.52
  199.6 5.9 %gather_fusion = bf16[32,64,576]{2,1,0:T(8,128)(2,1)} fusion(bf16[112,64,576]{2,1,0:T(8,128)(2,1)} %get-tuple-element.126, s32[1024]{0:T(1024)S(1)} %pad_clamp_fusion.4), kind=kCustom, calls=%fused_computation.clone.1 | custom fusion | bytes 4718720 | tf_op jit(solution)/shard_map/while/body/eval_jaxpr/gather | solution.py:21
  207.0 2.8 fusion.50
  211.9 5.9 %gather_fusion = bf16[32,64,576]{2,1,0:T(8,128)(2,1)} fusion(bf16[112,64,576]{2,1,0:T(8,128)(2,1)} %get-tuple-element.126, s32[1024]{0:T(1024)S(1)} %pad_clamp_fusion.4), kind=kCustom, calls=%fused_computation.clone.1 | custom fusion | bytes 4718720 | tf_op jit(solution)/shard_map/while/body/eval_jaxpr/gather | solution.py:21
  219.2 2.8 fusion.50
  222.3 1.2 fusion.52
  224.2 5.9 %gather_fusion = bf16[32,64,576]{2,1,0:T(8,128)(2,1)} fusion(bf16[112,64,576]{2,1,0:T(8,128)(2,1)} %get-tuple-element.126, s32[1024]{0:T(1024)S(1)} %pad_clamp_fusion.4), kind=kCustom, calls=%fused_computation.clone.1 | custom fusion | bytes 4718720 | tf_op jit(solution)/shard_map/while/body/eval_jaxpr/gather | solution.py:21
  231.6 2.8 fusion.50
  234.6 1.2 fusion.52
  236.5 5.9 %gather_fusion = bf16[32,64,576]{2,1,0:T(8,128)(2,1)} fusion(bf16[112,64,576]{2,1,0:T(8,128)(2,1)} %get-tuple-element.126, s32[1024]{0:T(1024)S(1)} %pad_clamp_fusion.4), kind=kCustom, calls=%fused_computation.clone.1 | custom fusion | bytes 4718720 | tf_op jit(solution)/shard_map/while/body/eval_jaxpr/gather | solution.py:21
  243.9 2.8 fusion.50
  246.9 1.2 fusion.52
  248.8 5.9 %gather_fusion = bf16[32,64,576]{2,1,0:T(8,128)(2,1)} fusion(bf16[112,64,576]{2,1,0:T(8,128)(2,1)} %get-tuple-element.126, s32[1024]{0:T(1024)S(1)} %pad_clamp_fusion.4), kind=kCustom, calls=%fused_computation.clone.1 | custom fusion | bytes 4718720 | tf_op jit(solution)/shard_map/while/body/eval_jaxpr/gather | solution.py:21
  256.1 2.8 fusion.50
  259.2 1.2 fusion.52
  261.1 5.9 %gather_fusion = bf16[32,64,576]{2,1,0:T(8,128)(2,1)} fusion(bf16[112,64,576]{2,1,0:T(8,128)(2,1)} %get-tuple-element.126, s32[1024]{0:T(1024)S(1)} %pad_clamp_fusion.4), kind=kCustom, calls=%fused_computation.clone.1 | custom fusion | bytes 4718720 | tf_op jit(solution)/shard_map/while/body/eval_jaxpr/gather | solution.py:21
  268.4 2.8 fusion.50
  271.5 1.2 fusion.52
  273.4 5.9 %gather_fusion = bf16[32,64,576]{2,1,0:T(8,128)(2,1)} fusion(bf16[112,64,576]{2,1,0:T(8,128)(2,1)} %get-tuple-element.126, s32[1024]{0:T(1024)S(1)} %pad_clamp_fusion.4), kind=kCustom, calls=%fused_computation.clone.1 | custom fusion | bytes 4718720 | tf_op jit(solution)/shard_map/while/body/eval_jaxpr/gather | solution.py:21
  280.7 2.8 fusion.50
  283.8 1.2 fusion.52
  285.7 5.9 %gather_fusion = bf16[32,64,576]{2,1,0:T(8,128)(2,1)} fusion(bf16[112,64,576]{2,1,0:T(8,128)(2,1)} %get-tuple-element.126, s32[1024]{0:T(1024)S(1)} %pad_clamp_fusion.4), kind=kCustom, calls=%fused_computation.clone.1 | custom fusion | bytes 4718720 | tf_op jit(solution)/shard_map/while/body/eval_jaxpr/gather | solution.py:21
  293.0 2.8 fusion.50
  296.1 1.2 fusion.52
  298.0 5.9 %gather_fusion = bf16[32,64,576]{2,1,0:T(8,128)(2,1)} fusion(bf16[112,64,576]{2,1,0:T(8,128)(2,1)} %get-tuple-element.126, s32[1024]{0:T(1024)S(1)} %pad_clamp_fusion.4), kind=kCustom, calls=%fused_computation.clone.1 | custom fusion | bytes 4718720 | tf_op jit(solution)/shard_map/while/body/eval_jaxpr/gather | solution.py:21
  305.3 2.8 fusion.50
  308.4 1.2 fusion.52
  309.6 1.8 copy_select_fusion
  311.4 29.6 %all_to_all.23 = bf16[16,64,512]{2,0,1:T(8,128)(2,1)S(1)} all-to-all(bf16[16,64,512]{2,0,1:T(8,128)(2,1)S(1)} %copy_select_fusion), channel_id=1, replica_groups=mesh['dp'=8,'rep'=4] {'dp'}, dimensions={1} | all-to-all | bytes 2097152 | tf_op jit(solution)/shard_map/all_to_all | solution.py:88
  341.6 8.6 %convolution_convert_fusion.1 = bf16[128,7168]{1,0:T(8,128)(2,1)} fusion(bf16[128,1024]{0,1:T(8,128)(2,1)S(1)} %bitcast.77, bf16[1024,7168]{1,0:T(8,128)(2,1)} %param.26), kind=kOutput, calls=%fused_computation.26 | convolution fusion | flops 1879965696 | bytes 16777216 | tf_op jit(solution)/shard_map/dot_general | solution.py:95
  350.4 65.3 %reduce-scatter.3.cloned.1.call-done = bf16[16,7168]{1,0:T(8,128)(2,1)} async-done(((bf16[128,7168]{1,0:T(8,128)(2,1)}), bf16[16,7168]{1,0:T(8,128)(2,1)}) %reduce-scatter.3.cloned.1.call-update) | async-done | bytes 229392 | tf_op jit(solution)/shard_map/reduce_scatter | solution.py:94
  416.8 1.7 multiply_convert_fusion
  418.8 45.0 %all-gather.2.cloned.1.call-done = bf16[128,7168]{1,0:T(8,128)(2,1)} async-done(((bf16[16,7168]{1,0:T(8,128)(2,1)}), bf16[128,7168]{1,0:T(8,128)(2,1)}) %all-gather.2.cloned.1.call-update) | async-done | bytes 1835024 | tf_op jit(solution)/shard_map/all_gather | solution.py:102
  463.8 8.9 %fusion.29 = f32[128,1152]{1,0:T(8,128)S(1)} fusion(bf16[128,7168]{1,0:T(8,128)(2,1)} %all-gather.2.cloned.1.call-done, bf16[7168,1152]{1,0:T(8,128)(2,1)} %param.29), kind=kOutput, calls=%fused_computation.58 | convolution fusion | flops 2113929216 | bytes 18939904 | tf_op jit(solution)/shard_map/dot_general | solution.py:103
  472.8 8.6 %fusion.20 = bf16[128,1152]{1,0:T(8,128)(2,1)S(1)} fusion(bf16[128,7168]{1,0:T(8,128)(2,1)S(1)} %copy-done.3, bf16[7168,1152]{1,0:T(8,128)(2,1)} %param.30, f32[128,1152]{1,0:T(8,128)S(1)} %fusion.29), kind=kOutput, calls=%fused_computation.28 | convolution fusion | flops 2114813952 | bytes 19234816 | tf_op jit(solution)/shard_map/dot_general | solution.py:104
  481.5 3.8 convolution_convert_fusion
  485.3 65.3 %reduce-scatter.5.cloned.1.call-done = bf16[16,7168]{1,0:T(8,128)(2,1)} async-done(((bf16[128,7168]{1,0:T(8,128)(2,1)}), bf16[16,7168]{1,0:T(8,128)(2,1)}) %reduce-scatter.5.cloned.1.call-update) | async-done | bytes 229392 | tf_op jit(solution)/shard_map/reduce_scatter | solution.py:107
  550.6 1.7 add_convert_fusion
  (170 shorter events, 44.5 us)
Async XLA Ops:
  6.5 334.6 %copy-start = (bf16[8,512,128]{2,1,0:T(8,128)(2,1)S(1)}, bf16[8,512,128]{2,1,0:T(8,128)(2,1)}, u32[]{:S(2)}) copy-start(bf16[8,512,128]{2,1,0:T(8,128)(2,1)} %param.25) | copy-start | bytes 3145732
  6.5 8.7 %copy-start.9 = (s32[192,1]{0,1:T(1,128)S(1)}, s32[192,1]{0,1:T(1,128)}, u32[]{:S(2)}) copy-start(s32[192,1]{0,1:T(1,128)} %param.18) | copy-start | bytes 2308
  6.5 9.8 %copy-start.7 = (s32[192]{0:T(256)S(1)}, s32[192]{0:T(256)}, u32[]{:S(2)}) copy-start(s32[192]{0:T(256)} %param.19) | copy-start | bytes 2308
  23.3 7.4 %copy-start.8 = (s32[192]{0:T(256)S(1)}, s32[192]{0:T(256)}, u32[]{:S(2)}) copy-start(s32[192]{0:T(256)} %param.20) | copy-start | bytes 2308
  23.3 81.0 %all-to-all-start = ((bf16[8,5,64,576]{3,2,1,0:T(8,128)(2,1)}), bf16[8,5,64,576]{3,2,1,0:T(8,128)(2,1)}, u32[]{:S(2)}, u32[]{:S(2)}) async-start(bf16[8,5,64,576]{3,2,1,0:T(8,128)(2,1)} %bitcast.74), calls=%async_computation | async-start | bytes 6553600 | tf_op jit(solution)/shard_map/all_to_all | solution.py:77
  30.7 385.0 %reduce-scatter.3.cloned.1.call-start = ((), (), s32[]{:S(2)}) async-start(), calls=%async_computation.4 | async-start | bytes 2064384 | tf_op jit(solution)/shard_map/reduce_scatter | solution.py:94
  107.2 5.7 %copy-start.10 = (s32[16]{0:T(128)S(1)}, s32[16]{0:T(128)}, u32[]{:S(2)}) copy-start(s32[16]{0:T(128)} %param.22) | copy-start | bytes 196
  119.5 4.5 copy-start.2
  131.8 4.5 copy-start.2
  144.1 4.5 copy-start.2
  156.4 4.5 copy-start.2
  168.6 4.5 copy-start.2
  180.9 4.5 copy-start.2
  193.2 4.5 copy-start.2
  205.5 4.5 copy-start.2
  217.8 4.5 copy-start.2
  230.1 4.5 copy-start.2
  242.4 4.5 copy-start.2
  254.7 4.5 copy-start.2
  267.0 4.5 copy-start.2
  279.3 4.5 copy-start.2
  291.6 4.5 copy-start.2
  303.9 4.5 copy-start.2
  341.6 74.1 %copy-start.4 = (bf16[16,7168]{1,0:T(8,128)(2,1)S(1)}, bf16[16,7168]{1,0:T(8,128)(2,1)}, u32[]{:S(2)}) copy-start(bf16[16,7168]{1,0:T(8,128)(2,1)} %param.27) | copy-start | bytes 688132
  341.6 75.2 %copy-start.6 = (f32[7168]{0:T(1024)S(1)}, f32[7168]{0:T(1024)}, u32[]{:S(2)}) copy-start(f32[7168]{0:T(1024)} %param.28) | copy-start | bytes 86020
  350.3 113.5 %all-gather.2.cloned.1.call-start = ((), (), s32[]{:S(2)}) async-start(), calls=%async_computation.5 | async-start | bytes 2064384 | tf_op jit(solution)/shard_map/all_gather | solution.py:102
  418.6 132.0 %reduce-scatter.5.cloned.1.call-start = ((), (), s32[]{:S(2)}) async-start(), calls=%async_computation.6 | async-start | bytes 2064384 | tf_op jit(solution)/shard_map/reduce_scatter | solution.py:107
  463.8 9.0 %copy-start.3 = (bf16[128,7168]{1,0:T(8,128)(2,1)S(1)}, bf16[128,7168]{1,0:T(8,128)(2,1)}, u32[]{:S(2)}) copy-start(bf16[128,7168]{1,0:T(8,128)(2,1)} %all-gather.2.cloned.1.call-done) | copy-start | bytes 5505028
  463.8 17.6 %slice-start = ((s8[16515072]{0:T(1024)(128)(4,1)}), s8[4194304]{0:T(1024)(128)(4,1)S(1)}, s32[]{:S(2)}) async-start(s8[16515072]{0:T(1024)(128)(4,1)} %bitcast.72), calls=%async_computation.7 | async-start | bytes 8388608
  463.8 17.6 %slice-start.1 = ((s8[16515072]{0:T(1024)(128)(4,1)}), s8[4194304]{0:T(1024)(128)(4,1)S(1)}, s32[]{:S(2)}) async-start(s8[16515072]{0:T(1024)(128)(4,1)} %bitcast.72), calls=%async_computation.8 | async-start | bytes 8388608
  472.8 8.6 %slice-start.2 = ((s8[16515072]{0:T(1024)(128)(4,1)}), s8[4194304]{0:T(1024)(128)(4,1)S(1)}, s32[]{:S(2)}) async-start(s8[16515072]{0:T(1024)(128)(4,1)} %bitcast.72), calls=%async_computation.9 | async-start | bytes 8388608
  472.8 8.6 %slice-start.3 = ((s8[16515072]{0:T(1024)(128)(4,1)}), s8[3932160]{0:T(1024)(128)(4,1)S(1)}, s32[]{:S(2)}) async-start(s8[16515072]{0:T(1024)(128)(4,1)} %bitcast.72), calls=%async_computation.10 | async-start | bytes 7864320
  481.4 69.2 %copy-start.5 = (bf16[16,7168]{1,0:T(8,128)(2,1)S(1)}, bf16[16,7168]{1,0:T(8,128)(2,1)}, u32[]{:S(2)}) copy-start(bf16[16,7168]{1,0:T(8,128)(2,1)} %reduce-scatter.3.cloned.1.call-done) | copy-start | bytes 688132
  481.4 70.9 %copy-start.1 = (bf16[8,512,128]{2,1,0:T(8,128)(2,1)S(1)}, bf16[8,512,128]{2,1,0:T(8,128)(2,1)}, u32[]{:S(2)}) copy-start(bf16[8,512,128]{2,1,0:T(8,128)(2,1)} %param.25) | copy-start | bytes 3145732
Sparse Core Ops, SparseCore 0:
  350.4 65.2 reduce-scatter.2
  418.7 45.0 all-gather.1
  485.4 65.1 reduce-scatter.4
where the time goes:
time: 561 us; the launch traced here: 559 us
  waiting for transfers between devices  248 us (44%)
  local copies, waits for them, and re-layouts  129 us (23%)
  matrix products  94 us (17%)
  other arithmetic  35.2 us (6%)
  blocking collectives  29.6 us (5%)
  between operations  14 us (2%)
  starting transfers between devices  7.68 us (1%)
    gather x16, local copies, waits for them, and re-layouts, one_row(): tokens = cache_pages[table_row].reshape(-1, cache_pages.shape[2])  94.9 us
    all_to_all x1, waiting for transfers between devices, body(): lax.all_to_all(outgoing, 'dp', split_axis=0, concat_axis=0, tiled=True)  72.8 us
    reduce_scatter x1, waiting for transfers between devices, body(): lax.psum_scatter(jnp.dot(rows_slice, out_proj, preferred_element_type=jnp...  65.3 us
    reduce_scatter x1, waiting for transfers between devices, body(): lax.psum_scatter(jnp.dot(rows_slice, down_proj, preferred_element_type=jn...  65.3 us
    dot_general x16, matrix products, one_row(): jnp.einsum('hk,tk->ht', query_row, tokens, preferred_element_type=jnp.flo...  45.1 us
    all_gather x1, waiting for transfers between devices, body(): row_piece = lax.all_gather(normed, 'dp', axis=0, tiled=True)  45 us
    all_to_all x1, blocking collectives, body(): lax.all_to_all(latent_out, 'dp', split_axis=1, concat_axis=0, tiled=True)  29.6 us
    dot_general x16, matrix products, one_row(): jnp.einsum('ht,tl->hl', weights, tokens[:, :LATENT], preferred_element_ty...  18.5 us
  transfers between devices with their start and end apart: 4, of which 4 were waited for; matrix products, arithmetic and copies ran while one was open for 0% of the time, Pallas kernels for 0%

commit v1 on v0

v1 whole, which is shorter than its diff:
```python
import functools
import math

import jax
import jax.numpy as jnp
from jax import lax
from jax.experimental import pallas as pl
from jax.experimental.pallas import tpu as pltpu
from jax.sharding import PartitionSpec as P

LATENT = 512
SOFTMAX_SCALE = 192 ** (-0.5)
LOG2_SCALE = SOFTMAX_SCALE * math.log2(math.e)
MASKED = -1e30
MIB = 1 << 20
CHUNKS = 2


def in_hbm(array):
    return pltpu.with_memory_space_constraint(array, pltpu.HBM)


def in_vmem(array):
    return pltpu.with_memory_space_constraint(array, pltpu.VMEM)


def pack_kernel(peers, near, capacity, ids_ref, rank_ref, pool_ref, _, *refs):
    out_refs, (pages_ref, sems) = refs[:-2], refs[-2:]
    if near:
        out_refs = [out_refs[0].at[k] for k in range(len(peers))]
    own = rank_ref[0]
    page_size = pages_ref.shape[1]
    half = page_size // 2
    slots = [(k, c) for k in range(len(peers)) for c in range(capacity)]

    def copy(n):
        k, c = slots[n]
        peer = (own & ~(len(peers) - 1)) + k if near else own ^ peers[k]
        page = ids_ref[peer * capacity + c]
        return pltpu.make_async_copy(pool_ref.at[page], pages_ref.at[n], sems.at[n])

    for n in range(len(slots)):
        copy(n).start()
    for n, (k, c) in enumerate(slots):
        copy(n).wait()
        for block in range(LATENT // 128):
            out_refs[k][c, pl.ds(block * page_size, page_size), :] = pages_ref[
                n, :, pl.ds(block * 128, 128)
            ]
        rope = pages_ref[n, :, LATENT:]
        out_refs[k][c, pl.ds(LATENT // 128 * page_size, half), :] = jnp.concatenate(
            [rope[:half], rope[half:]], axis=1
        )


def pack_pages(page_pool, ids, rank, peers, near, capacity, after):
    page_size, width = page_pool.shape[1:]
    shape = (capacity, page_size * width // 128, 128)
    count = len(peers) * capacity
    shapes = [(len(peers),) + shape] if near else [shape] * len(peers)
    return pl.pallas_call(
        functools.partial(pack_kernel, tuple(peers), near, capacity),
        out_shape=[jax.ShapeDtypeStruct(shape, page_pool.dtype) for shape in shapes],
        grid_spec=pltpu.PrefetchScalarGridSpec(
            num_scalar_prefetch=2,
            grid=(),
            in_specs=[pl.BlockSpec(memory_space=pltpu.HBM), pl.BlockSpec(memory_space=pl.ANY)],
            out_specs=[pl.BlockSpec(memory_space=pltpu.VMEM)] * len(shapes),
            scratch_shapes=[
                pltpu.VMEM((count, page_size, width), page_pool.dtype),
                pltpu.SemaphoreType.DMA((count,)),
            ],
        ),
        compiler_params=pltpu.CompilerParams(vmem_limit_bytes=16 * MIB),
        name="pack_near" if near else "pack_far",
    )(ids, rank, in_hbm(page_pool), after)


def unpack_pages(packed_refs, tokens_ref, page_size):
    half = page_size // 2
    width = tokens_ref.shape[1] - LATENT
    at = 0
    for packed_ref in packed_refs:
        for c in range(packed_ref.shape[0]):
            span = pl.ds(at, page_size)
            for block in range(LATENT // 128):
                tokens_ref[span, pl.ds(block * 128, 128)] = packed_ref[
                    c, pl.ds(block * page_size, page_size), :
                ]
            rope = packed_ref[c, pl.ds(LATENT // 128 * page_size, half), :]
            tokens_ref[span, LATENT:] = jnp.concatenate([rope[:, :width], rope[:, width:]], axis=0)
            at += page_size


def token_bias(counts, first_page, tokens, page_size):
    whole, last, part = counts
    rows, slots = whole.shape
    shift = page_size.bit_length() - 1
    page = (lax.broadcasted_iota(jnp.int32, (slots, tokens), 1) >> shift) + first_page
    spread = jnp.where(
        page == lax.broadcasted_iota(jnp.int32, (slots, tokens), 0), 1.0, 0.0
    ).astype(jnp.bfloat16)
    times = jnp.dot(whole, spread, preferred_element_type=jnp.float32)
    ends = jnp.dot(last, spread, preferred_element_type=jnp.float32)
    offset = lax.broadcasted_iota(jnp.int32, (rows, tokens), 1) & (page_size - 1)
    times = times + jnp.where(offset < part, ends, 0.0)
    return jnp.where(times > 0.5, jnp.log2(jnp.maximum(times, 1.0)), MASKED)


def absorb(raw, tokens, bias, state):
    top, total, acc = state
    rows, count = bias.shape
    scores = (raw.reshape(-1, rows, count) * LOG2_SCALE + bias[None]).reshape(-1, count)
    new_top = jnp.maximum(top, jnp.max(scores, axis=1, keepdims=True))
    weights = jnp.exp2(scores - new_top)
    shrink = jnp.exp2(top - new_top)
    total = total * shrink + jnp.sum(weights, axis=1, keepdims=True)
    acc = acc * shrink + jnp.dot(
        weights.astype(jnp.bfloat16), tokens[:, :LATENT], preferred_element_type=jnp.float32
    )
    return new_top, total, acc


def attend(q_ref, tokens, bias, states):
    size = q_ref.shape[0] // len(states)
    raw = [
        lax.dot_general(
            q_ref[pl.ds(i * size, size), :],
            tokens,
            (((1,), (1,)), ((), ())),
            preferred_element_type=jnp.float32,
        )
        for i in range(len(states))
    ]
    return [absorb(scores, tokens, bias, state) for scores, state in zip(raw, states)]


PARTS = 2


def store_state(states, refs):
    stats_ref, acc_ref = refs
    half = stats_ref.shape[1] // 2
    for i, (top, total, acc) in enumerate(states):
        span = pl.ds(i * acc.shape[0], acc.shape[0])
        stats_ref[span, :] = jnp.concatenate(
            [jnp.broadcast_to(x, (x.shape[0], half)) for x in (top, total)], axis=1
        )
        acc_ref[span, :] = acc


def load_state(refs):
    stats_ref, acc_ref = refs
    half = stats_ref.shape[1] // 2
    size = acc_ref.shape[0] // PARTS
    spans = [pl.ds(i * size, size) for i in range(PARTS)]
    return [
        (stats_ref[span, :1], stats_ref[span, half : half + 1], acc_ref[span, :]) for span in spans
    ]


def counts_of(refs):
    return tuple(ref[...] for ref in refs)


def resident_kernel(
    chunk, page_size, whole_ref, last_ref, part_ref, q_ref, pool_ref, *refs
):
    state_refs, (tokens_ref, bias_ref, sem) = refs[:2], refs[2:]
    token_count = tokens_ref.shape[0]
    count = q_ref.shape[0] // PARTS

    @pl.when(pl.program_id(0) == 0)
    def _():
        copy = pltpu.make_async_copy(pool_ref, tokens_ref, sem)
        copy.start()
        counts = counts_of((whole_ref, last_ref, part_ref))
        for first in range(0, token_count, chunk):
            bias_ref[:, pl.ds(first, chunk)] = token_bias(
                counts, first // page_size, chunk, page_size
            )
        copy.wait()

    def step(index, state):
        span = pl.ds(pl.multiple_of(index * chunk, chunk), chunk)
        return attend(q_ref, tokens_ref[span, :], bias_ref[:, span], state)

    empty = (
        jnp.full((count, 1), MASKED, jnp.float32),
        jnp.zeros((count, 1), jnp.float32),
        jnp.zeros((count, LATENT), jnp.float32),
    )
    states = lax.fori_loop(0, token_count // chunk, step, [empty] * PARTS)
    store_state(states, state_refs)


def state_layout(count, group, block):
    widths = (128, LATENT)
    shapes = tuple(pltpu.HBM((count, w), jnp.float32) for w in widths)
    specs = tuple(pl.BlockSpec((group, w), block) for w in widths)
    return shapes, specs


def attend_resident(queries, pool, counts, page_size, group=512, chunk=1024):
    count, width = queries.shape
    token_count = pool.shape[0]
    rows = counts[0].shape[0]
    block = lambda g: (g, 0)
    fixed = lambda g: (0, 0)
    shapes, specs = state_layout(count, group, block)
    return pl.pallas_call(
        functools.partial(resident_kernel, chunk, page_size),
        out_shape=shapes,
        grid=(count // group,),
        in_specs=[pl.BlockSpec(array.shape, fixed) for array in counts]
        + [pl.BlockSpec((group, width), block), pl.BlockSpec(memory_space=pltpu.HBM)],
        out_specs=specs,
        scratch_shapes=[
            pltpu.VMEM((token_count, width), pool.dtype),
            pltpu.VMEM((rows, token_count), jnp.float32),
            pltpu.SemaphoreType.DMA,
        ],
        compiler_params=pltpu.CompilerParams(vmem_limit_bytes=32 * MIB),
        cost_estimate=pl.CostEstimate(
            flops=2 * count * token_count * (width + LATENT),
            bytes_accessed=2 * token_count * width + 4 * count * LATENT,
            transcendentals=count * token_count,
        ),
        name="attend_resident",
    )(*counts, queries, in_hbm(pool))


def near_kernel(pages, place, page_size, whole_ref, last_ref, part_ref, q_ref, *refs):
    packed_refs, refs = refs[:pages], refs[pages:]
    before, after, (tokens_ref, bias_ref) = refs[:2], refs[2:4], refs[4:]

    @pl.when(pl.program_id(0) == 0)
    def _():
        unpack_pages(packed_refs, tokens_ref, page_size)
        counts = counts_of((whole_ref, last_ref, part_ref))
        bias_ref[...] = token_bias(counts, place, tokens_ref.shape[0], page_size)

    store_state(attend(q_ref, tokens_ref[...], bias_ref[...], load_state(before)), after)


def arrival_operands(packed, counts, fixed):
    once = pl.Buffered(1)
    count_specs = [pl.BlockSpec(array.shape, fixed) for array in counts]
    page_specs = [
        pl.BlockSpec(p.shape, lambda *_: (0, 0, 0), pipeline_mode=once) for p in packed
    ]
    tokens = sum(p.shape[0] for p in packed)
    return count_specs, page_specs, tokens


def attend_near(queries, packed, counts, place, state, page_size, group=512):
    count, width = queries.shape
    block = lambda g: (g, 0)
    count_specs, page_specs, pages = arrival_operands(packed, counts, lambda g: (0, 0))
    tokens = pages * page_size
    shapes, specs = state_layout(count, group, block)
    return pl.pallas_call(
        functools.partial(near_kernel, len(packed), place, page_size),
        out_shape=shapes,
        grid=(count // group,),
        in_specs=count_specs + [pl.BlockSpec((group, width), block)] + page_specs + list(specs),
        out_specs=specs,
        scratch_shapes=[
            pltpu.VMEM((tokens, width), queries.dtype),
            pltpu.VMEM((counts[0].shape[0], tokens), jnp.float32),
        ],
        compiler_params=pltpu.CompilerParams(vmem_limit_bytes=24 * MIB),
        cost_estimate=pl.CostEstimate(
            flops=2 * count * tokens * (width + LATENT),
            bytes_accessed=2 * tokens * width + 8 * count * LATENT,
            transcendentals=count * tokens,
        ),
        name="attend_near",
    )(*counts, queries, *packed, *map(in_hbm, state))


def latents_of(limit_ref, q_ref, tokens, bias, before):
    states = attend(q_ref, tokens, bias, load_state(before))
    latent = jnp.concatenate([acc / total for _, total, acc in states], axis=0)
    latent = latent.reshape(-1, bias.shape[0], LATENT)
    live = lax.broadcasted_iota(jnp.int32, latent.shape, 1) < limit_ref[0]
    return jnp.where(live, latent, 0.0).reshape(-1, LATENT).astype(jnp.bfloat16)


def latents_far_kernel(pages, place, page_size, rank_ref, limit_ref, *refs):
    count_refs, q_ref, refs = refs[:3], refs[3], refs[4:]
    packed_refs, before, refs = refs[:pages], refs[pages : pages + 2], refs[pages + 2 :]
    out_refs, (tokens_ref, bias_ref, latent_ref) = refs[:-3], refs[-3:]
    unpack_pages(packed_refs, tokens_ref, page_size)
    bias_ref[...] = token_bias(counts_of(count_refs), place, tokens_ref.shape[0], page_size)
    latent_ref[...] = latents_of(limit_ref, q_ref, tokens_ref[...], bias_ref[...], before)
    sharing, size = len(out_refs), out_refs[0].shape[0]
    for u, out_ref in enumerate(out_refs):
        at = pl.multiple_of(((rank_ref[0] & (sharing - 1)) ^ u) * size, size)
        out_ref[...] = latent_ref[pl.ds(at, size), :]


def latents_near_kernel(rank_ref, limit_ref, q_ref, tokens_ref, bias_ref, *refs):
    before, out_ref = refs[:2], refs[2]
    out_ref[...] = latents_of(limit_ref, q_ref, tokens_ref[...], bias_ref[...], before)


def latents(queries, packed, counts, place, state, rank, limit, page_size, ranks):
    count, width = queries.shape
    half, size = ranks // 2, count // ranks
    tokens = sum(p.shape[0] for p in packed) * page_size
    own = lambda g, rank, _: (lax.div(rank[0], half), 0)
    other = lambda g, rank, _: (1 - lax.div(rank[0], half), 0)
    fixed = lambda g, *_: (0, 0)
    state_shapes = ((count // 2, 128), (count // 2, LATENT))
    state_specs = lambda block: [pl.BlockSpec(shape, block) for shape in state_shapes]
    array = jax.ShapeDtypeStruct
    options = dict(
        compiler_params=pltpu.CompilerParams(vmem_limit_bytes=28 * MIB),
        cost_estimate=pl.CostEstimate(
            flops=count * tokens * (width + LATENT),
            bytes_accessed=2 * tokens * width + 2 * count * LATENT,
            transcendentals=count * tokens // 2,
        ),
    )
    state = [in_hbm(x) for x in state]
    *far, unpacked, bias = pl.pallas_call(
        functools.partial(latents_far_kernel, len(packed), place, page_size),
        out_shape=[array((size, LATENT), jnp.bfloat16)] * half
        + [array((tokens, width), queries.dtype), array((counts[0].shape[0], tokens), jnp.float32)],
        grid_spec=pltpu.PrefetchScalarGridSpec(
            num_scalar_prefetch=2,
            grid=(1,),
            in_specs=[pl.BlockSpec(x.shape, fixed) for x in counts]
            + [pl.BlockSpec((count // 2, width), other)]
            + [pl.BlockSpec(p.shape, lambda *_: (0, 0, 0)) for p in packed]
            + state_specs(other),
            out_specs=[pl.BlockSpec((size, LATENT), fixed)] * half
            + [pl.BlockSpec((tokens, width), fixed)]
            + [pl.BlockSpec((counts[0].shape[0], tokens), fixed)],
            scratch_shapes=[pltpu.VMEM((count // 2, LATENT), jnp.bfloat16)],
        ),
        name="latents_far",
        **options,
    )(rank, limit, *counts, queries, *packed, *state)
    near = pl.pallas_call(
        latents_near_kernel,
        out_shape=pltpu.HBM((count // 2, LATENT), jnp.bfloat16),
        grid_spec=pltpu.PrefetchScalarGridSpec(
            num_scalar_prefetch=2,
            grid=(1,),
            in_specs=[pl.BlockSpec((count // 2, width), own)]
            + [pl.BlockSpec(x.shape, fixed) for x in (unpacked, bias)]
            + state_specs(own),
            out_specs=pl.BlockSpec((count // 2, LATENT), fixed),
        ),
        name="latents_near",
        **options,
    )(rank, limit, queries, unpacked, bias, *state)
    return far, near


def slot_counts(content, lengths, slots, page_size):
    full = lengths // page_size
    order = jnp.arange(content.shape[1])
    same = content[:, :, None] == slots[None, None, :]
    whole = jnp.sum((same & (order < full[:, None])[:, :, None]).astype(jnp.float32), axis=1)
    last = jnp.sum((same & (order == full[:, None])[:, :, None]).astype(jnp.float32), axis=1)
    return whole.astype(jnp.bfloat16), last.astype(jnp.bfloat16), (lengths % page_size)[:, None]


def stream(weight_ref, tiles_ref, sems, row, column):
    count, depth, width = tiles_ref.shape
    along_rows = depth < weight_ref.shape[0]
    copies = []
    for n in range(count):
        rows = pl.ds(row + (n * depth if along_rows else 0), depth)
        columns = pl.ds(column + (0 if along_rows else n * width), width)
        copies.append(
            pltpu.make_async_copy(weight_ref.at[rows, columns], tiles_ref.at[n], sems.at[n])
        )
    for copy in copies:
        copy.start()
    return copies


def multiply_tiles(places, rows_ref, tiles_ref, copies, keep_ref, send_ref):
    half, width = keep_ref.shape[0], tiles_ref.shape[2]
    size = 2 * half // len(places)
    for n, copy in enumerate(copies):
        copy.wait()
        product = jnp.dot(
            rows_ref[...], tiles_ref[n], preferred_element_type=jnp.float32
        ).astype(jnp.bfloat16)
        for to, at in enumerate(places):
            out_ref, to = (keep_ref, to * size) if to * size < half else (send_ref, to * size - half)
            out_ref[pl.ds(to, size), pl.ds(n * width, width)] = product[at * size : (at + 1) * size]


def project_first_kernel(column, order, rank_ref, near_ref, *refs):
    split = near_ref.shape[0]
    far_refs, refs = refs[:split], refs[split:]
    value_ref, weight_ref, head_ref, keep_ref, send_ref, tiles_ref, sems = refs
    copies = stream(weight_ref, tiles_ref, sems, 0, column)
    own = rank_ref[0] & (split - 1)
    parts = [near_ref.at[own ^ k] for k in range(split)] + list(far_refs)
    heads, width = value_ref.shape[0], value_ref.shape[2]
    slots = near_ref.shape[1] // heads
    for h in range(heads):
        rows = jnp.concatenate([parts[k][pl.ds(h * slots, slots), :] for k in order], axis=0)
        head_ref[:, pl.ds(h * width, width)] = jnp.dot(
            rows, value_ref[h], preferred_element_type=jnp.float32
        ).astype(jnp.bfloat16)
    multiply_tiles(range(len(order)), head_ref, tiles_ref, copies, keep_ref, send_ref)


def project_kernel(column, places, rows_ref, weight_ref, keep_ref, send_ref, tiles_ref, sems):
    copies = stream(weight_ref, tiles_ref, sems, 0, column)
    multiply_tiles(places, rows_ref, tiles_ref, copies, keep_ref, send_ref)


def project_options(rows, depth, columns, tile):
    return dict(
        scratch_shapes=[
            pltpu.VMEM((columns // tile, depth, tile), jnp.bfloat16),
            pltpu.SemaphoreType.DMA((columns // tile,)),
        ],
        compiler_params=pltpu.CompilerParams(vmem_limit_bytes=20 * MIB),
        cost_estimate=pl.CostEstimate(
            flops=2 * rows * depth * columns,
            bytes_accessed=2 * depth * columns + 2 * rows * (columns + depth),
            transcendentals=0,
        ),
    )


def project_first(order, rank, near, far, value_up, weight, columns, tile=512):
    depth = weight.shape[0]
    rows = len(order) * near.shape[1] // value_up.shape[0]
    vmem = pl.BlockSpec(memory_space=pltpu.VMEM)
    half = jax.ShapeDtypeStruct((rows // 2, columns), jnp.bfloat16)
    return pl.pallas_call(
        functools.partial(project_first_kernel, 0, order),
        out_shape=(jax.ShapeDtypeStruct((rows, depth), jnp.bfloat16), half, half),
        in_specs=[pl.BlockSpec(memory_space=pltpu.SMEM)]
        + [vmem] * (len(far) + 2)
        + [pl.BlockSpec(memory_space=pltpu.HBM)],
        name="project_first",
        **project_options(rows, depth, columns, tile),
    )(rank, near, *far, value_up, in_hbm(weight))


def project(rows, weight, columns, chunk, places, name, tile=512):
    count, depth = rows.shape
    half = jax.ShapeDtypeStruct((count // 2, columns), jnp.bfloat16)
    return pl.pallas_call(
        functools.partial(project_kernel, chunk * columns, tuple(places)),
        out_shape=(half, half),
        in_specs=[
            pl.BlockSpec(memory_space=pltpu.VMEM),
            pl.BlockSpec(memory_space=pltpu.HBM),
        ],
        name=name,
        **project_options(count, depth, columns, tile),
    )(rows, in_hbm(weight))


def halve_kernel(keep_ref, came_ref, own_ref, send_ref):
    total = keep_ref[...].astype(jnp.float32) + came_ref[...].astype(jnp.float32)
    half = own_ref.shape[0]
    own_ref[...] = total[:half]
    send_ref[...] = total[half:].astype(send_ref.dtype)


def halve(keep, came):
    shape = (keep.shape[0] // 2, keep.shape[1])
    return pl.pallas_call(
        halve_kernel,
        out_shape=(
            jax.ShapeDtypeStruct(shape, jnp.float32),
            jax.ShapeDtypeStruct(shape, jnp.bfloat16),
        ),
        compiler_params=pltpu.CompilerParams(vmem_limit_bytes=16 * MIB),
        name="halve",
    )(keep, came)


def finish_kernel(residual_ref, gain_ref, own_ref, *refs):
    others, (middle_ref, scaled_ref) = refs[:-2], refs[-2:]
    middle = residual_ref[...].astype(jnp.float32) + own_ref[...]
    for other in others:
        middle = middle + other[...].astype(jnp.float32)
    middle_ref[...] = middle
    scaled_ref[...] = (middle * gain_ref[...]).astype(scaled_ref.dtype)


def finish_middle(residual, gain, sums, chunk):
    rows, columns = sums[0].shape
    here = lambda _: (0, chunk)
    block = pl.BlockSpec((rows, columns), lambda _: (0, 0))
    return pl.pallas_call(
        finish_kernel,
        out_shape=(
            jax.ShapeDtypeStruct((rows, columns), jnp.float32),
            jax.ShapeDtypeStruct((rows, columns), jnp.bfloat16),
        ),
        grid=(1,),
        in_specs=[pl.BlockSpec((rows, columns), here), pl.BlockSpec((1, columns), here)]
        + [block] * len(sums),
        out_specs=(block, block),
        compiler_params=pltpu.CompilerParams(vmem_limit_bytes=16 * MIB),
        name="finish_middle",
    )(residual, gain, *sums)


def gather_matmul_kernel(row, first, last, n_pieces, places, mean_over, *refs):
    pieces, refs = refs[:n_pieces], refs[n_pieces:]
    inverse_ref, gate_ref, up_ref, refs = refs[0], refs[1], refs[2], refs[3:]
    before, refs = ((), refs) if first else (refs[:3], refs[3:])
    if last:
        hidden_ref, gate_acc, up_acc, squares, *refs = refs
    else:
        gate_acc, up_acc, squares, *refs = refs
    (rows_ref,) = refs
    steps, _, depth = rows_ref.shape
    size = pieces[0].shape[0]
    sources = [(piece, b) for piece in pieces for b in range(piece.shape[0] // size)]
    for (piece, b), place in zip(sources, places):
        for k in range(steps):
            rows_ref[k, pl.ds(place * size, size), :] = piece[
                pl.ds(b * size, size), pl.ds(k * depth, depth)
            ]
    for now, old in zip((gate_acc, up_acc, squares), before):
        now[...] = old[...]

    for k in range(steps):
        rows = rows_ref[k]
        plain = rows.astype(jnp.float32) * inverse_ref[:, pl.ds(k * depth, depth)]
        square = jnp.broadcast_to(jnp.sum(plain * plain, axis=1, keepdims=True), squares.shape)
        span = pl.ds(row + k * depth, depth)
        gate = jnp.dot(rows, gate_ref[span, :], preferred_element_type=jnp.float32)
        up = jnp.dot(rows, up_ref[span, :], preferred_element_type=jnp.float32)
        if first and k == 0:
            squares[...], gate_acc[...], up_acc[...] = square, gate, up
        else:
            squares[...] += square
            gate_acc[...] += gate
            up_acc[...] += up

    if last:
        factor = lax.rsqrt(squares[:, :1] / mean_over + 1e-06)
        gate = gate_acc[...] * factor
        hidden_ref[...] = (gate * jax.nn.sigmoid(gate) * (up_acc[...] * factor)).astype(
            jnp.bfloat16
        )


def gather_matmul(
    pieces, places, inverse_gain, gate_proj, up_proj, before, chunk, last, tile=512
):
    columns = pieces[0].shape[1]
    rows = sum(piece.shape[0] for piece in pieces)
    width, units = gate_proj.shape
    steps = columns // tile
    sums = ((rows, units), (rows, units), (rows, 128))
    if last:
        out_shape = jax.ShapeDtypeStruct((rows, units), jnp.bfloat16)
        scratch = [pltpu.VMEM(shape, jnp.float32) for shape in sums]
    else:
        out_shape = tuple(jax.ShapeDtypeStruct(shape, jnp.float32) for shape in sums)
        scratch = []
    vmem = pl.BlockSpec(memory_space=pltpu.VMEM)
    return pl.pallas_call(
        functools.partial(
            gather_matmul_kernel,
            chunk * columns,
            before is None,
            last,
            len(pieces),
            tuple(places),
            width,
        ),
        out_shape=out_shape,
        in_specs=[vmem] * (len(pieces) + 3 + len(before or ())),
        scratch_shapes=scratch + [pltpu.VMEM((steps, rows, tile), jnp.bfloat16)],
        compiler_params=pltpu.CompilerParams(vmem_limit_bytes=12 * MIB),
        cost_estimate=pl.CostEstimate(
            flops=4 * rows * columns * units,
            bytes_accessed=4 * columns * units + 2 * rows * columns,
            transcendentals=0,
        ),
        name="gate_up",
    )(*pieces, inverse_gain, in_vmem(gate_proj), in_vmem(up_proj), *(before or ()))


class Grid:
    def __init__(self, count):
        self.count = count
        self.bits = count.bit_length() - 1

    def dims(self, chunk):
        first = [1, 0] if chunk % 2 else [0, 1]
        return first + list(range(2, self.bits))

    def order(self, chunk):
        dims = self.dims(chunk)
        return [
            sum(1 << d for i, d in enumerate(dims) if n >> (self.bits - 1 - i) & 1)
            for n in range(self.count)
        ]

    def places(self, chunk):
        base = self.order(0)
        return [base.index(k) for k in self.order(chunk)]

    def exchange(self, array, k):
        return lax.ppermute(array, "dp", [(i, i ^ k) for i in range(self.count)])

    def exchange_near(self, array):
        half = self.count // 2
        groups = [list(range(half)), list(range(half, self.count))]
        return lax.all_to_all(
            array, "dp", split_axis=0, concat_axis=0, axis_index_groups=groups, tiled=True
        )

    def scatter_sum(self, keep, send, chunk):
        *before, last = self.dims(chunk)
        for d in before:
            keep, send = halve(keep, self.exchange(send, 1 << d))
        return [keep, self.exchange(send, 1 << last)]

    def gather(self, block, chunk):
        pieces = [block]
        for d in reversed(self.dims(chunk)):
            held = jnp.concatenate(pieces, axis=0) if len(pieces) > 1 else block
            pieces.append(self.exchange(held, 1 << d))
        return pieces


def add_up(base, parts):
    for part in parts:
        base = base + part.astype(jnp.float32)
    return base


def body(
    page_pool,
    move_source,
    move_page,
    move_slot,
    row_count,
    lengths,
    page_table,
    queries,
    value_up,
    out_proj,
    residual,
    norm_gain,
    gate_proj,
    up_proj,
    down_proj,
):
    rank_count = lax.axis_size("dp")
    own_rank = lax.axis_index("dp")
    grid = Grid(rank_count)
    rank = own_rank[None]
    move_count = move_page.shape[0] // rank_count
    capacity = max(2, (3 * move_count + 2 * rank_count - 1) // (2 * rank_count))
    slot_count, page_size, feature_width = page_pool.shape
    sources = move_source.T.reshape(rank_count, move_count)
    page_ids = move_page.reshape(rank_count, move_count)
    slot_ids = move_slot.reshape(rank_count, move_count)
    move_order = jnp.arange(move_count)
    earlier = (sources[:, :, None] == sources[:, None, :]) & (
        move_order[None, None, :] < move_order[None, :, None]
    )
    arrival = jnp.sum(earlier.astype(jnp.int32), axis=2)
    chosen = (sources == own_rank)[:, :, None] & (
        arrival[:, :, None] == jnp.arange(capacity)[None, None, :]
    )
    send_ids = jnp.sum(jnp.where(chosen, page_ids[:, :, None], 0), axis=1).reshape(-1)
    split = rank_count // 2
    far_peers = range(split, rank_count)
    packed = pack_pages(page_pool, send_ids, rank, far_peers, False, capacity, rank)
    far_pages = [grid.exchange(pages, k) for k, pages in zip(far_peers, packed)]
    (packed,) = pack_pages(page_pool, send_ids, rank, range(split), True, capacity, packed[0])
    near_pages = grid.exchange_near(packed)

    pick = lambda array: lax.dynamic_index_in_dim(array, own_rank, 0, keepdims=False)
    own_slots, own_pages = pick(slot_ids), pick(page_ids)
    peer = pick(sources) ^ own_rank
    place = jnp.where(peer < split, pick(sources) & (split - 1), peer) * capacity + pick(arrival)
    content_of = jnp.where(peer == 0, own_pages, slot_count + place)
    hit = page_table[:, :, None] == own_slots[None, None, :]
    content = jnp.where(
        jnp.any(hit, axis=2), jnp.sum(jnp.where(hit, content_of, 0), axis=2), page_table
    )
    places = slot_count + rank_count * capacity
    counts = slot_counts(content, lengths, jnp.arange(places), page_size)
    far_place = slot_count + split * capacity

    row_slots, head_count = queries.shape[:2]
    by_head_queries = queries.transpose(1, 0, 2).reshape(head_count * row_slots, feature_width)
    state = attend_resident(
        by_head_queries,
        page_pool.reshape(slot_count * page_size, feature_width),
        counts,
        page_size,
    )
    near_pages = near_pages.reshape((split * capacity,) + near_pages.shape[2:])
    state = attend_near(by_head_queries, [near_pages], counts, slot_count, state, page_size)
    far_latents, near_latents = latents(
        by_head_queries,
        far_pages,
        counts,
        far_place,
        state,
        rank,
        row_count,
        page_size,
        rank_count,
    )
    far_latents = [grid.exchange(x, k) for k, x in zip(far_peers, far_latents)]
    near_latents = grid.exchange_near(near_latents.reshape(split, -1, LATENT))

    width = residual.shape[1]
    columns = width // CHUNKS
    head_out, *halves = project_first(
        grid.order(0), rank, near_latents, far_latents, value_up, out_proj, columns
    )
    projected = [halves] + [
        project(head_out, out_proj, columns, c, grid.places(c), "project_out")
        for c in range(1, CHUNKS)
    ]
    middle, gathered = [], []
    for c, (keep, send) in enumerate(projected):
        row_sum, scaled = finish_middle(
            residual, norm_gain[None, :], grid.scatter_sum(keep, send, c), c
        )
        middle.append(row_sum)
        gathered.append(grid.gather(scaled, c))
    inverse_gain = (1.0 / norm_gain)[None, :]
    sums = None
    for c, pieces in enumerate(gathered):
        span = slice(c * columns, (c + 1) * columns)
        sums = gather_matmul(
            pieces,
            grid.places(c),
            inverse_gain[:, span],
            gate_proj,
            up_proj,
            sums,
            c,
            c == CHUNKS - 1,
        )
    hidden = sums
    outputs = []
    for c in range(CHUNKS):
        keep, send = project(hidden, down_proj, columns, c, grid.places(c), "project_down")
        outputs.append(add_up(middle[c], grid.scatter_sum(keep, send, c)).astype(jnp.bfloat16))
    return jnp.concatenate(outputs, axis=1)


def solution(mesh):
    in_specs = (
        P(("rep", "dp"), None, None),
        P("rep", None),
        P("rep"),
        P("rep"),
        P(("rep", "dp")),
        P(("rep", "dp")),
        P(("rep", "dp"), None),
        P(("rep", "dp"), None, None),
        P("dp", None, None),
        P("dp", None),
        P(("rep", "dp"), None),
        P(),
        P(None, "dp"),
        P(None, "dp"),
        P("dp", None),
    )
    out_specs = P(("rep", "dp"), None)
    return jax.shard_map(body, mesh=mesh, in_specs=in_specs, out_specs=out_specs, check_vma=False)
```

time: 561 us -> 226 us (0.40)
  waiting for transfers between devices: 248 us -> 81.2 us
  local copies, waits for them, and re-layouts: 129 us -> 9.56 us
  matrix products: 94 us -> 0 us
  Pallas kernels: 0 us -> 76.3 us
  starting transfers between devices: 7.68 us -> 53.5 us
  other arithmetic: 35.2 us -> 3.37 us
  blocking collectives: 29.6 us -> 0 us
  between operations: 14 us -> 1.02 us
    reduce_scatter x2 -> x0, waiting for transfers between devices: 131 us -> none  [the longest x1 65.3 us: body(): lax.psum_scatter(jnp.dot(rows_slice, out_proj, preferred_element_type=jnp...]
    gather x18 -> x0, local copies, waits for them, and re-layouts: 104 us -> none  [the longest x16 94.9 us: one_row(): tokens = cache_pages[table_row].reshape(-1, cache_pages.shape[2])]
    dot_general x37 -> x0, matrix products: 94 us -> none  [the longest x16 45.1 us: one_row(): jnp.einsum('hk,tk->ht', query_row, tokens, preferred_element_type=jnp.flo...]
    pallas_call x0 -> x22, Pallas kernels: none -> 76.3 us  [the longest x1 30.3 us: attend_resident(): pl.pallas_call(functools.partial(resident_kernel, chunk, page_size), out_...]
    ppermute x0 -> x26, waiting for transfers between devices: none -> 72.8 us  [exchange(): return lax.ppermute(array, 'dp', [(i, i ^ k) for i in range(self.count)])]
    all_to_all x1 -> x2, waiting for transfers between devices: 72.8 us -> 8.44 us  [exchange_near(): lax.all_to_all(array, 'dp', split_axis=0, concat_axis=0, axis_index_group...]
    ppermute x0 -> x26, starting transfers between devices: none -> 46 us  [exchange(): return lax.ppermute(array, 'dp', [(i, i ^ k) for i in range(self.count)])]
    all_gather x1 -> x0, waiting for transfers between devices: 45 us -> none  [body(): row_piece = lax.all_gather(normed, 'dp', axis=0, tiled=True)]
  transfers between devices with their start and end apart: 4 -> 28, of which waited for: 4 -> 21; matrix products, arithmetic and copies ran while one was open for 0% -> 1% of each run, Pallas kernels for 0% -> 24%
where the time goes in v1:
time: 226 us; the launch traced here: 225 us
  waiting for transfers between devices  81.2 us (36%)
  Pallas kernels  76.3 us (34%)
  starting transfers between devices  53.5 us (24%)
  local copies, waits for them, and re-layouts  9.56 us (4%)
  other arithmetic  3.37 us (1%)
    ppermute x26, waiting for transfers between devices, exchange(): return lax.ppermute(array, 'dp', [(i, i ^ k) for i in range(self.count)])  72.8 us
    ppermute x26, starting transfers between devices, exchange(): return lax.ppermute(array, 'dp', [(i, i ^ k) for i in range(self.count)])  46 us
    pallas_call x1, Pallas kernels, attend_resident(): pl.pallas_call(functools.partial(resident_kernel, chunk, page_size), out_...  30.3 us
    pallas_call x3, Pallas kernels, project(): pl.pallas_call(functools.partial(project_kernel, chunk * columns, tuple(p...  11.4 us
    pallas_call x2, Pallas kernels, pack_pages(): pl.pallas_call(functools.partial(pack_kernel, tuple(peers), near, capacit...  8.65 us
    all_to_all x2, waiting for transfers between devices, exchange_near(): lax.all_to_all(array, 'dp', split_axis=0, concat_axis=0, axis_index_group...  8.44 us
    all_to_all x2, starting transfers between devices, exchange_near(): lax.all_to_all(array, 'dp', split_axis=0, concat_axis=0, axis_index_group...  7.57 us
    pallas_call x1, Pallas kernels, attend_near(): pl.pallas_call(functools.partial(near_kernel, len(packed), place, page_si...  7.47 us
  transfers between devices with their start and end apart: 28, of which 21 were waited for; matrix products, arithmetic and copies ran while one was open for 1% of the time, Pallas kernels for 24%

profile of v1, /device:TPU:0, one launch (start us, length us, event | category | flops | bytes accessed | tf_op | source)
XLA Modules:
  0.0 225.0 jit_solution(17288078782221661442)
XLA Ops:
  0.0 0.6 broadcast.104
  0.6 1.3 reduce.3
  2.0 0.8 reshape.95
  2.8 0.3 convert_reduce_fusion.2
  3.1 0.2 select_reduce_fusion
  3.4 4.2 %pack_far.1 = (bf16[5,288,128]{2,1,0:T(8,128)(2,1)S(1)}, bf16[5,288,128]{2,1,0:T(8,128)(2,1)}, bf16[5,288,128]{2,1,0:T(8,128)(2,1)}, bf16[5,288,128]{2,1,0:T(8,128)(2,1)}) custom-call(s32[40]{0:T(128)S(1)} %reshape.96.ids_ref, s32[1]{0:T(128)} %bitcast.1.rank_ref._, bf16[112,64,576]{2,1,0:T(8,128)(2,1)} %pool_ref.3, s32[1]{0:T(128)} %bitcast.1.rank_ref._), custom_call_target="tpu_custom_call" | custom-call | tf_op jit(solution)/shard_map/pack_far/pallas_call | solution.py:61
  7.6 4.1 %collective-permute-start = (bf16[5,288,128]{2,1,0:T(8,128)(2,1)S(1)}, bf16[5,288,128]{2,1,0:T(8,128)(2,1)S(1)}, u32[]{:S(2)}, u32[]{:S(2)}) collective-permute-start(bf16[5,288,128]{2,1,0:T(8,128)(2,1)S(1)} %get-tuple-element.51._), channel_id=1, source_target_pairs={{0,16},{4,20},{8,24},{12,28},{16,0},{20,4},{24,8},{28,12},{1,17},{... | collective-permute-start | bytes 1105928 | tf_op jit(solution)/shard_map/ppermute | solution.py:617
  11.7 4.4 %pack_near.1 = bf16[4,5,288,128]{3,2,1,0:T(8,128)(2,1)} custom-call(s32[40]{0:T(128)S(1)} %reshape.96.ids_ref, s32[1]{0:T(128)} %bitcast.1.rank_ref._, bf16[112,64,576]{2,1,0:T(8,128)(2,1)} %pool_ref.3, bf16[5,288,128]{2,1,0:T(8,128)(2,1)S(1)} %get-tuple-element.51._), custom_call_target="tpu_custom_call" | custom-call | tf_op jit(solution)/shard_map/pack_near/pallas_call | solution.py:61
  16.2 3.9 %all-to-all-start = ((bf16[4,5,288,128]{3,2,1,0:T(8,128)(2,1)}), bf16[4,5,288,128]{3,2,1,0:T(8,128)(2,1)S(1)}, u32[]{:S(2)}, u32[]{:S(2)}) async-start(bf16[4,5,288,128]{3,2,1,0:T(8,128)(2,1)} %pack_near.1), calls=%async_computation | async-start | bytes 2949120 | tf_op jit(solution)/shard_map/all_to_all | solution.py:622
  20.1 1.8 collective-permute-start.1
  21.9 3.5 %collective-permute-start.2 = (bf16[5,288,128]{2,1,0:T(8,128)(2,1)}, bf16[5,288,128]{2,1,0:T(8,128)(2,1)}, u32[]{:S(2)}, u32[]{:S(2)}) collective-permute-start(bf16[5,288,128]{2,1,0:T(8,128)(2,1)} %get-tuple-element.53), channel_id=1, source_target_pairs={{0,24},{4,28},{8,16},{12,20},{16,8},{20,12},{24,0},{28,4},{1,25},{... | collective-permute-start | bytes 1105928 | tf_op jit(solution)/shard_map/ppermute | solution.py:617
  25.5 2.1 copy.20
  28.0 0.4 convert_reduce_fusion
  28.4 30.3 %attend_resident.1 = (f32[1024,128]{1,0:T(8,128)}, f32[1024,512]{1,0:T(8,128)}) custom-call(bf16[16,152]{1,0:T(8,128)(2,1)S(1)} %get-tuple-element.98.whole_ref.refs_0_, bf16[16,152]{1,0:T(8,128)(2,1)S(1)} %get-tuple-element.97.last_ref.refs_1_, s32[16,1]{1,0:T(8,128)S(1)} %copy.24.part_ref.refs_2_, bf16[1024,576]{1,0:T(8,128)(2,1)S(1)} %bitcast.31, ...), custom_call_target="tpu_custom_call" | custom-call | flops 15971909632 | bytes 10354688 | tf_op jit(solution)/shard_map/attend_resident/pallas_call | solution.py:211
  59.3 8.4 %all-to-all-done = bf16[4,5,288,128]{3,2,1,0:T(8,128)(2,1)S(1)} async-done(((bf16[4,5,288,128]{3,2,1,0:T(8,128)(2,1)}), bf16[4,5,288,128]{3,2,1,0:T(8,128)(2,1)S(1)}, u32[]{:S(2)}, u32[]{:S(2)}) %all-to-all-start) | async-done | bytes 1474592 | tf_op jit(solution)/shard_map/all_to_all | solution.py:622
  67.8 7.5 %attend_near.1 = (f32[1024,128]{1,0:T(8,128)}, f32[1024,512]{1,0:T(8,128)}) custom-call(bf16[16,152]{1,0:T(8,128)(2,1)S(1)} %get-tuple-element.98.whole_ref.refs_0_, bf16[16,152]{1,0:T(8,128)(2,1)S(1)} %get-tuple-element.97.last_ref.refs_1_, s32[16,1]{1,0:T(8,128)S(1)} %copy.24.part_ref.refs_2_, bf16[1024,576]{1,0:T(8,128)(2,1)S(1)} %bitcast.32, ...), custom_call_target="tpu_custom_call" | custom-call | flops 2852126720 | bytes 5668864 | tf_op jit(solution)/shard_map/attend_near/pallas_call | solution.py:262
  75.3 4.1 %latents_far.1 = (bf16[128,512]{1,0:T(8,128)(2,1)S(1)}, bf16[128,512]{1,0:T(8,128)(2,1)S(1)}, bf16[128,512]{1,0:T(8,128)(2,1)S(1)}, bf16[128,512]{1,0:T(8,128)(2...) custom-call(s32[1]{0:T(128)} %bitcast.1.rank_ref._, s32[1]{0:T(128)S(6)} %copy.25.limit_ref, ...), custom_call_target="tpu_custom_call" | custom-call | flops 1426063360 | bytes 2523136 | tf_op jit(solution)/shard_map/latents_far/pallas_call | solution.py:327
  79.4 4.5 %latents_near.1 = bf16[512,512]{1,0:T(8,128)(2,1)} custom-call(s32[1]{0:T(128)} %bitcast.1.rank_ref._, s32[1]{0:T(128)S(6)} %copy.25.limit_ref, bf16[1024,576]{1,0:T(8,128)(2,1)S(1)} %bitcast.34, bf16[1280,576]{1,0:T(8,128)(2,1)S(1)} %get-tuple-element.59.tokens_ref, f32[16,1280]{1,0:T(8,128)S(1)} %get-tuple-element.60.bias_ref, ...), custom_call_target="tpu_custom_call" | custom-call | flops 1426063360 | bytes 2523136 | tf_op jit(solution)/shard_map/latents_near/pallas_call | solution.py:346
  83.9 3.6 %all-to-all-start.1 = ((bf16[4,128,512]{2,1,0:T(8,128)(2,1)}), bf16[4,128,512]{2,1,0:T(8,128)(2,1)S(1)}, u32[]{:S(2)}, u32[]{:S(2)}) async-start(bf16[4,128,512]{2,1,0:T(8,128)(2,1)} %bitcast.39), calls=%async_computation.1 | async-start | bytes 1048576 | tf_op jit(solution)/shard_map/all_to_all | solution.py:622
  87.6 4.2 %collective-permute-start.4 = (bf16[128,512]{1,0:T(8,128)(2,1)S(1)}, bf16[128,512]{1,0:T(8,128)(2,1)S(1)}, u32[]{:S(2)}, u32[]{:S(2)}) collective-permute-start(bf16[128,512]{1,0:T(8,128)(2,1)S(1)} %get-tuple-element.61), channel_id=1, source_target_pairs={{0,16},{4,20},{8,24},{12,28},{16,0},{20,4},{24,8},{28,12},{1,17},{... | collective-permute-start | bytes 393224 | tf_op jit(solution)/shard_map/ppermute | solution.py:617
  91.7 1.2 collective-permute-start.5
  92.9 3.8 %collective-permute-start.6 = (bf16[128,512]{1,0:T(8,128)(2,1)S(1)}, bf16[128,512]{1,0:T(8,128)(2,1)S(1)}, u32[]{:S(2)}, u32[]{:S(2)}) collective-permute-start(bf16[128,512]{1,0:T(8,128)(2,1)S(1)} %get-tuple-element.63), channel_id=1, source_target_pairs={{0,24},{4,28},{8,16},{12,20},{16,8},{20,12},{24,0},{28,4},{1,25},{... | collective-permute-start | bytes 393224 | tf_op jit(solution)/shard_map/ppermute | solution.py:617
  96.7 0.4 collective-permute-done.4.refs_0_
  97.1 3.4 %collective-permute-done.5.refs_1_ = bf16[128,512]{1,0:T(8,128)(2,1)S(1)} collective-permute-done((bf16[128,512]{1,0:T(8,128)(2,1)S(1)}, bf16[128,512]{1,0:T(8,128)(2,1)S(1)}, u32[]{:S(2)}, u32[]{:S(2)}) %collective-permute-start.5) | collective-permute-done | bytes 131104 | tf_op jit(solution)/shard_map/ppermute | solution.py:617
  100.5 8.3 %collective-permute-done.6.refs_2_ = bf16[128,512]{1,0:T(8,128)(2,1)S(1)} collective-permute-done((bf16[128,512]{1,0:T(8,128)(2,1)S(1)}, bf16[128,512]{1,0:T(8,128)(2,1)S(1)}, u32[]{:S(2)}, u32[]{:S(2)}) %collective-permute-start.6) | collective-permute-done | bytes 131104 | tf_op jit(solution)/shard_map/ppermute | solution.py:617
  108.8 2.8 %collective-permute-done.7.refs_3_ = bf16[128,512]{1,0:T(8,128)(2,1)S(1)} collective-permute-done((bf16[128,512]{1,0:T(8,128)(2,1)S(1)}, bf16[128,512]{1,0:T(8,128)(2,1)S(1)}, u32[]{:S(2)}, u32[]{:S(2)}) %collective-permute-start.7) | collective-permute-done | bytes 131104 | tf_op jit(solution)/shard_map/ppermute | solution.py:617
  111.6 4.0 %project_first.1 = (bf16[128,1024]{1,0:T(8,128)(2,1)S(1)}, bf16[64,3584]{1,0:T(8,128)(2,1)S(1)}, bf16[64,3584]{1,0:T(8,128)(2,1)S(1)}) custom-call(s32[1]{0:T(128)} %bitcast.1.rank_ref._, bf16[4,128,512]{2,1,0:T(8,128)(2,1)S(1)} %all-to-all-done.1.near_ref, bf16[128,512]{1,0:T(8,128)(2,1)S(1)} %collective-permute-done.4.refs_0_, ...), custom_call_target="tpu_custom_call" | custom-call | flops 939524096 | bytes 8519680 | tf_op jit(solution)/shard_map/project_first/pallas_call | solution.py:442
  115.6 1.4 collective-permute-start.8
  117.0 3.7 %project_out.1 = (bf16[64,3584]{1,0:T(8,128)(2,1)S(1)}, bf16[64,3584]{1,0:T(8,128)(2,1)S(1)}) custom-call(bf16[128,1024]{1,0:T(8,128)(2,1)S(1)} %get-tuple-element.72.rows_ref, bf16[1024,7168]{1,0:T(8,128)(2,1)} %weight_ref.3), custom_call_target="tpu_custom_call" | custom-call | flops 939524096 | bytes 8519680 | tf_op jit(solution)/shard_map/project_out/pallas_call | solution.py:456
  120.7 4.6 %collective-permute-start.11 = (bf16[64,3584]{1,0:T(8,128)(2,1)S(1)}, bf16[64,3584]{1,0:T(8,128)(2,1)S(1)}, u32[]{:S(2)}, u32[]{:S(2)}) collective-permute-start(bf16[64,3584]{1,0:T(8,128)(2,1)S(1)} %get-tuple-element.74), channel_id=1, source_target_pairs={{0,8},{4,12},{8,0},{12,4},{16,24},{20,28},{24,16},{28,20},{1,9},{5... | collective-permute-start | bytes 1376264 | tf_op jit(solution)/shard_map/ppermute | solution.py:617
  125.4 1.8 collective-permute-done.8.came_ref
  127.3 5.3 %collective-permute-start.9 = (bf16[32,3584]{1,0:T(8,128)(2,1)S(1)}, bf16[32,3584]{1,0:T(8,128)(2,1)S(1)}, u32[]{:S(2)}, u32[]{:S(2)}) collective-permute-start(bf16[32,3584]{1,0:T(8,128)(2,1)S(1)} %get-tuple-element.68), channel_id=1, source_target_pairs={{0,8},{4,12},{8,0},{12,4},{16,24},{20,28},{24,16},{28,20},{1,9},{5... | collective-permute-start | bytes 688136 | tf_op jit(solution)/shard_map/ppermute | solution.py:617
  132.6 4.3 %collective-permute-done.11.came_ref = bf16[64,3584]{1,0:T(8,128)(2,1)S(1)} collective-permute-done((bf16[64,3584]{1,0:T(8,128)(2,1)S(1)}, bf16[64,3584]{1,0:T(8,128)(2,1)S(1)}, u32[]{:S(2)}, u32[]{:S(2)}) %collective-permute-start.11) | collective-permute-done | bytes 458784 | tf_op jit(solution)/shard_map/ppermute | solution.py:617
  136.9 1.1 collective-permute-start.12
  138.0 1.8 collective-permute-done.9.came_ref
  139.9 3.5 %collective-permute-start.10 = (bf16[16,3584]{1,0:T(8,128)(2,1)S(1)}, bf16[16,3584]{1,0:T(8,128)(2,1)S(1)}, u32[]{:S(2)}, u32[]{:S(2)}) collective-permute-start(bf16[16,3584]{1,0:T(8,128)(2,1)S(1)} %get-tuple-element.70), channel_id=1, source_target_pairs={{0,16},{4,20},{8,24},{12,28},{16,0},{20,4},{24,8},{28,12},{1,17},{... | collective-permute-start | bytes 344072 | tf_op jit(solution)/shard_map/ppermute | solution.py:617
  143.4 3.4 %collective-permute-start.13 = (bf16[16,3584]{1,0:T(8,128)(2,1)S(1)}, bf16[16,3584]{1,0:T(8,128)(2,1)S(1)}, u32[]{:S(2)}, u32[]{:S(2)}) collective-permute-start(bf16[16,3584]{1,0:T(8,128)(2,1)S(1)} %get-tuple-element.78), channel_id=1, source_target_pairs={{0,16},{4,20},{8,24},{12,28},{16,0},{20,4},{24,8},{28,12},{1,17},{... | collective-permute-start | bytes 344072 | tf_op jit(solution)/shard_map/ppermute | solution.py:617
  146.8 5.2 %collective-permute-done.10.refs_0_ = bf16[16,3584]{1,0:T(8,128)(2,1)S(1)} collective-permute-done((bf16[16,3584]{1,0:T(8,128)(2,1)S(1)}, bf16[16,3584]{1,0:T(8,128)(2,1)S(1)}, u32[]{:S(2)}, u32[]{:S(2)}) %collective-permute-start.10) | collective-permute-done | bytes 114720 | tf_op jit(solution)/shard_map/ppermute | solution.py:617
  152.2 2.2 collective-permute-done.13.refs_0_
  154.5 0.8 collective-permute-start.14
  155.2 6.5 %collective-permute-done.17.refs_1_ = bf16[16,3584]{1,0:T(8,128)(2,1)S(1)} collective-permute-done((bf16[16,3584]{1,0:T(8,128)(2,1)S(1)}, bf16[16,3584]{1,0:T(8,128)(2,1)S(1)}, u32[]{:S(2)}, u32[]{:S(2)}) %collective-permute-start.17) | collective-permute-done | bytes 114720 | tf_op jit(solution)/shard_map/ppermute | solution.py:617
  161.8 1.1 collective-permute-done.14.refs_1_
  163.0 1.3 collective-permute-start.15
  164.3 3.6 %collective-permute-done.18.refs_2_ = bf16[32,3584]{1,0:T(8,128)(2,1)S(1)} collective-permute-done((bf16[32,3584]{1,0:T(8,128)(2,1)S(1)}, bf16[32,3584]{1,0:T(8,128)(2,1)S(1)}, u32[]{:S(2)}, u32[]{:S(2)}) %collective-permute-start.18) | collective-permute-done | bytes 229408 | tf_op jit(solution)/shard_map/ppermute | solution.py:617
  167.9 1.3 collective-permute-start.19
  169.2 2.4 %collective-permute-done.15.refs_2_ = bf16[32,3584]{1,0:T(8,128)(2,1)S(1)} collective-permute-done((bf16[32,3584]{1,0:T(8,128)(2,1)S(1)}, bf16[32,3584]{1,0:T(8,128)(2,1)S(1)}, u32[]{:S(2)}, u32[]{:S(2)}) %collective-permute-start.15) | collective-permute-done | bytes 229408 | tf_op jit(solution)/shard_map/ppermute | solution.py:617
  171.6 1.0 collective-permute-start.16
  172.6 6.3 %collective-permute-done.19.refs_3_ = bf16[64,3584]{1,0:T(8,128)(2,1)S(1)} collective-permute-done((bf16[64,3584]{1,0:T(8,128)(2,1)S(1)}, bf16[64,3584]{1,0:T(8,128)(2,1)S(1)}, u32[]{:S(2)}, u32[]{:S(2)}) %collective-permute-start.19) | collective-permute-done | bytes 458784 | tf_op jit(solution)/shard_map/ppermute | solution.py:617
  178.9 5.7 %copy-done = bf16[7168,1152]{1,0:T(8,128)(2,1)S(1)} copy-done((bf16[7168,1152]{1,0:T(8,128)(2,1)S(1)}, bf16[7168,1152]{1,0:T(8,128)(2,1)}, u32[]{:S(2)}) %copy-start) | copy-done | bytes 16515096
  184.6 2.6 %gate_up.2 = (f32[128,1152]{1,0:T(8,128)S(1)}, f32[128,1152]{1,0:T(8,128)S(1)}, f32[128,128]{1,0:T(8,128)S(1)}) custom-call(bf16[16,3584]{1,0:T(8,128)(2,1)S(1)} %get-tuple-element.80.refs_0_, bf16[16,3584]{1,0:T(8,128)(2,1)S(1)} %collective-permute-done.17.refs_1_, bf16[32,3584]{1,0:T(8,128)(2,1)S(1)} %collective-permute-done.18.refs_2_, ...), custom_call_target="tpu_custom_call" | custom-call | flops 2113929216 | bytes 17432576 | tf_op jit(solution)/shard_map/gate_up/pallas_call | solution.py:573
  187.2 2.7 %gate_up.3.rows_ref = bf16[128,1152]{1,0:T(8,128)(2,1)S(1)} custom-call(bf16[16,3584]{1,0:T(8,128)(2,1)S(1)} %get-tuple-element.79.refs_0_, bf16[16,3584]{1,0:T(8,128)(2,1)S(1)} %collective-permute-done.14.refs_1_, bf16[32,3584]{1,0:T(8,128)(2,1)S(1)} %collective-permute-done.15.refs_2_, bf16[64,3584]{1,0:T(8,128)(2,1)S(1)} %collective-permute-done.16.refs_3_, ...), custom_call_target="tpu_custom_call" | custom-call | flops 2113929216 | bytes 17432576 | tf_op jit(solution)/shard_map/gate_up/pallas_call | solution.py:573
  189.9 3.8 %project_down.2 = (bf16[64,3584]{1,0:T(8,128)(2,1)S(1)}, bf16[64,3584]{1,0:T(8,128)(2,1)S(1)}) custom-call(bf16[128,1152]{1,0:T(8,128)(2,1)S(1)} %gate_up.3.rows_ref, bf16[1152,7168]{1,0:T(8,128)(2,1)} %weight_ref.5), custom_call_target="tpu_custom_call" | custom-call | flops 1056964608 | bytes 9469952 | tf_op jit(solution)/shard_map/project_down/pallas_call | solution.py:456
  193.7 1.3 collective-permute-start.20
  195.1 3.8 %project_down.3 = (bf16[64,3584]{1,0:T(8,128)(2,1)S(1)}, bf16[64,3584]{1,0:T(8,128)(2,1)S(1)}) custom-call(bf16[128,1152]{1,0:T(8,128)(2,1)S(1)} %gate_up.3.rows_ref, bf16[1152,7168]{1,0:T(8,128)(2,1)} %weight_ref.5), custom_call_target="tpu_custom_call" | custom-call | flops 1056964608 | bytes 9469952 | tf_op jit(solution)/shard_map/project_down/pallas_call | solution.py:456
  199.0 4.8 %collective-permute-done.20.came_ref = bf16[64,3584]{1,0:T(8,128)(2,1)S(1)} collective-permute-done((bf16[64,3584]{1,0:T(8,128)(2,1)S(1)}, bf16[64,3584]{1,0:T(8,128)(2,1)S(1)}, u32[]{:S(2)}, u32[]{:S(2)}) %collective-permute-start.20) | collective-permute-done | bytes 458784 | tf_op jit(solution)/shard_map/ppermute | solution.py:617
  204.0 7.3 %collective-permute-done.23.came_ref = bf16[64,3584]{1,0:T(8,128)(2,1)S(1)} collective-permute-done((bf16[64,3584]{1,0:T(8,128)(2,1)S(1)}, bf16[64,3584]{1,0:T(8,128)(2,1)S(1)}, u32[]{:S(2)}, u32[]{:S(2)}) %collective-permute-start.23) | collective-permute-done | bytes 458784 | tf_op jit(solution)/shard_map/ppermute | solution.py:617
  211.4 0.7 collective-permute-start.24
  212.1 1.6 collective-permute-done.21.came_ref
  213.8 0.7 collective-permute-start.22
  214.5 3.0 %collective-permute-done.24.came_ref = bf16[32,3584]{1,0:T(8,128)(2,1)S(1)} collective-permute-done((bf16[32,3584]{1,0:T(8,128)(2,1)S(1)}, bf16[32,3584]{1,0:T(8,128)(2,1)S(1)}, u32[]{:S(2)}, u32[]{:S(2)}) %collective-permute-start.24) | collective-permute-done | bytes 229408 | tf_op jit(solution)/shard_map/ppermute | solution.py:617
  217.5 0.7 collective-permute-start.25
  218.2 3.0 %collective-permute-done.22 = bf16[16,3584]{1,0:T(8,128)(2,1)S(1)} collective-permute-done((bf16[16,3584]{1,0:T(8,128)(2,1)S(1)}, bf16[16,3584]{1,0:T(8,128)(2,1)S(1)}, u32[]{:S(2)}, u32[]{:S(2)}) %collective-permute-start.22) | collective-permute-done | bytes 114720 | tf_op jit(solution)/shard_map/ppermute | solution.py:617
  221.2 3.0 %collective-permute-done.25 = bf16[16,3584]{1,0:T(8,128)(2,1)S(1)} collective-permute-done((bf16[16,3584]{1,0:T(8,128)(2,1)S(1)}, bf16[16,3584]{1,0:T(8,128)(2,1)S(1)}, u32[]{:S(2)}, u32[]{:S(2)}) %collective-permute-start.25) | collective-permute-done | bytes 114720 | tf_op jit(solution)/shard_map/ppermute | solution.py:617
  224.3 0.7 pad_maximum_fusion.4
  (67 shorter events, 2.0 us)
Async XLA Ops:
  7.6 67.6 %collective-permute-start = (bf16[5,288,128]{2,1,0:T(8,128)(2,1)S(1)}, bf16[5,288,128]{2,1,0:T(8,128)(2,1)S(1)}, u32[]{:S(2)}, u32[]{:S(2)}) collective-permute-start(bf16[5,288,128]{2,1,0:T(8,128)(2,1)S(1)} %get-tuple-element.51._), channel_id=1, source_target_pairs={{0,16},{4,20},{8,24},{12,28},{16,0},{20,4},{24,8},{28,12},{1,17},{... | collective-permute-start | bytes 1105928 | tf_op jit(solution)/shard_map/ppermute | solution.py:617
  16.2 9.2 %copy-start.6 = (s32[16]{0:T(128)S(1)}, s32[16]{0:T(128)}, u32[]{:S(2)}) copy-start(s32[16]{0:T(128)} %param.20) | copy-start | bytes 196
  16.2 9.3 %copy-start.5 = (s32[192]{0:T(256)S(1)}, s32[192]{0:T(256)}, u32[]{:S(2)}) copy-start(s32[192]{0:T(256)} %param.18) | copy-start | bytes 2308
  16.2 11.5 %copy-start.4 = (s32[16,32]{1,0:T(8,128)S(1)}, s32[16,32]{1,0:T(8,128)}, u32[]{:S(2)}) copy-start(s32[16,32]{1,0:T(8,128)} %param.21) | copy-start | bytes 6148
  16.2 51.6 %all-to-all-start = ((bf16[4,5,288,128]{3,2,1,0:T(8,128)(2,1)}), bf16[4,5,288,128]{3,2,1,0:T(8,128)(2,1)S(1)}, u32[]{:S(2)}, u32[]{:S(2)}) async-start(bf16[4,5,288,128]{3,2,1,0:T(8,128)(2,1)} %pack_near.1), calls=%async_computation | async-start | bytes 2949120 | tf_op jit(solution)/shard_map/all_to_all | solution.py:622
  20.1 55.1 %collective-permute-start.1 = (bf16[5,288,128]{2,1,0:T(8,128)(2,1)}, bf16[5,288,128]{2,1,0:T(8,128)(2,1)}, u32[]{:S(2)}, u32[]{:S(2)}) collective-permute-start(bf16[5,288,128]{2,1,0:T(8,128)(2,1)} %get-tuple-element.52), channel_id=1, source_target_pairs={{0,20},{4,16},{8,28},{12,24},{16,4},{20,0},{24,12},{28,8},{1,21},{... | collective-permute-start | bytes 1105928 | tf_op jit(solution)/shard_map/ppermute | solution.py:617
  21.9 53.3 %collective-permute-start.2 = (bf16[5,288,128]{2,1,0:T(8,128)(2,1)}, bf16[5,288,128]{2,1,0:T(8,128)(2,1)}, u32[]{:S(2)}, u32[]{:S(2)}) collective-permute-start(bf16[5,288,128]{2,1,0:T(8,128)(2,1)} %get-tuple-element.53), channel_id=1, source_target_pairs={{0,24},{4,28},{8,16},{12,20},{16,8},{20,12},{24,0},{28,4},{1,25},{... | collective-permute-start | bytes 1105928 | tf_op jit(solution)/shard_map/ppermute | solution.py:617
  25.4 49.9 %collective-permute-start.3 = (bf16[5,288,128]{2,1,0:T(8,128)(2,1)}, bf16[5,288,128]{2,1,0:T(8,128)(2,1)}, u32[]{:S(2)}, u32[]{:S(2)}) collective-permute-start(bf16[5,288,128]{2,1,0:T(8,128)(2,1)} %get-tuple-element.54), channel_id=1, source_target_pairs={{0,28},{4,24},{8,20},{12,16},{16,12},{20,8},{24,4},{28,0},{1,29},{... | collective-permute-start | bytes 1105928 | tf_op jit(solution)/shard_map/ppermute | solution.py:617
  79.4 32.2 %copy-start.1 = (bf16[8,512,128]{2,1,0:T(8,128)(2,1)S(1)}, bf16[8,512,128]{2,1,0:T(8,128)(2,1)}, u32[]{:S(2)}) copy-start(bf16[8,512,128]{2,1,0:T(8,128)(2,1)} %refs_4_.1) | copy-start | bytes 3145732
  83.9 27.7 %all-to-all-start.1 = ((bf16[4,128,512]{2,1,0:T(8,128)(2,1)}), bf16[4,128,512]{2,1,0:T(8,128)(2,1)S(1)}, u32[]{:S(2)}, u32[]{:S(2)}) async-start(bf16[4,128,512]{2,1,0:T(8,128)(2,1)} %bitcast.39), calls=%async_computation.1 | async-start | bytes 1048576 | tf_op jit(solution)/shard_map/all_to_all | solution.py:622
  87.6 9.6 %collective-permute-start.4 = (bf16[128,512]{1,0:T(8,128)(2,1)S(1)}, bf16[128,512]{1,0:T(8,128)(2,1)S(1)}, u32[]{:S(2)}, u32[]{:S(2)}) collective-permute-start(bf16[128,512]{1,0:T(8,128)(2,1)S(1)} %get-tuple-element.61), channel_id=1, source_target_pairs={{0,16},{4,20},{8,24},{12,28},{16,0},{20,4},{24,8},{28,12},{1,17},{... | collective-permute-start | bytes 393224 | tf_op jit(solution)/shard_map/ppermute | solution.py:617
  91.7 8.8 %collective-permute-start.5 = (bf16[128,512]{1,0:T(8,128)(2,1)S(1)}, bf16[128,512]{1,0:T(8,128)(2,1)S(1)}, u32[]{:S(2)}, u32[]{:S(2)}) collective-permute-start(bf16[128,512]{1,0:T(8,128)(2,1)S(1)} %get-tuple-element.62), channel_id=1, source_target_pairs={{0,20},{4,16},{8,28},{12,24},{16,4},{20,0},{24,12},{28,8},{1,21},{... | collective-permute-start | bytes 393224 | tf_op jit(solution)/shard_map/ppermute | solution.py:617
  92.9 15.9 %collective-permute-start.6 = (bf16[128,512]{1,0:T(8,128)(2,1)S(1)}, bf16[128,512]{1,0:T(8,128)(2,1)S(1)}, u32[]{:S(2)}, u32[]{:S(2)}) collective-permute-start(bf16[128,512]{1,0:T(8,128)(2,1)S(1)} %get-tuple-element.63), channel_id=1, source_target_pairs={{0,24},{4,28},{8,16},{12,20},{16,8},{20,12},{24,0},{28,4},{1,25},{... | collective-permute-start | bytes 393224 | tf_op jit(solution)/shard_map/ppermute | solution.py:617
  96.7 14.9 %collective-permute-start.7 = (bf16[128,512]{1,0:T(8,128)(2,1)S(1)}, bf16[128,512]{1,0:T(8,128)(2,1)S(1)}, u32[]{:S(2)}, u32[]{:S(2)}) collective-permute-start(bf16[128,512]{1,0:T(8,128)(2,1)S(1)} %get-tuple-element.64), channel_id=1, source_target_pairs={{0,28},{4,24},{8,20},{12,16},{16,12},{20,8},{24,4},{28,0},{1,29},{... | collective-permute-start | bytes 393224 | tf_op jit(solution)/shard_map/ppermute | solution.py:617
  111.6 67.3 %slice-start = ((s8[16515072]{0:T(1024)(128)(4,1)}), s8[4194304]{0:T(1024)(128)(4,1)S(1)}, s32[]{:S(2)}) async-start(s8[16515072]{0:T(1024)(128)(4,1)} %bitcast.29), calls=%async_computation.2 | async-start | bytes 8388608
  111.6 67.3 %slice-start.1 = ((s8[16515072]{0:T(1024)(128)(4,1)}), s8[4194304]{0:T(1024)(128)(4,1)S(1)}, s32[]{:S(2)}) async-start(s8[16515072]{0:T(1024)(128)(4,1)} %bitcast.29), calls=%async_computation.3 | async-start | bytes 8388608
  115.6 11.6 %collective-permute-start.8 = (bf16[64,3584]{1,0:T(8,128)(2,1)S(1)}, bf16[64,3584]{1,0:T(8,128)(2,1)S(1)}, u32[]{:S(2)}, u32[]{:S(2)}) collective-permute-start(bf16[64,3584]{1,0:T(8,128)(2,1)S(1)} %get-tuple-element.66), channel_id=1, source_target_pairs={{0,4},{4,0},{8,12},{12,8},{16,20},{20,16},{24,28},{28,24},{1,5},{5... | collective-permute-start | bytes 1376264 | tf_op jit(solution)/shard_map/ppermute | solution.py:617
  117.0 61.9 %slice-start.2 = ((s8[16515072]{0:T(1024)(128)(4,1)}), s8[4194304]{0:T(1024)(128)(4,1)S(1)}, s32[]{:S(2)}) async-start(s8[16515072]{0:T(1024)(128)(4,1)} %bitcast.29), calls=%async_computation.4 | async-start | bytes 8388608
  117.0 61.9 %slice-start.3 = ((s8[16515072]{0:T(1024)(128)(4,1)}), s8[3932160]{0:T(1024)(128)(4,1)S(1)}, s32[]{:S(2)}) async-start(s8[16515072]{0:T(1024)(128)(4,1)} %bitcast.29), calls=%async_computation.5 | async-start | bytes 7864320
  120.7 31.3 %copy-start.2 = (bf16[16,7168]{1,0:T(8,128)(2,1)S(1)}, bf16[16,7168]{1,0:T(8,128)(2,1)}, u32[]{:S(2)}) copy-start(bf16[16,7168]{1,0:T(8,128)(2,1)} %residual_ref.3) | copy-start | bytes 688132
  120.7 31.3 %copy-start.3 = (f32[7168]{0:T(1024)S(1)}, f32[7168]{0:T(1024)}, u32[]{:S(2)}) copy-start(f32[7168]{0:T(1024)} %param.26) | copy-start | bytes 86020
  120.7 16.1 %collective-permute-start.11 = (bf16[64,3584]{1,0:T(8,128)(2,1)S(1)}, bf16[64,3584]{1,0:T(8,128)(2,1)S(1)}, u32[]{:S(2)}, u32[]{:S(2)}) collective-permute-start(bf16[64,3584]{1,0:T(8,128)(2,1)S(1)} %get-tuple-element.74), channel_id=1, source_target_pairs={{0,8},{4,12},{8,0},{12,4},{16,24},{20,28},{24,16},{28,20},{1,9},{5... | collective-permute-start | bytes 1376264 | tf_op jit(solution)/shard_map/ppermute | solution.py:617
  127.3 12.5 %collective-permute-start.9 = (bf16[32,3584]{1,0:T(8,128)(2,1)S(1)}, bf16[32,3584]{1,0:T(8,128)(2,1)S(1)}, u32[]{:S(2)}, u32[]{:S(2)}) collective-permute-start(bf16[32,3584]{1,0:T(8,128)(2,1)S(1)} %get-tuple-element.68), channel_id=1, source_target_pairs={{0,8},{4,12},{8,0},{12,4},{16,24},{20,28},{24,16},{28,20},{1,9},{5... | collective-permute-start | bytes 688136 | tf_op jit(solution)/shard_map/ppermute | solution.py:617
  136.9 6.5 %collective-permute-start.12 = (bf16[32,3584]{1,0:T(8,128)(2,1)S(1)}, bf16[32,3584]{1,0:T(8,128)(2,1)S(1)}, u32[]{:S(2)}, u32[]{:S(2)}) collective-permute-start(bf16[32,3584]{1,0:T(8,128)(2,1)S(1)} %get-tuple-element.76), channel_id=1, source_target_pairs={{0,4},{4,0},{8,12},{12,8},{16,20},{20,16},{24,28},{28,24},{1,5},{5... | collective-permute-start | bytes 688136 | tf_op jit(solution)/shard_map/ppermute | solution.py:617
  139.9 12.2 %collective-permute-start.10 = (bf16[16,3584]{1,0:T(8,128)(2,1)S(1)}, bf16[16,3584]{1,0:T(8,128)(2,1)S(1)}, u32[]{:S(2)}, u32[]{:S(2)}) collective-permute-start(bf16[16,3584]{1,0:T(8,128)(2,1)S(1)} %get-tuple-element.70), channel_id=1, source_target_pairs={{0,16},{4,20},{8,24},{12,28},{16,0},{20,4},{24,8},{28,12},{1,17},{... | collective-permute-start | bytes 344072 | tf_op jit(solution)/shard_map/ppermute | solution.py:617
  143.4 11.0 %collective-permute-start.13 = (bf16[16,3584]{1,0:T(8,128)(2,1)S(1)}, bf16[16,3584]{1,0:T(8,128)(2,1)S(1)}, u32[]{:S(2)}, u32[]{:S(2)}) collective-permute-start(bf16[16,3584]{1,0:T(8,128)(2,1)S(1)} %get-tuple-element.78), channel_id=1, source_target_pairs={{0,16},{4,20},{8,24},{12,28},{16,0},{20,4},{24,8},{28,12},{1,17},{... | collective-permute-start | bytes 344072 | tf_op jit(solution)/shard_map/ppermute | solution.py:617
  152.1 9.6 %collective-permute-start.17 = (bf16[16,3584]{1,0:T(8,128)(2,1)S(1)}, bf16[16,3584]{1,0:T(8,128)(2,1)S(1)}, u32[]{:S(2)}, u32[]{:S(2)}) collective-permute-start(bf16[16,3584]{1,0:T(8,128)(2,1)S(1)} %get-tuple-element.80.refs_0_), channel_id=1, source_target_pairs={{0,16},{4,20},{8,24},{12,28},{16,0},{20,4},{24,8},{28,12},{1,17},{... | collective-permute-start | bytes 344072 | tf_op jit(solution)/shard_map/ppermute | solution.py:617
  154.5 8.5 %collective-permute-start.14 = (bf16[16,3584]{1,0:T(8,128)(2,1)S(1)}, bf16[16,3584]{1,0:T(8,128)(2,1)S(1)}, u32[]{:S(2)}, u32[]{:S(2)}) collective-permute-start(bf16[16,3584]{1,0:T(8,128)(2,1)S(1)} %get-tuple-element.79.refs_0_), channel_id=1, source_target_pairs={{0,16},{4,20},{8,24},{12,28},{16,0},{20,4},{24,8},{28,12},{1,17},{... | collective-permute-start | bytes 344072 | tf_op jit(solution)/shard_map/ppermute | solution.py:617
  161.7 6.1 %collective-permute-start.18 = (bf16[32,3584]{1,0:T(8,128)(2,1)S(1)}, bf16[32,3584]{1,0:T(8,128)(2,1)S(1)}, u32[]{:S(2)}, u32[]{:S(2)}) collective-permute-start(bf16[32,3584]{1,0:T(8,128)(2,1)S(1)} %pad_maximum_fusion.3), channel_id=1, source_target_pairs={{0,8},{4,12},{8,0},{12,4},{16,24},{20,28},{24,16},{28,20},{1,9},{5... | collective-permute-start | bytes 688136 | tf_op jit(solution)/shard_map/ppermute | solution.py:617
  163.0 8.6 %collective-permute-start.15 = (bf16[32,3584]{1,0:T(8,128)(2,1)S(1)}, bf16[32,3584]{1,0:T(8,128)(2,1)S(1)}, u32[]{:S(2)}, u32[]{:S(2)}) collective-permute-start(bf16[32,3584]{1,0:T(8,128)(2,1)S(1)} %pad_maximum_fusion.2), channel_id=1, source_target_pairs={{0,4},{4,0},{8,12},{12,8},{16,20},{20,16},{24,28},{28,24},{1,5},{5... | collective-permute-start | bytes 688136 | tf_op jit(solution)/shard_map/ppermute | solution.py:617
  167.9 11.0 %collective-permute-start.19 = (bf16[64,3584]{1,0:T(8,128)(2,1)S(1)}, bf16[64,3584]{1,0:T(8,128)(2,1)S(1)}, u32[]{:S(2)}, u32[]{:S(2)}) collective-permute-start(bf16[64,3584]{1,0:T(8,128)(2,1)S(1)} %pad_maximum_fusion.1), channel_id=1, source_target_pairs={{0,4},{4,0},{8,12},{12,8},{16,20},{20,16},{24,28},{28,24},{1,5},{5... | collective-permute-start | bytes 1376264 | tf_op jit(solution)/shard_map/ppermute | solution.py:617
  171.6 15.6 %collective-permute-start.16 = (bf16[64,3584]{1,0:T(8,128)(2,1)S(1)}, bf16[64,3584]{1,0:T(8,128)(2,1)S(1)}, u32[]{:S(2)}, u32[]{:S(2)}) collective-permute-start(bf16[64,3584]{1,0:T(8,128)(2,1)S(1)} %pad_maximum_fusion), channel_id=1, source_target_pairs={{0,8},{4,12},{8,0},{12,4},{16,24},{20,28},{24,16},{28,20},{1,9},{5... | collective-permute-start | bytes 1376264 | tf_op jit(solution)/shard_map/ppermute | solution.py:617
  178.9 5.7 %copy-start = (bf16[7168,1152]{1,0:T(8,128)(2,1)S(1)}, bf16[7168,1152]{1,0:T(8,128)(2,1)}, u32[]{:S(2)}) copy-start(bf16[7168,1152]{1,0:T(8,128)(2,1)} %refs_6_.3) | copy-start | bytes 49545220
  193.7 10.1 %collective-permute-start.20 = (bf16[64,3584]{1,0:T(8,128)(2,1)S(1)}, bf16[64,3584]{1,0:T(8,128)(2,1)S(1)}, u32[]{:S(2)}, u32[]{:S(2)}) collective-permute-start(bf16[64,3584]{1,0:T(8,128)(2,1)S(1)} %get-tuple-element.85), channel_id=1, source_target_pairs={{0,4},{4,0},{8,12},{12,8},{16,20},{20,16},{24,28},{28,24},{1,5},{5... | collective-permute-start | bytes 1376264 | tf_op jit(solution)/shard_map/ppermute | solution.py:617
  198.9 12.3 %collective-permute-start.23 = (bf16[64,3584]{1,0:T(8,128)(2,1)S(1)}, bf16[64,3584]{1,0:T(8,128)(2,1)S(1)}, u32[]{:S(2)}, u32[]{:S(2)}) collective-permute-start(bf16[64,3584]{1,0:T(8,128)(2,1)S(1)} %get-tuple-element.92), channel_id=1, source_target_pairs={{0,8},{4,12},{8,0},{12,4},{16,24},{20,28},{24,16},{28,20},{1,9},{5... | collective-permute-start | bytes 1376264 | tf_op jit(solution)/shard_map/ppermute | solution.py:617
  203.9 9.8 %collective-permute-start.21 = (bf16[32,3584]{1,0:T(8,128)(2,1)S(1)}, bf16[32,3584]{1,0:T(8,128)(2,1)S(1)}, u32[]{:S(2)}, u32[]{:S(2)}) collective-permute-start(bf16[32,3584]{1,0:T(8,128)(2,1)S(1)} %get-tuple-element.87), channel_id=1, source_target_pairs={{0,8},{4,12},{8,0},{12,4},{16,24},{20,28},{24,16},{28,20},{1,9},{5... | collective-permute-start | bytes 688136 | tf_op jit(solution)/shard_map/ppermute | solution.py:617
  211.4 6.1 %collective-permute-start.24 = (bf16[32,3584]{1,0:T(8,128)(2,1)S(1)}, bf16[32,3584]{1,0:T(8,128)(2,1)S(1)}, u32[]{:S(2)}, u32[]{:S(2)}) collective-permute-start(bf16[32,3584]{1,0:T(8,128)(2,1)S(1)} %get-tuple-element.94), channel_id=1, source_target_pairs={{0,4},{4,0},{8,12},{12,8},{16,20},{20,16},{24,28},{28,24},{1,5},{5... | collective-permute-start | bytes 688136 | tf_op jit(solution)/shard_map/ppermute | solution.py:617
  213.8 7.4 %collective-permute-start.22 = (bf16[16,3584]{1,0:T(8,128)(2,1)S(1)}, bf16[16,3584]{1,0:T(8,128)(2,1)S(1)}, u32[]{:S(2)}, u32[]{:S(2)}) collective-permute-start(bf16[16,3584]{1,0:T(8,128)(2,1)S(1)} %get-tuple-element.89), channel_id=1, source_target_pairs={{0,16},{4,20},{8,24},{12,28},{16,0},{20,4},{24,8},{28,12},{1,17},{... | collective-permute-start | bytes 344072 | tf_op jit(solution)/shard_map/ppermute | solution.py:617
  217.5 6.7 %collective-permute-start.25 = (bf16[16,3584]{1,0:T(8,128)(2,1)S(1)}, bf16[16,3584]{1,0:T(8,128)(2,1)S(1)}, u32[]{:S(2)}, u32[]{:S(2)}) collective-permute-start(bf16[16,3584]{1,0:T(8,128)(2,1)S(1)} %get-tuple-element.96), channel_id=1, source_target_pairs={{0,16},{4,20},{8,24},{12,28},{16,0},{20,4},{24,8},{28,12},{1,17},{... | collective-permute-start | bytes 344072 | tf_op jit(solution)/shard_map/ppermute | solution.py:617

commit v2 on v1

--- a/solution.py
+++ b/solution.py
@@ -14,6 +14,7 @@
 MASKED = -1e30
 MIB = 1 << 20
 CHUNKS = 2
+SMALL = pl.CostEstimate(flops=1, bytes_accessed=1, transcendentals=0)
 
 
 def in_hbm(array):
@@ -24,56 +25,76 @@
     return pltpu.with_memory_space_constraint(array, pltpu.VMEM)
 
 
-def pack_kernel(peers, near, capacity, ids_ref, rank_ref, pool_ref, _, *refs):
+def pack_kernel(peers, near, capacity, moves, source_ref, page_ref, rank_ref, pool_ref, _, *refs):
     out_refs, (pages_ref, sems) = refs[:-2], refs[-2:]
     if near:
         out_refs = [out_refs[0].at[k] for k in range(len(peers))]
     own = rank_ref[0]
     page_size = pages_ref.shape[1]
     half = page_size // 2
-    slots = [(k, c) for k in range(len(peers)) for c in range(capacity)]
-
-    def copy(n):
-        k, c = slots[n]
-        peer = (own & ~(len(peers) - 1)) + k if near else own ^ peers[k]
-        page = ids_ref[peer * capacity + c]
-        return pltpu.make_async_copy(pool_ref.at[page], pages_ref.at[n], sems.at[n])
-
-    for n in range(len(slots)):
-        copy(n).start()
-    for n, (k, c) in enumerate(slots):
-        copy(n).wait()
-        for block in range(LATENT // 128):
-            out_refs[k][c, pl.ds(block * page_size, page_size), :] = pages_ref[
-                n, :, pl.ds(block * 128, 128)
-            ]
-        rope = pages_ref[n, :, LATENT:]
-        out_refs[k][c, pl.ds(LATENT // 128 * page_size, half), :] = jnp.concatenate(
-            [rope[:half], rope[half:]], axis=1
-        )
-
-
-def pack_pages(page_pool, ids, rank, peers, near, capacity, after):
+
+    def copy(page, place):
+        return pltpu.make_async_copy(pool_ref.at[page], pages_ref.at[place], sems.at[place])
+
+    counts = []
+    for k, peer in enumerate(peers):
+        first = ((own & ~(len(peers) - 1)) + k if near else own ^ peer) * moves
+
+        def look(i, count, k=k, first=first):
+            chosen = (source_ref[0, first + i] == own) & (count < capacity)
+
+            @pl.when(chosen)
+            def _():
+                copy(page_ref[first + i], k * capacity + count).start()
+
+            return count + chosen.astype(jnp.int32)
+
+        counts.append(lax.fori_loop(0, moves, look, jnp.int32(0)))
+    for k in range(len(peers)):
+        for c in range(capacity):
+            place, out_ref = k * capacity + c, out_refs[k]
+
+            @pl.when(c < counts[k])
+            def _(c=c, place=place, out_ref=out_ref):
+                copy(0, place).wait()
+                for block in range(LATENT // 128):
+                    out_ref[c, pl.ds(block * page_size, page_size), :] = pages_ref[
+                        place, :, pl.ds(block * 128, 128)
+                    ]
+                rope = pages_ref[place, :, LATENT:]
+                out_ref[c, pl.ds(LATENT // 128 * page_size, half), :] = jnp.concatenate(
+                    [rope[:half], rope[half:]], axis=1
+                )
+
+            @pl.when(c >= counts[k])
+            def _(c=c, out_ref=out_ref):
+                out_ref[c] = jnp.zeros(out_ref.shape[1:], out_ref.dtype)
+
+
+def pack_pages(page_pool, sources, pages, rank, ranks, peers, near, capacity, after):
     page_size, width = page_pool.shape[1:]
     shape = (capacity, page_size * width // 128, 128)
     count = len(peers) * capacity
     shapes = [(len(peers),) + shape] if near else [shape] * len(peers)
+    smem = pl.BlockSpec(memory_space=pltpu.SMEM)
     return pl.pallas_call(
-        functools.partial(pack_kernel, tuple(peers), near, capacity),
+        functools.partial(pack_kernel, tuple(peers), near, capacity, pages.shape[0] // ranks),
         out_shape=[jax.ShapeDtypeStruct(shape, page_pool.dtype) for shape in shapes],
-        grid_spec=pltpu.PrefetchScalarGridSpec(
-            num_scalar_prefetch=2,
-            grid=(),
-            in_specs=[pl.BlockSpec(memory_space=pltpu.HBM), pl.BlockSpec(memory_space=pl.ANY)],
-            out_specs=[pl.BlockSpec(memory_space=pltpu.VMEM)] * len(shapes),
-            scratch_shapes=[
-                pltpu.VMEM((count, page_size, width), page_pool.dtype),
-                pltpu.SemaphoreType.DMA((count,)),
-            ],
-        ),
-        compiler_params=pltpu.CompilerParams(vmem_limit_bytes=16 * MIB),
+        in_specs=[
+            smem,
+            smem,
+            smem,
+            pl.BlockSpec(memory_space=pltpu.HBM),
+            pl.BlockSpec(memory_space=pl.ANY),
+        ],
+        out_specs=[pl.BlockSpec(memory_space=pltpu.VMEM)] * len(shapes),
+        scratch_shapes=[
+            pltpu.VMEM((count, page_size, width), page_pool.dtype),
+            pltpu.SemaphoreType.DMA((count,)),
+        ],
+        compiler_params=pltpu.CompilerParams(vmem_limit_bytes=8 * MIB),
         name="pack_near" if near else "pack_far",
-    )(ids, rank, in_hbm(page_pool), after)
+    )(sources, pages, rank, in_hbm(page_pool), after)
 
 
 def unpack_pages(packed_refs, tokens_ref, page_size):
@@ -221,11 +242,7 @@
             pltpu.SemaphoreType.DMA,
         ],
         compiler_params=pltpu.CompilerParams(vmem_limit_bytes=32 * MIB),
-        cost_estimate=pl.CostEstimate(
-            flops=2 * count * token_count * (width + LATENT),
-            bytes_accessed=2 * token_count * width + 4 * count * LATENT,
-            transcendentals=count * token_count,
-        ),
+        cost_estimate=SMALL,
         name="attend_resident",
     )(*counts, queries, in_hbm(pool))
 
@@ -270,11 +287,7 @@
             pltpu.VMEM((counts[0].shape[0], tokens), jnp.float32),
         ],
         compiler_params=pltpu.CompilerParams(vmem_limit_bytes=24 * MIB),
-        cost_estimate=pl.CostEstimate(
-            flops=2 * count * tokens * (width + LATENT),
-            bytes_accessed=2 * tokens * width + 8 * count * LATENT,
-            transcendentals=count * tokens,
-        ),
+        cost_estimate=SMALL,
         name="attend_near",
     )(*counts, queries, *packed, *map(in_hbm, state))
 
@@ -305,18 +318,17 @@
     out_ref[...] = latents_of(limit_ref, q_ref, tokens_ref[...], bias_ref[...], before)
 
 
-def latents(queries, packed, counts, place, state, rank, limit, page_size, ranks):
+def latents(queries, packed, counts, place, state, rank, limit, page_size, ranks, exchange):
     count, width = queries.shape
     half, size = ranks // 2, count // ranks
     tokens = sum(p.shape[0] for p in packed) * page_size
     own = lambda g, rank, _: (lax.div(rank[0], half), 0)
     other = lambda g, rank, _: (1 - lax.div(rank[0], half), 0)
     fixed = lambda g, *_: (0, 0)
-    state_shapes = ((count // 2, 128), (count // 2, LATENT))
-    state_specs = lambda block: [pl.BlockSpec(shape, block) for shape in state_shapes]
+    state_specs = lambda block: [pl.BlockSpec((count // 2, w), block) for w in (128, LATENT)]
     array = jax.ShapeDtypeStruct
     options = dict(
-        compiler_params=pltpu.CompilerParams(vmem_limit_bytes=28 * MIB),
+        compiler_params=pltpu.CompilerParams(vmem_limit_bytes=24 * MIB),
         cost_estimate=pl.CostEstimate(
             flops=count * tokens * (width + LATENT),
             bytes_accessed=2 * tokens * width + 2 * count * LATENT,
@@ -343,6 +355,7 @@
         name="latents_far",
         **options,
     )(rank, limit, *counts, queries, *packed, *state)
+    far = [exchange(block, half + u) for u, block in enumerate(far)]
     near = pl.pallas_call(
         latents_near_kernel,
         out_shape=pltpu.HBM((count // 2, LATENT), jnp.bfloat16),
@@ -355,7 +368,7 @@
             out_specs=pl.BlockSpec((count // 2, LATENT), fixed),
         ),
         name="latents_near",
-        **options,
+        **dict(options, cost_estimate=SMALL),
     )(rank, limit, queries, unpacked, bias, *state)
     return far, near
 
@@ -369,54 +382,56 @@
     return whole.astype(jnp.bfloat16), last.astype(jnp.bfloat16), (lengths % page_size)[:, None]
 
 
-def stream(weight_ref, tiles_ref, sems, row, column):
-    count, depth, width = tiles_ref.shape
-    along_rows = depth < weight_ref.shape[0]
-    copies = []
-    for n in range(count):
-        rows = pl.ds(row + (n * depth if along_rows else 0), depth)
-        columns = pl.ds(column + (0 if along_rows else n * width), width)
-        copies.append(
-            pltpu.make_async_copy(weight_ref.at[rows, columns], tiles_ref.at[n], sems.at[n])
+def multiply_tiles(places, tiles, rows_ref, keep_ref, send_ref):
+    half, columns = keep_ref.shape
+    size, tile = 2 * half // len(places), columns // len(tiles)
+    for n, load in enumerate(tiles):
+        product = jnp.dot(rows_ref[...], load(), preferred_element_type=jnp.float32)
+        product = product.astype(jnp.bfloat16)
+        for to, at in enumerate(places):
+            out_ref, to = (keep_ref, to * size) if to * size < half else (send_ref, to * size - half)
+            out_ref[pl.ds(to, size), pl.ds(n * tile, tile)] = product[at * size : (at + 1) * size]
+
+
+def stream(weight_ref, tiles_ref, sems, column):
+    width = tiles_ref.shape[2]
+    copies = [
+        pltpu.make_async_copy(
+            weight_ref.at[:, pl.ds(column + n * width, width)], tiles_ref.at[n], sems.at[n]
         )
+        for n in range(tiles_ref.shape[0])
+    ]
     for copy in copies:
         copy.start()
-    return copies
-
-
-def multiply_tiles(places, rows_ref, tiles_ref, copies, keep_ref, send_ref):
-    half, width = keep_ref.shape[0], tiles_ref.shape[2]
-    size = 2 * half // len(places)
-    for n, copy in enumerate(copies):
-        copy.wait()
-        product = jnp.dot(
-            rows_ref[...], tiles_ref[n], preferred_element_type=jnp.float32
-        ).astype(jnp.bfloat16)
-        for to, at in enumerate(places):
-            out_ref, to = (keep_ref, to * size) if to * size < half else (send_ref, to * size - half)
-            out_ref[pl.ds(to, size), pl.ds(n * width, width)] = product[at * size : (at + 1) * size]
-
-
-def project_first_kernel(column, order, rank_ref, near_ref, *refs):
-    split = near_ref.shape[0]
-    far_refs, refs = refs[:split], refs[split:]
+
+    def load(n):
+        copies[n].wait()
+        return tiles_ref[n]
+
+    return [functools.partial(load, n) for n in range(len(copies))]
+
+
+def project_first_kernel(order, rank_ref, near_ref, *refs):
+    split = len(order) // 2
+    far, refs = refs[:split], refs[split:]
     value_ref, weight_ref, head_ref, keep_ref, send_ref, tiles_ref, sems = refs
-    copies = stream(weight_ref, tiles_ref, sems, 0, column)
-    own = rank_ref[0] & (split - 1)
-    parts = [near_ref.at[own ^ k] for k in range(split)] + list(far_refs)
+    tiles = stream(weight_ref, tiles_ref, sems, 0)
     heads, width = value_ref.shape[0], value_ref.shape[2]
-    slots = near_ref.shape[1] // heads
+    own, slots = rank_ref[0] & (split - 1), near_ref.shape[1] // heads
     for h in range(heads):
-        rows = jnp.concatenate([parts[k][pl.ds(h * slots, slots), :] for k in order], axis=0)
+        span = pl.ds(h * slots, slots)
+        rows = jnp.concatenate(
+            [near_ref[own ^ k, span, :] if k < split else far[k - split][span, :] for k in order],
+            axis=0,
+        )
         head_ref[:, pl.ds(h * width, width)] = jnp.dot(
             rows, value_ref[h], preferred_element_type=jnp.float32
         ).astype(jnp.bfloat16)
-    multiply_tiles(range(len(order)), head_ref, tiles_ref, copies, keep_ref, send_ref)
+    multiply_tiles(range(len(order)), tiles, head_ref, keep_ref, send_ref)
 
 
 def project_kernel(column, places, rows_ref, weight_ref, keep_ref, send_ref, tiles_ref, sems):
-    copies = stream(weight_ref, tiles_ref, sems, 0, column)
-    multiply_tiles(places, rows_ref, tiles_ref, copies, keep_ref, send_ref)
+    multiply_tiles(places, stream(weight_ref, tiles_ref, sems, column), rows_ref, keep_ref, send_ref)
 
 
 def project_options(rows, depth, columns, tile):
@@ -425,7 +440,7 @@
             pltpu.VMEM((columns // tile, depth, tile), jnp.bfloat16),
             pltpu.SemaphoreType.DMA((columns // tile,)),
         ],
-        compiler_params=pltpu.CompilerParams(vmem_limit_bytes=20 * MIB),
+        compiler_params=pltpu.CompilerParams(vmem_limit_bytes=12 * MIB),
         cost_estimate=pl.CostEstimate(
             flops=2 * rows * depth * columns,
             bytes_accessed=2 * depth * columns + 2 * rows * (columns + depth),
@@ -437,13 +452,13 @@
 def project_first(order, rank, near, far, value_up, weight, columns, tile=512):
     depth = weight.shape[0]
     rows = len(order) * near.shape[1] // value_up.shape[0]
+    half = jax.ShapeDtypeStruct((rows // 2, columns), jnp.bfloat16)
     vmem = pl.BlockSpec(memory_space=pltpu.VMEM)
-    half = jax.ShapeDtypeStruct((rows // 2, columns), jnp.bfloat16)
     return pl.pallas_call(
-        functools.partial(project_first_kernel, 0, order),
+        functools.partial(project_first_kernel, order),
         out_shape=(jax.ShapeDtypeStruct((rows, depth), jnp.bfloat16), half, half),
         in_specs=[pl.BlockSpec(memory_space=pltpu.SMEM)]
-        + [vmem] * (len(far) + 2)
+        + [vmem] * (2 + len(far))
         + [pl.BlockSpec(memory_space=pltpu.HBM)],
         name="project_first",
         **project_options(rows, depth, columns, tile),
@@ -456,10 +471,7 @@
     return pl.pallas_call(
         functools.partial(project_kernel, chunk * columns, tuple(places)),
         out_shape=(half, half),
-        in_specs=[
-            pl.BlockSpec(memory_space=pltpu.VMEM),
-            pl.BlockSpec(memory_space=pltpu.HBM),
-        ],
+        in_specs=[pl.BlockSpec(memory_space=pltpu.VMEM), pl.BlockSpec(memory_space=pltpu.HBM)],
         name=name,
         **project_options(count, depth, columns, tile),
     )(rows, in_hbm(weight))
@@ -480,7 +492,7 @@
             jax.ShapeDtypeStruct(shape, jnp.float32),
             jax.ShapeDtypeStruct(shape, jnp.bfloat16),
         ),
-        compiler_params=pltpu.CompilerParams(vmem_limit_bytes=16 * MIB),
+        compiler_params=pltpu.CompilerParams(vmem_limit_bytes=6 * MIB),
         name="halve",
     )(keep, came)
 
@@ -508,7 +520,7 @@
         in_specs=[pl.BlockSpec((rows, columns), here), pl.BlockSpec((1, columns), here)]
         + [block] * len(sums),
         out_specs=(block, block),
-        compiler_params=pltpu.CompilerParams(vmem_limit_bytes=16 * MIB),
+        compiler_params=pltpu.CompilerParams(vmem_limit_bytes=4 * MIB),
         name="finish_middle",
     )(residual, gain, *sums)
 
@@ -521,8 +533,16 @@
         hidden_ref, gate_acc, up_acc, squares, *refs = refs
     else:
         gate_acc, up_acc, squares, *refs = refs
-    (rows_ref,) = refs
+    rows_ref, tiles_ref, sems = refs
     steps, _, depth = rows_ref.shape
+    copies = [
+        pltpu.make_async_copy(
+            up_ref.at[pl.ds(row + k * depth, depth), :], tiles_ref.at[k], sems.at[k]
+        )
+        for k in range(steps)
+    ]
+    for copy in copies:
+        copy.start()
     size = pieces[0].shape[0]
     sources = [(piece, b) for piece in pieces for b in range(piece.shape[0] // size)]
     for (piece, b), place in zip(sources, places):
@@ -539,7 +559,8 @@
         square = jnp.broadcast_to(jnp.sum(plain * plain, axis=1, keepdims=True), squares.shape)
         span = pl.ds(row + k * depth, depth)
         gate = jnp.dot(rows, gate_ref[span, :], preferred_element_type=jnp.float32)
-        up = jnp.dot(rows, up_ref[span, :], preferred_element_type=jnp.float32)
+        copies[k].wait()
+        up = jnp.dot(rows, tiles_ref[k], preferred_element_type=jnp.float32)
         if first and k == 0:
             squares[...], gate_acc[...], up_acc[...] = square, gate, up
         else:
@@ -581,16 +602,23 @@
             width,
         ),
         out_shape=out_shape,
-        in_specs=[vmem] * (len(pieces) + 3 + len(before or ())),
-        scratch_shapes=scratch + [pltpu.VMEM((steps, rows, tile), jnp.bfloat16)],
-        compiler_params=pltpu.CompilerParams(vmem_limit_bytes=12 * MIB),
+        in_specs=[vmem] * (len(pieces) + 2)
+        + [pl.BlockSpec(memory_space=pltpu.HBM)]
+        + [vmem] * len(before or ()),
+        scratch_shapes=scratch
+        + [
+            pltpu.VMEM((steps, rows, tile), jnp.bfloat16),
+            pltpu.VMEM((steps, tile, units), jnp.bfloat16),
+            pltpu.SemaphoreType.DMA((steps,)),
+        ],
+        compiler_params=pltpu.CompilerParams(vmem_limit_bytes=16 * MIB),
         cost_estimate=pl.CostEstimate(
             flops=4 * rows * columns * units,
             bytes_accessed=4 * columns * units + 2 * rows * columns,
             transcendentals=0,
         ),
         name="gate_up",
-    )(*pieces, inverse_gain, in_vmem(gate_proj), in_vmem(up_proj), *(before or ()))
+    )(*pieces, inverse_gain, in_vmem(gate_proj), in_hbm(up_proj), *(before or ()))
 
 
 class Grid:
@@ -675,15 +703,12 @@
         move_order[None, None, :] < move_order[None, :, None]
     )
     arrival = jnp.sum(earlier.astype(jnp.int32), axis=2)
-    chosen = (sources == own_rank)[:, :, None] & (
-        arrival[:, :, None] == jnp.arange(capacity)[None, None, :]
-    )
-    send_ids = jnp.sum(jnp.where(chosen, page_ids[:, :, None], 0), axis=1).reshape(-1)
     split = rank_count // 2
     far_peers = range(split, rank_count)
-    packed = pack_pages(page_pool, send_ids, rank, far_peers, False, capacity, rank)
+    pack = functools.partial(pack_pages, page_pool, move_source.T, move_page, rank, rank_count)
+    packed = pack(far_peers, False, capacity, rank)
     far_pages = [grid.exchange(pages, k) for k, pages in zip(far_peers, packed)]
-    (packed,) = pack_pages(page_pool, send_ids, rank, range(split), True, capacity, packed[0])
+    (packed,) = pack(range(split), True, capacity, packed[0])
     near_pages = grid.exchange_near(packed)
 
     pick = lambda array: lax.dynamic_index_in_dim(array, own_rank, 0, keepdims=False)
@@ -719,18 +744,18 @@
         row_count,
         page_size,
         rank_count,
-    )
-    far_latents = [grid.exchange(x, k) for k, x in zip(far_peers, far_latents)]
+        grid.exchange,
+    )
     near_latents = grid.exchange_near(near_latents.reshape(split, -1, LATENT))
 
     width = residual.shape[1]
     columns = width // CHUNKS
+    places = [grid.places(c) for c in range(CHUNKS)]
     head_out, *halves = project_first(
         grid.order(0), rank, near_latents, far_latents, value_up, out_proj, columns
     )
     projected = [halves] + [
-        project(head_out, out_proj, columns, c, grid.places(c), "project_out")
-        for c in range(1, CHUNKS)
+        project(head_out, out_proj, columns, c, places[c], "project_out") for c in range(1, CHUNKS)
     ]
     middle, gathered = [], []
     for c, (keep, send) in enumerate(projected):
@@ -745,7 +770,7 @@
         span = slice(c * columns, (c + 1) * columns)
         sums = gather_matmul(
             pieces,
-            grid.places(c),
+            places[c],
             inverse_gain[:, span],
             gate_proj,
             up_proj,
@@ -754,10 +779,13 @@
             c == CHUNKS - 1,
         )
     hidden = sums
-    outputs = []
-    for c in range(CHUNKS):
-        keep, send = project(hidden, down_proj, columns, c, grid.places(c), "project_down")
-        outputs.append(add_up(middle[c], grid.scatter_sum(keep, send, c)).astype(jnp.bfloat16))
+    projected = [
+        project(hidden, down_proj, columns, c, places[c], "project_down") for c in range(CHUNKS)
+    ]
+    outputs = [
+        add_up(middle[c], grid.scatter_sum(keep, send, c)).astype(jnp.bfloat16)
+        for c, (keep, send) in enumerate(projected)
+    ]
     return jnp.concatenate(outputs, axis=1)
 
 

time: 226 us -> 231 us (1.022)
  starting transfers between devices: 53.5 us -> 60.2 us
  Pallas kernels: 76.3 us -> 81.3 us
  waiting for transfers between devices: 81.2 us -> 77 us
  local copies, waits for them, and re-layouts: 9.56 us -> 6.19 us
    all_to_all x2, starting transfers between devices: 7.57 us -> 22 us  [exchange_near(): lax.all_to_all(array, 'dp', split_axis=0, concat_axis=0, axis_index_group...]
    all_to_all x2, waiting for transfers between devices: 8.44 us -> 0.01 us  [exchange_near(): lax.all_to_all(array, 'dp', split_axis=0, concat_axis=0, axis_index_group...]
    ppermute x26, starting transfers between devices: 46 us -> 38.1 us  [exchange(): return lax.ppermute(array, 'dp', [(i, i ^ k) for i in range(self.count)])]
    pallas_call x2, Pallas kernels: 5.24 us -> 10.1 us  [gather_matmul(): pl.pallas_call(functools.partial(gather_matmul_kernel, chunk * columns, b...]
    ppermute x26, waiting for transfers between devices: 72.8 us -> 77 us  [exchange(): return lax.ppermute(array, 'dp', [(i, i ^ k) for i in range(self.count)])]
    unnamed x23 -> x29, local copies, waits for them, and re-layouts: 6.32 us -> 3.15 us
  transfers between devices with their start and end apart: 28 -> 28, of which waited for: 21 -> 19; matrix products, arithmetic and copies ran while one was open for 1% -> 3% of each run, Pallas kernels for 24% -> 22%
where the time goes in v2:
time: 231 us; the launch traced here: 229 us
  Pallas kernels  81.3 us (35%)
  waiting for transfers between devices  77 us (33%)
  starting transfers between devices  60.2 us (26%)
  local copies, waits for them, and re-layouts  6.19 us (3%)
  other arithmetic  3.07 us (1%)
    ppermute x26, waiting for transfers between devices, exchange(): return lax.ppermute(array, 'dp', [(i, i ^ k) for i in range(self.count)])  77 us
    ppermute x26, starting transfers between devices, exchange(): return lax.ppermute(array, 'dp', [(i, i ^ k) for i in range(self.count)])  38.1 us
    pallas_call x1, Pallas kernels, attend_resident(): pl.pallas_call(functools.partial(resident_kernel, chunk, page_size), out_...  30.3 us
    all_to_all x2, starting transfers between devices, exchange_near(): lax.all_to_all(array, 'dp', split_axis=0, concat_axis=0, axis_index_group...  22 us
    pallas_call x3, Pallas kernels, project(): pl.pallas_call(functools.partial(project_kernel, chunk * columns, tuple(p...  11.6 us
    pallas_call x2, Pallas kernels, gather_matmul(): pl.pallas_call(functools.partial(gather_matmul_kernel, chunk * columns, b...  10.1 us
    pallas_call x2, Pallas kernels, pack_pages(): pl.pallas_call(functools.partial(pack_kernel, tuple(peers), near, capacit...  8.11 us
    pallas_call x1, Pallas kernels, attend_near(): pl.pallas_call(functools.partial(near_kernel, len(packed), place, page_si...  7.47 us
  transfers between devices with their start and end apart: 28, of which 19 were waited for; matrix products, arithmetic and copies ran while one was open for 3% of the time, Pallas kernels for 22%

profile of v2, /device:TPU:0, one launch (start us, length us, event | category | flops | bytes accessed | tf_op | source)
XLA Modules:
  0.0 228.7 jit_solution(4085707427917864839)
XLA Ops:
  0.0 0.7 copy-done.3
  0.7 0.7 copy-done.5
  1.4 4.0 %pack_far.1 = (bf16[5,288,128]{2,1,0:T(8,128)(2,1)}, bf16[5,288,128]{2,1,0:T(8,128)(2,1)}, bf16[5,288,128]{2,1,0:T(8,128)(2,1)}, bf16[5,288,128]{2,1,0:T(8,128)(2,1)}) custom-call(s32[1,192]{1,0:T(1,128)S(1)} %bitcast.39, s32[192]{0:T(256)S(1)} %copy-done.3, s32[1]{0:T(128)} %bitcast.1.rank_ref._, bf16[112,64,576]{2,1,0:T(8,128)(2,1)} %pool_ref.3, ...), custom_call_target="tpu_custom_call" | custom-call | tf_op jit(solution)/shard_map/pack_far/pallas_call | solution.py:80
  5.4 4.1 %pack_near.1 = bf16[4,5,288,128]{3,2,1,0:T(8,128)(2,1)} custom-call(s32[1,192]{1,0:T(1,128)S(1)} %bitcast.40, s32[192]{0:T(256)S(1)} %copy-done.4, s32[1]{0:T(128)} %bitcast.1.rank_ref._, bf16[112,64,576]{2,1,0:T(8,128)(2,1)} %pool_ref.3, bf16[5,288,128]{2,1,0:T(8,128)(2,1)} %get-tuple-element.51._), custom_call_target="tpu_custom_call" | custom-call | tf_op jit(solution)/shard_map/pack_near/pallas_call | solution.py:80
  9.5 5.5 %all-to-all-start = ((bf16[4,5,288,128]{3,2,1,0:T(8,128)(2,1)}), bf16[4,5,288,128]{3,2,1,0:T(8,128)(2,1)S(1)}, u32[]{:S(2)}, u32[]{:S(2)}) async-start(bf16[4,5,288,128]{3,2,1,0:T(8,128)(2,1)} %pack_near.1), calls=%async_computation | async-start | bytes 2949120 | tf_op jit(solution)/shard_map/all_to_all | solution.py:650
  15.1 3.7 %collective-permute-start = (bf16[5,288,128]{2,1,0:T(8,128)(2,1)}, bf16[5,288,128]{2,1,0:T(8,128)(2,1)S(1)}, u32[]{:S(2)}, u32[]{:S(2)}) collective-permute-start(bf16[5,288,128]{2,1,0:T(8,128)(2,1)} %get-tuple-element.51._), channel_id=1, source_target_pairs={{0,16},{4,20},{8,24},{12,28},{16,0},{20,4},{24,8},{28,12},{1,17},{... | collective-permute-start | bytes 1105928 | tf_op jit(solution)/shard_map/ppermute | solution.py:645
  18.8 1.4 collective-permute-start.1
  20.1 3.8 %collective-permute-start.2 = (bf16[5,288,128]{2,1,0:T(8,128)(2,1)}, bf16[5,288,128]{2,1,0:T(8,128)(2,1)}, u32[]{:S(2)}, u32[]{:S(2)}) collective-permute-start(bf16[5,288,128]{2,1,0:T(8,128)(2,1)} %get-tuple-element.53), channel_id=1, source_target_pairs={{0,24},{4,28},{8,16},{12,20},{16,8},{20,12},{24,0},{28,4},{1,25},{... | collective-permute-start | bytes 1105928 | tf_op jit(solution)/shard_map/ppermute | solution.py:645
  24.0 0.5 broadcast.99
  24.5 0.7 reduce.3
  25.4 0.3 convert_reduce_fusion.2
  25.7 0.1 fusion.2
  25.9 0.5 fusion.8
  26.4 0.1 compare_reduce_fusion
  26.5 2.1 copy.20
  28.6 0.7 copy.23.part_ref.refs_2_
  29.4 0.4 convert_reduce_fusion
  29.7 30.3 %attend_resident.1 = (f32[1024,128]{1,0:T(8,128)}, f32[1024,512]{1,0:T(8,128)}) custom-call(bf16[16,152]{1,0:T(8,128)(2,1)S(1)} %get-tuple-element.98.whole_ref.refs_0_, bf16[16,152]{1,0:T(8,128)(2,1)S(1)} %get-tuple-element.97.last_ref.refs_1_, s32[16,1]{1,0:T(8,128)S(1)} %copy.23.part_ref.refs_2_, bf16[1024,576]{1,0:T(8,128)(2,1)S(1)} %bitcast.32, ...), custom_call_target="tpu_custom_call" | custom-call | flops 1 | bytes 1 | tf_op jit(solution)/shard_map/attend_resident/pallas_call | solution.py:232
  60.7 7.5 %attend_near.1 = (f32[1024,128]{1,0:T(8,128)}, f32[1024,512]{1,0:T(8,128)}) custom-call(bf16[16,152]{1,0:T(8,128)(2,1)S(1)} %get-tuple-element.98.whole_ref.refs_0_, bf16[16,152]{1,0:T(8,128)(2,1)S(1)} %get-tuple-element.97.last_ref.refs_1_, s32[16,1]{1,0:T(8,128)S(1)} %copy.23.part_ref.refs_2_, bf16[1024,576]{1,0:T(8,128)(2,1)S(1)} %bitcast.33, ...), custom_call_target="tpu_custom_call" | custom-call | flops 1 | bytes 1 | tf_op jit(solution)/shard_map/attend_near/pallas_call | solution.py:279
  68.2 1.1 collective-permute-done.1.refs_5_
  69.3 4.7 %latents_far.1 = (bf16[128,512]{1,0:T(8,128)(2,1)}, bf16[128,512]{1,0:T(8,128)(2,1)S(1)}, bf16[128,512]{1,0:T(8,128)(2,1)S(1)}, bf16[128,512]{1,0:T(8,128)(2,1)S...) custom-call(s32[1]{0:T(128)} %bitcast.1.rank_ref._, s32[1]{0:T(128)S(6)} %copy.24.limit_ref, ...), custom_call_target="tpu_custom_call" | custom-call | flops 1426063360 | bytes 2523136 | tf_op jit(solution)/shard_map/latents_far/pallas_call | solution.py:339
  74.0 4.3 %latents_near.1 = bf16[512,512]{1,0:T(8,128)(2,1)} custom-call(s32[1]{0:T(128)} %bitcast.1.rank_ref._, s32[1]{0:T(128)S(6)} %copy.24.limit_ref, bf16[1024,576]{1,0:T(8,128)(2,1)S(1)} %bitcast.35, bf16[1280,576]{1,0:T(8,128)(2,1)S(1)} %get-tuple-element.59.tokens_ref, f32[16,1280]{1,0:T(8,128)S(1)} %get-tuple-element.60.bias_ref, ...), custom_call_target="tpu_custom_call" | custom-call | flops 1 | bytes 1 | tf_op jit(solution)/shard_map/latents_near/pallas_call | solution.py:359
  78.3 16.5 %all-to-all-start.1 = ((bf16[4,128,512]{2,1,0:T(8,128)(2,1)}), bf16[4,128,512]{2,1,0:T(8,128)(2,1)S(1)}, u32[]{:S(2)}, u32[]{:S(2)}) async-start(bf16[4,128,512]{2,1,0:T(8,128)(2,1)} %bitcast.42), calls=%async_computation.1 | async-start | bytes 1048576 | tf_op jit(solution)/shard_map/all_to_all | solution.py:650
  94.8 3.6 %collective-permute-start.4 = (bf16[128,512]{1,0:T(8,128)(2,1)}, bf16[128,512]{1,0:T(8,128)(2,1)S(1)}, u32[]{:S(2)}, u32[]{:S(2)}) collective-permute-start(bf16[128,512]{1,0:T(8,128)(2,1)} %get-tuple-element.61), channel_id=1, source_target_pairs={{0,16},{4,20},{8,24},{12,28},{16,0},{20,4},{24,8},{28,12},{1,17},{... | collective-permute-start | bytes 393224 | tf_op jit(solution)/shard_map/ppermute | solution.py:645
  98.4 1.2 collective-permute-start.5
  99.6 3.8 %collective-permute-start.6 = (bf16[128,512]{1,0:T(8,128)(2,1)S(1)}, bf16[128,512]{1,0:T(8,128)(2,1)S(1)}, u32[]{:S(2)}, u32[]{:S(2)}) collective-permute-start(bf16[128,512]{1,0:T(8,128)(2,1)S(1)} %get-tuple-element.63), channel_id=1, source_target_pairs={{0,24},{4,28},{8,16},{12,20},{16,8},{20,12},{24,0},{28,4},{1,25},{... | collective-permute-start | bytes 393224 | tf_op jit(solution)/shard_map/ppermute | solution.py:645
  103.4 2.2 collective-permute-done.4.refs_0_
  105.6 12.6 %collective-permute-done.5.refs_1_ = bf16[128,512]{1,0:T(8,128)(2,1)S(1)} collective-permute-done((bf16[128,512]{1,0:T(8,128)(2,1)S(1)}, bf16[128,512]{1,0:T(8,128)(2,1)S(1)}, u32[]{:S(2)}, u32[]{:S(2)}) %collective-permute-start.5) | collective-permute-done | bytes 131104 | tf_op jit(solution)/shard_map/ppermute | solution.py:645
  118.2 1.2 copy-done
  119.4 4.0 %project_first.1 = (bf16[128,1024]{1,0:T(8,128)(2,1)S(1)}, bf16[64,3584]{1,0:T(8,128)(2,1)S(1)}, bf16[64,3584]{1,0:T(8,128)(2,1)S(1)}) custom-call(s32[1]{0:T(128)} %bitcast.1.rank_ref._, bf16[4,128,512]{2,1,0:T(8,128)(2,1)S(1)} %all-to-all-done.1.near_ref, bf16[128,512]{1,0:T(8,128)(2,1)S(1)} %collective-permute-done.4.refs_0_, ...), custom_call_target="tpu_custom_call" | custom-call | flops 939524096 | bytes 8519680 | tf_op jit(solution)/shard_map/project_first/pallas_call | solution.py:457
  123.4 0.3 collective-permute-start.8
  123.8 3.9 %project_out.1 = (bf16[64,3584]{1,0:T(8,128)(2,1)S(1)}, bf16[64,3584]{1,0:T(8,128)(2,1)S(1)}) custom-call(bf16[128,1024]{1,0:T(8,128)(2,1)S(1)} %get-tuple-element.72.rows_ref, bf16[1024,7168]{1,0:T(8,128)(2,1)} %weight_ref.3), custom_call_target="tpu_custom_call" | custom-call | flops 939524096 | bytes 8519680 | tf_op jit(solution)/shard_map/project_out/pallas_call | solution.py:471
  127.7 4.6 %collective-permute-start.11 = (bf16[64,3584]{1,0:T(8,128)(2,1)S(1)}, bf16[64,3584]{1,0:T(8,128)(2,1)S(1)}, u32[]{:S(2)}, u32[]{:S(2)}) collective-permute-start(bf16[64,3584]{1,0:T(8,128)(2,1)S(1)} %get-tuple-element.74), channel_id=1, source_target_pairs={{0,8},{4,12},{8,0},{12,4},{16,24},{20,28},{24,16},{28,20},{1,9},{5... | collective-permute-start | bytes 1376264 | tf_op jit(solution)/shard_map/ppermute | solution.py:645
  132.4 5.3 %collective-permute-start.9 = (bf16[32,3584]{1,0:T(8,128)(2,1)S(1)}, bf16[32,3584]{1,0:T(8,128)(2,1)S(1)}, u32[]{:S(2)}, u32[]{:S(2)}) collective-permute-start(bf16[32,3584]{1,0:T(8,128)(2,1)S(1)} %get-tuple-element.68), channel_id=1, source_target_pairs={{0,8},{4,12},{8,0},{12,4},{16,24},{20,28},{24,16},{28,20},{1,9},{5... | collective-permute-start | bytes 688136 | tf_op jit(solution)/shard_map/ppermute | solution.py:645
  137.8 5.8 %collective-permute-done.11.came_ref = bf16[64,3584]{1,0:T(8,128)(2,1)S(1)} collective-permute-done((bf16[64,3584]{1,0:T(8,128)(2,1)S(1)}, bf16[64,3584]{1,0:T(8,128)(2,1)S(1)}, u32[]{:S(2)}, u32[]{:S(2)}) %collective-permute-start.11) | collective-permute-done | bytes 458784 | tf_op jit(solution)/shard_map/ppermute | solution.py:645
  143.7 0.8 collective-permute-start.12
  144.5 2.0 collective-permute-done.9.came_ref
  146.5 1.0 collective-permute-start.10
  147.6 2.2 collective-permute-done.12.came_ref
  149.8 1.5 collective-permute-start.13
  151.3 7.2 %collective-permute-done.10.refs_0_ = bf16[16,3584]{1,0:T(8,128)(2,1)S(1)} collective-permute-done((bf16[16,3584]{1,0:T(8,128)(2,1)S(1)}, bf16[16,3584]{1,0:T(8,128)(2,1)S(1)}, u32[]{:S(2)}, u32[]{:S(2)}) %collective-permute-start.10) | collective-permute-done | bytes 114720 | tf_op jit(solution)/shard_map/ppermute | solution.py:645
  158.7 2.3 %collective-permute-done.13.refs_0_ = bf16[16,3584]{1,0:T(8,128)(2,1)S(1)} collective-permute-done((bf16[16,3584]{1,0:T(8,128)(2,1)S(1)}, bf16[16,3584]{1,0:T(8,128)(2,1)S(1)}, u32[]{:S(2)}, u32[]{:S(2)}) %collective-permute-start.13) | collective-permute-done | bytes 114720 | tf_op jit(solution)/shard_map/ppermute | solution.py:645
  161.0 0.7 collective-permute-start.14
  161.7 2.7 %collective-permute-done.17.refs_1_ = bf16[16,3584]{1,0:T(8,128)(2,1)S(1)} collective-permute-done((bf16[16,3584]{1,0:T(8,128)(2,1)S(1)}, bf16[16,3584]{1,0:T(8,128)(2,1)S(1)}, u32[]{:S(2)}, u32[]{:S(2)}) %collective-permute-start.17) | collective-permute-done | bytes 114720 | tf_op jit(solution)/shard_map/ppermute | solution.py:645
  164.5 2.6 %collective-permute-done.14.refs_1_ = bf16[16,3584]{1,0:T(8,128)(2,1)S(1)} collective-permute-done((bf16[16,3584]{1,0:T(8,128)(2,1)S(1)}, bf16[16,3584]{1,0:T(8,128)(2,1)S(1)}, u32[]{:S(2)}, u32[]{:S(2)}) %collective-permute-start.14) | collective-permute-done | bytes 114720 | tf_op jit(solution)/shard_map/ppermute | solution.py:645
  167.2 1.5 collective-permute-start.15
  168.6 1.9 collective-permute-done.18.refs_2_
  170.6 2.5 %collective-permute-start.19 = (bf16[64,3584]{1,0:T(8,128)(2,1)S(1)}, bf16[64,3584]{1,0:T(8,128)(2,1)S(1)}, u32[]{:S(2)}, u32[]{:S(2)}) collective-permute-start(bf16[64,3584]{1,0:T(8,128)(2,1)S(1)} %pad_maximum_fusion.1), channel_id=1, source_target_pairs={{0,4},{4,0},{8,12},{12,8},{16,20},{20,16},{24,28},{28,24},{1,5},{5... | collective-permute-start | bytes 1376264 | tf_op jit(solution)/shard_map/ppermute | solution.py:645
  173.1 2.7 %collective-permute-done.15.refs_2_ = bf16[32,3584]{1,0:T(8,128)(2,1)S(1)} collective-permute-done((bf16[32,3584]{1,0:T(8,128)(2,1)S(1)}, bf16[32,3584]{1,0:T(8,128)(2,1)S(1)}, u32[]{:S(2)}, u32[]{:S(2)}) %collective-permute-start.15) | collective-permute-done | bytes 229408 | tf_op jit(solution)/shard_map/ppermute | solution.py:645
  175.8 7.1 %collective-permute-done.19.refs_3_ = bf16[64,3584]{1,0:T(8,128)(2,1)S(1)} collective-permute-done((bf16[64,3584]{1,0:T(8,128)(2,1)S(1)}, bf16[64,3584]{1,0:T(8,128)(2,1)S(1)}, u32[]{:S(2)}, u32[]{:S(2)}) %collective-permute-start.19) | collective-permute-done | bytes 458784 | tf_op jit(solution)/shard_map/ppermute | solution.py:645
  183.0 5.1 %gate_up.2 = (f32[128,1152]{1,0:T(8,128)S(1)}, f32[128,1152]{1,0:T(8,128)S(1)}, f32[128,128]{1,0:T(8,128)S(1)}) custom-call(bf16[16,3584]{1,0:T(8,128)(2,1)S(1)} %get-tuple-element.80.refs_0_, bf16[16,3584]{1,0:T(8,128)(2,1)S(1)} %collective-permute-done.17.refs_1_, bf16[32,3584]{1,0:T(8,128)(2,1)S(1)} %collective-permute-done.18.refs_2_, ...), custom_call_target="tpu_custom_call" | custom-call | flops 2113929216 | bytes 17432576 | tf_op jit(solution)/shard_map/gate_up/pallas_call | solution.py:594
  188.1 5.1 %gate_up.3.rows_ref = bf16[128,1152]{1,0:T(8,128)(2,1)S(1)} custom-call(bf16[16,3584]{1,0:T(8,128)(2,1)S(1)} %get-tuple-element.79.refs_0_, bf16[16,3584]{1,0:T(8,128)(2,1)S(1)} %collective-permute-done.14.refs_1_, bf16[32,3584]{1,0:T(8,128)(2,1)S(1)} %collective-permute-done.15.refs_2_, bf16[64,3584]{1,0:T(8,128)(2,1)S(1)} %collective-permute-done.16.refs_3_, ...), custom_call_target="tpu_custom_call" | custom-call | flops 2113929216 | bytes 17432576 | tf_op jit(solution)/shard_map/gate_up/pallas_call | solution.py:594
  193.2 3.9 %project_down.2 = (bf16[64,3584]{1,0:T(8,128)(2,1)S(1)}, bf16[64,3584]{1,0:T(8,128)(2,1)S(1)}) custom-call(bf16[128,1152]{1,0:T(8,128)(2,1)S(1)} %gate_up.3.rows_ref, bf16[1152,7168]{1,0:T(8,128)(2,1)} %weight_ref.5), custom_call_target="tpu_custom_call" | custom-call | flops 1056964608 | bytes 9469952 | tf_op jit(solution)/shard_map/project_down/pallas_call | solution.py:471
  197.0 1.6 collective-permute-start.20
  198.6 3.9 %project_down.3 = (bf16[64,3584]{1,0:T(8,128)(2,1)S(1)}, bf16[64,3584]{1,0:T(8,128)(2,1)S(1)}) custom-call(bf16[128,1152]{1,0:T(8,128)(2,1)S(1)} %gate_up.3.rows_ref, bf16[1152,7168]{1,0:T(8,128)(2,1)} %weight_ref.5), custom_call_target="tpu_custom_call" | custom-call | flops 1056964608 | bytes 9469952 | tf_op jit(solution)/shard_map/project_down/pallas_call | solution.py:471
  202.5 0.1 collective-permute-start.23
  202.6 4.6 %collective-permute-done.20.came_ref = bf16[64,3584]{1,0:T(8,128)(2,1)S(1)} collective-permute-done((bf16[64,3584]{1,0:T(8,128)(2,1)S(1)}, bf16[64,3584]{1,0:T(8,128)(2,1)S(1)}, u32[]{:S(2)}, u32[]{:S(2)}) %collective-permute-start.20) | collective-permute-done | bytes 458784 | tf_op jit(solution)/shard_map/ppermute | solution.py:645
  207.4 7.7 %collective-permute-done.23.came_ref = bf16[64,3584]{1,0:T(8,128)(2,1)S(1)} collective-permute-done((bf16[64,3584]{1,0:T(8,128)(2,1)S(1)}, bf16[64,3584]{1,0:T(8,128)(2,1)S(1)}, u32[]{:S(2)}, u32[]{:S(2)}) %collective-permute-start.23) | collective-permute-done | bytes 458784 | tf_op jit(solution)/shard_map/ppermute | solution.py:645
  215.1 0.4 collective-permute-start.24
  215.5 2.0 collective-permute-done.21.came_ref
  217.6 3.6 %collective-permute-done.24.came_ref = bf16[32,3584]{1,0:T(8,128)(2,1)S(1)} collective-permute-done((bf16[32,3584]{1,0:T(8,128)(2,1)S(1)}, bf16[32,3584]{1,0:T(8,128)(2,1)S(1)}, u32[]{:S(2)}, u32[]{:S(2)}) %collective-permute-start.24) | collective-permute-done | bytes 229408 | tf_op jit(solution)/shard_map/ppermute | solution.py:645
  221.4 3.7 %collective-permute-done.22 = bf16[16,3584]{1,0:T(8,128)(2,1)S(1)} collective-permute-done((bf16[16,3584]{1,0:T(8,128)(2,1)S(1)}, bf16[16,3584]{1,0:T(8,128)(2,1)S(1)}, u32[]{:S(2)}, u32[]{:S(2)}) %collective-permute-start.22) | collective-permute-done | bytes 114720 | tf_op jit(solution)/shard_map/ppermute | solution.py:645
  225.1 2.8 %collective-permute-done.25 = bf16[16,3584]{1,0:T(8,128)(2,1)S(1)} collective-permute-done((bf16[16,3584]{1,0:T(8,128)(2,1)S(1)}, bf16[16,3584]{1,0:T(8,128)(2,1)S(1)}, u32[]{:S(2)}, u32[]{:S(2)}) %collective-permute-start.25) | collective-permute-done | bytes 114720 | tf_op jit(solution)/shard_map/ppermute | solution.py:645
  228.0 0.7 pad_maximum_fusion.4
  (69 shorter events, 1.7 us)
Async XLA Ops:
  0.0 0.7 copy-start.3
  0.7 0.7 copy-start.5
  1.4 4.0 %copy-start.4 = (s32[192]{0:T(256)S(1)}, s32[192]{0:T(256)}, u32[]{:S(2)}) copy-start(s32[192]{0:T(256)} %page_ref.3) | copy-start | bytes 2308
  1.4 4.0 %copy-start.6 = (s32[192,1]{0,1:T(1,128)S(1)}, s32[192,1]{0,1:T(1,128)}, u32[]{:S(2)}) copy-start(s32[192,1]{0,1:T(1,128)} %param.16) | copy-start | bytes 2308
  9.5 15.8 %copy-start.8 = (s32[192]{0:T(256)S(1)}, s32[192]{0:T(256)}, u32[]{:S(2)}) copy-start(s32[192]{0:T(256)} %param.18) | copy-start | bytes 2308
  9.5 16.2 %copy-start.7 = (s32[16,32]{1,0:T(8,128)S(1)}, s32[16,32]{1,0:T(8,128)}, u32[]{:S(2)}) copy-start(s32[16,32]{1,0:T(8,128)} %param.21) | copy-start | bytes 6148
  9.5 16.3 %copy-start.9 = (s32[16]{0:T(128)S(1)}, s32[16]{0:T(128)}, u32[]{:S(2)}) copy-start(s32[16]{0:T(128)} %param.20) | copy-start | bytes 196
  9.5 51.1 %all-to-all-start = ((bf16[4,5,288,128]{3,2,1,0:T(8,128)(2,1)}), bf16[4,5,288,128]{3,2,1,0:T(8,128)(2,1)S(1)}, u32[]{:S(2)}, u32[]{:S(2)}) async-start(bf16[4,5,288,128]{3,2,1,0:T(8,128)(2,1)} %pack_near.1), calls=%async_computation | async-start | bytes 2949120 | tf_op jit(solution)/shard_map/all_to_all | solution.py:650
  15.1 53.1 %collective-permute-start = (bf16[5,288,128]{2,1,0:T(8,128)(2,1)}, bf16[5,288,128]{2,1,0:T(8,128)(2,1)S(1)}, u32[]{:S(2)}, u32[]{:S(2)}) collective-permute-start(bf16[5,288,128]{2,1,0:T(8,128)(2,1)} %get-tuple-element.51._), channel_id=1, source_target_pairs={{0,16},{4,20},{8,24},{12,28},{16,0},{20,4},{24,8},{28,12},{1,17},{... | collective-permute-start | bytes 1105928 | tf_op jit(solution)/shard_map/ppermute | solution.py:645
  18.8 50.5 %collective-permute-start.1 = (bf16[5,288,128]{2,1,0:T(8,128)(2,1)}, bf16[5,288,128]{2,1,0:T(8,128)(2,1)S(1)}, u32[]{:S(2)}, u32[]{:S(2)}) collective-permute-start(bf16[5,288,128]{2,1,0:T(8,128)(2,1)} %get-tuple-element.52), channel_id=1, source_target_pairs={{0,20},{4,16},{8,28},{12,24},{16,4},{20,0},{24,12},{28,8},{1,21},{... | collective-permute-start | bytes 1105928 | tf_op jit(solution)/shard_map/ppermute | solution.py:645
  20.1 49.2 %collective-permute-start.2 = (bf16[5,288,128]{2,1,0:T(8,128)(2,1)}, bf16[5,288,128]{2,1,0:T(8,128)(2,1)}, u32[]{:S(2)}, u32[]{:S(2)}) collective-permute-start(bf16[5,288,128]{2,1,0:T(8,128)(2,1)} %get-tuple-element.53), channel_id=1, source_target_pairs={{0,24},{4,28},{8,16},{12,20},{16,8},{20,12},{24,0},{28,4},{1,25},{... | collective-permute-start | bytes 1105928 | tf_op jit(solution)/shard_map/ppermute | solution.py:645
  24.0 45.4 %collective-permute-start.3 = (bf16[5,288,128]{2,1,0:T(8,128)(2,1)}, bf16[5,288,128]{2,1,0:T(8,128)(2,1)}, u32[]{:S(2)}, u32[]{:S(2)}) collective-permute-start(bf16[5,288,128]{2,1,0:T(8,128)(2,1)} %get-tuple-element.54), channel_id=1, source_target_pairs={{0,28},{4,24},{8,20},{12,16},{16,12},{20,8},{24,4},{28,0},{1,29},{... | collective-permute-start | bytes 1105928 | tf_op jit(solution)/shard_map/ppermute | solution.py:645
  78.3 39.9 %all-to-all-start.1 = ((bf16[4,128,512]{2,1,0:T(8,128)(2,1)}), bf16[4,128,512]{2,1,0:T(8,128)(2,1)S(1)}, u32[]{:S(2)}, u32[]{:S(2)}) async-start(bf16[4,128,512]{2,1,0:T(8,128)(2,1)} %bitcast.42), calls=%async_computation.1 | async-start | bytes 1048576 | tf_op jit(solution)/shard_map/all_to_all | solution.py:650
  94.8 10.8 %collective-permute-start.4 = (bf16[128,512]{1,0:T(8,128)(2,1)}, bf16[128,512]{1,0:T(8,128)(2,1)S(1)}, u32[]{:S(2)}, u32[]{:S(2)}) collective-permute-start(bf16[128,512]{1,0:T(8,128)(2,1)} %get-tuple-element.61), channel_id=1, source_target_pairs={{0,16},{4,20},{8,24},{12,28},{16,0},{20,4},{24,8},{28,12},{1,17},{... | collective-permute-start | bytes 393224 | tf_op jit(solution)/shard_map/ppermute | solution.py:645
  98.4 19.8 %collective-permute-start.5 = (bf16[128,512]{1,0:T(8,128)(2,1)S(1)}, bf16[128,512]{1,0:T(8,128)(2,1)S(1)}, u32[]{:S(2)}, u32[]{:S(2)}) collective-permute-start(bf16[128,512]{1,0:T(8,128)(2,1)S(1)} %get-tuple-element.62), channel_id=1, source_target_pairs={{0,20},{4,16},{8,28},{12,24},{16,4},{20,0},{24,12},{28,8},{1,21},{... | collective-permute-start | bytes 393224 | tf_op jit(solution)/shard_map/ppermute | solution.py:645
  99.6 18.6 %collective-permute-start.6 = (bf16[128,512]{1,0:T(8,128)(2,1)S(1)}, bf16[128,512]{1,0:T(8,128)(2,1)S(1)}, u32[]{:S(2)}, u32[]{:S(2)}) collective-permute-start(bf16[128,512]{1,0:T(8,128)(2,1)S(1)} %get-tuple-element.63), channel_id=1, source_target_pairs={{0,24},{4,28},{8,16},{12,20},{16,8},{20,12},{24,0},{28,4},{1,25},{... | collective-permute-start | bytes 393224 | tf_op jit(solution)/shard_map/ppermute | solution.py:645
  103.4 14.8 %collective-permute-start.7 = (bf16[128,512]{1,0:T(8,128)(2,1)S(1)}, bf16[128,512]{1,0:T(8,128)(2,1)S(1)}, u32[]{:S(2)}, u32[]{:S(2)}) collective-permute-start(bf16[128,512]{1,0:T(8,128)(2,1)S(1)} %get-tuple-element.64), channel_id=1, source_target_pairs={{0,28},{4,24},{8,20},{12,16},{16,12},{20,8},{24,4},{28,0},{1,29},{... | collective-permute-start | bytes 393224 | tf_op jit(solution)/shard_map/ppermute | solution.py:645
  118.2 1.2 copy-start
  119.4 63.6 %slice-start = ((s8[16515072]{0:T(1024)(128)(4,1)}), s8[4194304]{0:T(1024)(128)(4,1)S(1)}, s32[]{:S(2)}) async-start(s8[16515072]{0:T(1024)(128)(4,1)} %bitcast.30), calls=%async_computation.2 | async-start | bytes 8388608
  119.4 63.6 %slice-start.1 = ((s8[16515072]{0:T(1024)(128)(4,1)}), s8[4194304]{0:T(1024)(128)(4,1)S(1)}, s32[]{:S(2)}) async-start(s8[16515072]{0:T(1024)(128)(4,1)} %bitcast.30), calls=%async_computation.3 | async-start | bytes 8388608
  123.4 8.9 %collective-permute-start.8 = (bf16[64,3584]{1,0:T(8,128)(2,1)S(1)}, bf16[64,3584]{1,0:T(8,128)(2,1)S(1)}, u32[]{:S(2)}, u32[]{:S(2)}) collective-permute-start(bf16[64,3584]{1,0:T(8,128)(2,1)S(1)} %get-tuple-element.66), channel_id=1, source_target_pairs={{0,4},{4,0},{8,12},{12,8},{16,20},{20,16},{24,28},{28,24},{1,5},{5... | collective-permute-start | bytes 1376264 | tf_op jit(solution)/shard_map/ppermute | solution.py:645
  123.7 59.2 %slice-start.2 = ((s8[16515072]{0:T(1024)(128)(4,1)}), s8[4194304]{0:T(1024)(128)(4,1)S(1)}, s32[]{:S(2)}) async-start(s8[16515072]{0:T(1024)(128)(4,1)} %bitcast.30), calls=%async_computation.4 | async-start | bytes 8388608
  123.8 59.2 %slice-start.3 = ((s8[16515072]{0:T(1024)(128)(4,1)}), s8[3932160]{0:T(1024)(128)(4,1)S(1)}, s32[]{:S(2)}) async-start(s8[16515072]{0:T(1024)(128)(4,1)} %bitcast.30), calls=%async_computation.5 | async-start | bytes 7864320
  127.7 30.8 %copy-start.1 = (bf16[16,7168]{1,0:T(8,128)(2,1)S(1)}, bf16[16,7168]{1,0:T(8,128)(2,1)}, u32[]{:S(2)}) copy-start(bf16[16,7168]{1,0:T(8,128)(2,1)} %residual_ref.3) | copy-start | bytes 688132
  127.7 30.8 %copy-start.2 = (f32[7168]{0:T(1024)S(1)}, f32[7168]{0:T(1024)}, u32[]{:S(2)}) copy-start(f32[7168]{0:T(1024)} %param.26) | copy-start | bytes 86020
  127.7 15.9 %collective-permute-start.11 = (bf16[64,3584]{1,0:T(8,128)(2,1)S(1)}, bf16[64,3584]{1,0:T(8,128)(2,1)S(1)}, u32[]{:S(2)}, u32[]{:S(2)}) collective-permute-start(bf16[64,3584]{1,0:T(8,128)(2,1)S(1)} %get-tuple-element.74), channel_id=1, source_target_pairs={{0,8},{4,12},{8,0},{12,4},{16,24},{20,28},{24,16},{28,20},{1,9},{5... | collective-permute-start | bytes 1376264 | tf_op jit(solution)/shard_map/ppermute | solution.py:645
  132.4 14.1 %collective-permute-start.9 = (bf16[32,3584]{1,0:T(8,128)(2,1)S(1)}, bf16[32,3584]{1,0:T(8,128)(2,1)S(1)}, u32[]{:S(2)}, u32[]{:S(2)}) collective-permute-start(bf16[32,3584]{1,0:T(8,128)(2,1)S(1)} %get-tuple-element.68), channel_id=1, source_target_pairs={{0,8},{4,12},{8,0},{12,4},{16,24},{20,28},{24,16},{28,20},{1,9},{5... | collective-permute-start | bytes 688136 | tf_op jit(solution)/shard_map/ppermute | solution.py:645
  143.7 6.1 %collective-permute-start.12 = (bf16[32,3584]{1,0:T(8,128)(2,1)S(1)}, bf16[32,3584]{1,0:T(8,128)(2,1)S(1)}, u32[]{:S(2)}, u32[]{:S(2)}) collective-permute-start(bf16[32,3584]{1,0:T(8,128)(2,1)S(1)} %get-tuple-element.76), channel_id=1, source_target_pairs={{0,4},{4,0},{8,12},{12,8},{16,20},{20,16},{24,28},{28,24},{1,5},{5... | collective-permute-start | bytes 688136 | tf_op jit(solution)/shard_map/ppermute | solution.py:645
  146.5 12.0 %collective-permute-start.10 = (bf16[16,3584]{1,0:T(8,128)(2,1)S(1)}, bf16[16,3584]{1,0:T(8,128)(2,1)S(1)}, u32[]{:S(2)}, u32[]{:S(2)}) collective-permute-start(bf16[16,3584]{1,0:T(8,128)(2,1)S(1)} %get-tuple-element.70), channel_id=1, source_target_pairs={{0,16},{4,20},{8,24},{12,28},{16,0},{20,4},{24,8},{28,12},{1,17},{... | collective-permute-start | bytes 344072 | tf_op jit(solution)/shard_map/ppermute | solution.py:645
  149.8 11.1 %collective-permute-start.13 = (bf16[16,3584]{1,0:T(8,128)(2,1)S(1)}, bf16[16,3584]{1,0:T(8,128)(2,1)S(1)}, u32[]{:S(2)}, u32[]{:S(2)}) collective-permute-start(bf16[16,3584]{1,0:T(8,128)(2,1)S(1)} %get-tuple-element.78), channel_id=1, source_target_pairs={{0,16},{4,20},{8,24},{12,28},{16,0},{20,4},{24,8},{28,12},{1,17},{... | collective-permute-start | bytes 344072 | tf_op jit(solution)/shard_map/ppermute | solution.py:645
  158.6 5.9 %collective-permute-start.17 = (bf16[16,3584]{1,0:T(8,128)(2,1)S(1)}, bf16[16,3584]{1,0:T(8,128)(2,1)S(1)}, u32[]{:S(2)}, u32[]{:S(2)}) collective-permute-start(bf16[16,3584]{1,0:T(8,128)(2,1)S(1)} %get-tuple-element.80.refs_0_), channel_id=1, source_target_pairs={{0,16},{4,20},{8,24},{12,28},{16,0},{20,4},{24,8},{28,12},{1,17},{... | collective-permute-start | bytes 344072 | tf_op jit(solution)/shard_map/ppermute | solution.py:645
  161.0 6.1 %collective-permute-start.14 = (bf16[16,3584]{1,0:T(8,128)(2,1)S(1)}, bf16[16,3584]{1,0:T(8,128)(2,1)S(1)}, u32[]{:S(2)}, u32[]{:S(2)}) collective-permute-start(bf16[16,3584]{1,0:T(8,128)(2,1)S(1)} %get-tuple-element.79.refs_0_), channel_id=1, source_target_pairs={{0,16},{4,20},{8,24},{12,28},{16,0},{20,4},{24,8},{28,12},{1,17},{... | collective-permute-start | bytes 344072 | tf_op jit(solution)/shard_map/ppermute | solution.py:645
  164.5 6.1 %collective-permute-start.18 = (bf16[32,3584]{1,0:T(8,128)(2,1)S(1)}, bf16[32,3584]{1,0:T(8,128)(2,1)S(1)}, u32[]{:S(2)}, u32[]{:S(2)}) collective-permute-start(bf16[32,3584]{1,0:T(8,128)(2,1)S(1)} %pad_maximum_fusion.3), channel_id=1, source_target_pairs={{0,8},{4,12},{8,0},{12,4},{16,24},{20,28},{24,16},{28,20},{1,9},{5... | collective-permute-start | bytes 688136 | tf_op jit(solution)/shard_map/ppermute | solution.py:645
  167.2 8.5 %collective-permute-start.15 = (bf16[32,3584]{1,0:T(8,128)(2,1)S(1)}, bf16[32,3584]{1,0:T(8,128)(2,1)S(1)}, u32[]{:S(2)}, u32[]{:S(2)}) collective-permute-start(bf16[32,3584]{1,0:T(8,128)(2,1)S(1)} %pad_maximum_fusion.2), channel_id=1, source_target_pairs={{0,4},{4,0},{8,12},{12,8},{16,20},{20,16},{24,28},{28,24},{1,5},{5... | collective-permute-start | bytes 688136 | tf_op jit(solution)/shard_map/ppermute | solution.py:645
  170.6 12.4 %collective-permute-start.19 = (bf16[64,3584]{1,0:T(8,128)(2,1)S(1)}, bf16[64,3584]{1,0:T(8,128)(2,1)S(1)}, u32[]{:S(2)}, u32[]{:S(2)}) collective-permute-start(bf16[64,3584]{1,0:T(8,128)(2,1)S(1)} %pad_maximum_fusion.1), channel_id=1, source_target_pairs={{0,4},{4,0},{8,12},{12,8},{16,20},{20,16},{24,28},{28,24},{1,5},{5... | collective-permute-start | bytes 1376264 | tf_op jit(solution)/shard_map/ppermute | solution.py:645
  175.7 12.3 %collective-permute-start.16 = (bf16[64,3584]{1,0:T(8,128)(2,1)S(1)}, bf16[64,3584]{1,0:T(8,128)(2,1)S(1)}, u32[]{:S(2)}, u32[]{:S(2)}) collective-permute-start(bf16[64,3584]{1,0:T(8,128)(2,1)S(1)} %pad_maximum_fusion), channel_id=1, source_target_pairs={{0,8},{4,12},{8,0},{12,4},{16,24},{20,28},{24,16},{28,20},{1,9},{5... | collective-permute-start | bytes 1376264 | tf_op jit(solution)/shard_map/ppermute | solution.py:645
  197.0 10.1 %collective-permute-start.20 = (bf16[64,3584]{1,0:T(8,128)(2,1)S(1)}, bf16[64,3584]{1,0:T(8,128)(2,1)S(1)}, u32[]{:S(2)}, u32[]{:S(2)}) collective-permute-start(bf16[64,3584]{1,0:T(8,128)(2,1)S(1)} %get-tuple-element.85), channel_id=1, source_target_pairs={{0,4},{4,0},{8,12},{12,8},{16,20},{20,16},{24,28},{28,24},{1,5},{5... | collective-permute-start | bytes 1376264 | tf_op jit(solution)/shard_map/ppermute | solution.py:645
  202.5 12.6 %collective-permute-start.23 = (bf16[64,3584]{1,0:T(8,128)(2,1)S(1)}, bf16[64,3584]{1,0:T(8,128)(2,1)S(1)}, u32[]{:S(2)}, u32[]{:S(2)}) collective-permute-start(bf16[64,3584]{1,0:T(8,128)(2,1)S(1)} %get-tuple-element.92), channel_id=1, source_target_pairs={{0,8},{4,12},{8,0},{12,4},{16,24},{20,28},{24,16},{28,20},{1,9},{5... | collective-permute-start | bytes 1376264 | tf_op jit(solution)/shard_map/ppermute | solution.py:645
  207.3 10.2 %collective-permute-start.21 = (bf16[32,3584]{1,0:T(8,128)(2,1)S(1)}, bf16[32,3584]{1,0:T(8,128)(2,1)S(1)}, u32[]{:S(2)}, u32[]{:S(2)}) collective-permute-start(bf16[32,3584]{1,0:T(8,128)(2,1)S(1)} %get-tuple-element.87), channel_id=1, source_target_pairs={{0,8},{4,12},{8,0},{12,4},{16,24},{20,28},{24,16},{28,20},{1,9},{5... | collective-permute-start | bytes 688136 | tf_op jit(solution)/shard_map/ppermute | solution.py:645
  215.1 6.1 %collective-permute-start.24 = (bf16[32,3584]{1,0:T(8,128)(2,1)S(1)}, bf16[32,3584]{1,0:T(8,128)(2,1)S(1)}, u32[]{:S(2)}, u32[]{:S(2)}) collective-permute-start(bf16[32,3584]{1,0:T(8,128)(2,1)S(1)} %get-tuple-element.94), channel_id=1, source_target_pairs={{0,4},{4,0},{8,12},{12,8},{16,20},{20,16},{24,28},{28,24},{1,5},{5... | collective-permute-start | bytes 688136 | tf_op jit(solution)/shard_map/ppermute | solution.py:645
  217.5 7.5 %collective-permute-start.22 = (bf16[16,3584]{1,0:T(8,128)(2,1)S(1)}, bf16[16,3584]{1,0:T(8,128)(2,1)S(1)}, u32[]{:S(2)}, u32[]{:S(2)}) collective-permute-start(bf16[16,3584]{1,0:T(8,128)(2,1)S(1)} %get-tuple-element.89), channel_id=1, source_target_pairs={{0,16},{4,20},{8,24},{12,28},{16,0},{20,4},{24,8},{28,12},{1,17},{... | collective-permute-start | bytes 344072 | tf_op jit(solution)/shard_map/ppermute | solution.py:645
  221.3 6.7 %collective-permute-start.25 = (bf16[16,3584]{1,0:T(8,128)(2,1)S(1)}, bf16[16,3584]{1,0:T(8,128)(2,1)S(1)}, u32[]{:S(2)}, u32[]{:S(2)}) collective-permute-start(bf16[16,3584]{1,0:T(8,128)(2,1)S(1)} %get-tuple-element.96), channel_id=1, source_target_pairs={{0,16},{4,20},{8,24},{12,28},{16,0},{20,4},{24,8},{28,12},{1,17},{... | collective-permute-start | bytes 344072 | tf_op jit(solution)/shard_map/ppermute | solution.py:645

commit v3 on v2

--- a/solution.py
+++ b/solution.py
@@ -14,7 +14,7 @@
 MASKED = -1e30
 MIB = 1 << 20
 CHUNKS = 2
-SMALL = pl.CostEstimate(flops=1, bytes_accessed=1, transcendentals=0)
+LARGE = pl.CostEstimate(flops=10**11, bytes_accessed=10**8, transcendentals=10**7)
 
 
 def in_hbm(array):
@@ -242,7 +242,7 @@
             pltpu.SemaphoreType.DMA,
         ],
         compiler_params=pltpu.CompilerParams(vmem_limit_bytes=32 * MIB),
-        cost_estimate=SMALL,
+        cost_estimate=LARGE,
         name="attend_resident",
     )(*counts, queries, in_hbm(pool))
 
@@ -287,7 +287,11 @@
             pltpu.VMEM((counts[0].shape[0], tokens), jnp.float32),
         ],
         compiler_params=pltpu.CompilerParams(vmem_limit_bytes=24 * MIB),
-        cost_estimate=SMALL,
+        cost_estimate=pl.CostEstimate(
+            flops=2 * count * tokens * (width + LATENT),
+            bytes_accessed=2 * tokens * width + 8 * count * LATENT,
+            transcendentals=count * tokens,
+        ),
         name="attend_near",
     )(*counts, queries, *packed, *map(in_hbm, state))
 
@@ -355,6 +359,7 @@
         name="latents_far",
         **options,
     )(rank, limit, *counts, queries, *packed, *state)
+    ready = far[0]
     far = [exchange(block, half + u) for u, block in enumerate(far)]
     near = pl.pallas_call(
         latents_near_kernel,
@@ -368,9 +373,9 @@
             out_specs=pl.BlockSpec((count // 2, LATENT), fixed),
         ),
         name="latents_near",
-        **dict(options, cost_estimate=SMALL),
+        **options,
     )(rank, limit, queries, unpacked, bias, *state)
-    return far, near
+    return far, near, ready
 
 
 def slot_counts(content, lengths, slots, page_size):
@@ -411,11 +416,68 @@
     return [functools.partial(load, n) for n in range(len(copies))]
 
 
+def preload_kernel(column, _, weight_ref, out_ref, sems):
+    count = sems.shape[0]
+    width = out_ref.shape[1] // count
+    copies = [
+        pltpu.make_async_copy(
+            weight_ref.at[:, pl.ds(column + n * width, width)],
+            out_ref.at[:, pl.ds(n * width, width)],
+            sems.at[n],
+        )
+        for n in range(count)
+    ]
+    for copy in copies:
+        copy.start()
+    for copy in copies:
+        copy.wait()
+
+
+def preload(weight, column, columns, after, cost, tile=512):
+    shape = (weight.shape[0], columns)
+    return pl.pallas_call(
+        functools.partial(preload_kernel, column),
+        out_shape=pltpu.VMEM(shape, weight.dtype),
+        in_specs=[pl.BlockSpec(memory_space=pl.ANY), pl.BlockSpec(memory_space=pltpu.HBM)],
+        out_specs=pl.BlockSpec(memory_space=pltpu.VMEM),
+        scratch_shapes=[pltpu.SemaphoreType.DMA((columns // tile,))],
+        compiler_params=pltpu.CompilerParams(vmem_limit_bytes=2 * MIB),
+        cost_estimate=cost,
+        name="preload",
+    )(after, in_hbm(weight))
+
+
+def held(weight_ref, tile=512):
+    return [
+        lambda at=at: weight_ref[:, pl.ds(at, tile)] for at in range(0, weight_ref.shape[1], tile)
+    ]
+
+
+def held_kernel(places, rows_ref, weight_ref, keep_ref, send_ref):
+    multiply_tiles(places, held(weight_ref), rows_ref, keep_ref, send_ref)
+
+
+def project_held(rows, weight, places, name):
+    count, depth = rows.shape
+    columns = weight.shape[1]
+    half = jax.ShapeDtypeStruct((count // 2, columns), jnp.bfloat16)
+    return pl.pallas_call(
+        functools.partial(held_kernel, tuple(places)),
+        out_shape=(half, half),
+        compiler_params=pltpu.CompilerParams(vmem_limit_bytes=4 * MIB),
+        cost_estimate=pl.CostEstimate(
+            flops=2 * count * depth * columns,
+            bytes_accessed=2 * count * (columns + depth),
+            transcendentals=0,
+        ),
+        name=name,
+    )(rows, in_vmem(weight))
+
+
 def project_first_kernel(order, rank_ref, near_ref, *refs):
     split = len(order) // 2
     far, refs = refs[:split], refs[split:]
-    value_ref, weight_ref, head_ref, keep_ref, send_ref, tiles_ref, sems = refs
-    tiles = stream(weight_ref, tiles_ref, sems, 0)
+    value_ref, weight_ref, head_ref, keep_ref, send_ref = refs
     heads, width = value_ref.shape[0], value_ref.shape[2]
     own, slots = rank_ref[0] & (split - 1), near_ref.shape[1] // heads
     for h in range(heads):
@@ -427,7 +489,7 @@
         head_ref[:, pl.ds(h * width, width)] = jnp.dot(
             rows, value_ref[h], preferred_element_type=jnp.float32
         ).astype(jnp.bfloat16)
-    multiply_tiles(range(len(order)), tiles, head_ref, keep_ref, send_ref)
+    multiply_tiles(range(len(order)), held(weight_ref), head_ref, keep_ref, send_ref)
 
 
 def project_kernel(column, places, rows_ref, weight_ref, keep_ref, send_ref, tiles_ref, sems):
@@ -449,20 +511,23 @@
     )
 
 
-def project_first(order, rank, near, far, value_up, weight, columns, tile=512):
-    depth = weight.shape[0]
+def project_first(order, rank, near, far, value_up, weight):
+    depth, columns = weight.shape
     rows = len(order) * near.shape[1] // value_up.shape[0]
     half = jax.ShapeDtypeStruct((rows // 2, columns), jnp.bfloat16)
     vmem = pl.BlockSpec(memory_space=pltpu.VMEM)
     return pl.pallas_call(
         functools.partial(project_first_kernel, order),
         out_shape=(jax.ShapeDtypeStruct((rows, depth), jnp.bfloat16), half, half),
-        in_specs=[pl.BlockSpec(memory_space=pltpu.SMEM)]
-        + [vmem] * (2 + len(far))
-        + [pl.BlockSpec(memory_space=pltpu.HBM)],
+        in_specs=[pl.BlockSpec(memory_space=pltpu.SMEM)] + [vmem] * (3 + len(far)),
+        compiler_params=pltpu.CompilerParams(vmem_limit_bytes=6 * MIB),
+        cost_estimate=pl.CostEstimate(
+            flops=2 * rows * depth * columns,
+            bytes_accessed=2 * rows * (columns + depth),
+            transcendentals=0,
+        ),
         name="project_first",
-        **project_options(rows, depth, columns, tile),
-    )(rank, near, *far, value_up, in_hbm(weight))
+    )(rank, near, *far, value_up, in_vmem(weight))
 
 
 def project(rows, weight, columns, chunk, places, name, tile=512):
@@ -528,7 +593,7 @@
 def gather_matmul_kernel(row, first, last, n_pieces, places, mean_over, *refs):
     pieces, refs = refs[:n_pieces], refs[n_pieces:]
     inverse_ref, gate_ref, up_ref, refs = refs[0], refs[1], refs[2], refs[3:]
-    before, refs = ((), refs) if first else (refs[:3], refs[3:])
+    before, refs = ((), refs[1:]) if first else (refs[:3], refs[4:])
     if last:
         hidden_ref, gate_acc, up_acc, squares, *refs = refs
     else:
@@ -577,7 +642,7 @@
 
 
 def gather_matmul(
-    pieces, places, inverse_gain, gate_proj, up_proj, before, chunk, last, tile=512
+    pieces, places, inverse_gain, gate_proj, up_proj, before, chunk, last, after, tile=512
 ):
     columns = pieces[0].shape[1]
     rows = sum(piece.shape[0] for piece in pieces)
@@ -604,21 +669,22 @@
         out_shape=out_shape,
         in_specs=[vmem] * (len(pieces) + 2)
         + [pl.BlockSpec(memory_space=pltpu.HBM)]
-        + [vmem] * len(before or ()),
+        + [vmem] * len(before or ())
+        + [pl.BlockSpec(memory_space=pl.ANY)],
         scratch_shapes=scratch
         + [
             pltpu.VMEM((steps, rows, tile), jnp.bfloat16),
             pltpu.VMEM((steps, tile, units), jnp.bfloat16),
             pltpu.SemaphoreType.DMA((steps,)),
         ],
-        compiler_params=pltpu.CompilerParams(vmem_limit_bytes=16 * MIB),
+        compiler_params=pltpu.CompilerParams(vmem_limit_bytes=12 * MIB),
         cost_estimate=pl.CostEstimate(
             flops=4 * rows * columns * units,
             bytes_accessed=4 * columns * units + 2 * rows * columns,
             transcendentals=0,
         ),
         name="gate_up",
-    )(*pieces, inverse_gain, in_vmem(gate_proj), in_hbm(up_proj), *(before or ()))
+    )(*pieces, inverse_gain, in_vmem(gate_proj), in_hbm(up_proj), *(before or ()), after)
 
 
 class Grid:
@@ -734,7 +800,7 @@
     )
     near_pages = near_pages.reshape((split * capacity,) + near_pages.shape[2:])
     state = attend_near(by_head_queries, [near_pages], counts, slot_count, state, page_size)
-    far_latents, near_latents = latents(
+    far_latents, near_latents, ready = latents(
         by_head_queries,
         far_pages,
         counts,
@@ -751,8 +817,9 @@
     width = residual.shape[1]
     columns = width // CHUNKS
     places = [grid.places(c) for c in range(CHUNKS)]
+    out_first = preload(out_proj, 0, columns, ready, LARGE)
     head_out, *halves = project_first(
-        grid.order(0), rank, near_latents, far_latents, value_up, out_proj, columns
+        grid.order(0), rank, near_latents, far_latents, value_up, out_first
     )
     projected = [halves] + [
         project(head_out, out_proj, columns, c, places[c], "project_out") for c in range(1, CHUNKS)
@@ -764,6 +831,15 @@
         )
         middle.append(row_sum)
         gathered.append(grid.gather(scaled, c))
+    down_first = preload(
+        down_proj,
+        0,
+        columns,
+        gathered[-1][0],
+        pl.CostEstimate(
+            flops=0, bytes_accessed=2 * down_proj.shape[0] * columns, transcendentals=0
+        ),
+    )
     inverse_gain = (1.0 / norm_gain)[None, :]
     sums = None
     for c, pieces in enumerate(gathered):
@@ -777,10 +853,11 @@
             sums,
             c,
             c == CHUNKS - 1,
+            down_first,
         )
     hidden = sums
-    projected = [
-        project(hidden, down_proj, columns, c, places[c], "project_down") for c in range(CHUNKS)
+    projected = [project_held(hidden, down_first, places[0], "project_down")] + [
+        project(hidden, down_proj, columns, c, places[c], "project_down") for c in range(1, CHUNKS)
     ]
     outputs = [
         add_up(middle[c], grid.scatter_sum(keep, send, c)).astype(jnp.bfloat16)

time: 231 us -> 224 us (0.970); the launches traced: 229 us -> 224 us
  starting transfers between devices: 60.2 us -> 52.1 us
  local copies, waits for them, and re-layouts: 6.19 us -> 10.3 us
  waiting for transfers between devices: 77 us -> 73.6 us
    all_to_all x2, starting transfers between devices: 22 us -> 7.21 us  [exchange_near(): lax.all_to_all(array, 'dp', split_axis=0, concat_axis=0, axis_index_group...]
    pallas_call x0 -> x3, Pallas kernels: none -> 8.28 us  [the longest x2 6.92 us: preload(): pl.pallas_call(functools.partial(preload_kernel, column), out_shape=pltpu...]
    ppermute x26, starting transfers between devices: 38.1 us -> 44.9 us  [exchange(): return lax.ppermute(array, 'dp', [(i, i ^ k) for i in range(self.count)])]
    unnamed x29 -> x33, local copies, waits for them, and re-layouts: 3.15 us -> 7.9 us
    pallas_call x3 -> x2, Pallas kernels: 11.6 us -> 7.61 us  [project(): pl.pallas_call(functools.partial(project_kernel, chunk * columns, tuple(p...]
    ppermute x26, waiting for transfers between devices: 77 us -> 73.6 us  [exchange(): return lax.ppermute(array, 'dp', [(i, i ^ k) for i in range(self.count)])]
    pallas_call x1, Pallas kernels: 4.01 us -> 1.39 us  [project_first(): pl.pallas_call(functools.partial(project_first_kernel, order), out_shape=...]
  transfers between devices with their start and end apart: 28 -> 28, of which waited for: 19 -> 20; matrix products, arithmetic and copies ran while one was open for 3% -> 3% of each run, Pallas kernels for 22% -> 28%
where the time goes in v3:
time: 224 us
  Pallas kernels  83.3 us (37%)
  waiting for transfers between devices  73.6 us (33%)
  starting transfers between devices  52.1 us (23%)
  local copies, waits for them, and re-layouts  10.3 us (5%)
  other arithmetic  3.82 us (2%)
    ppermute x26, waiting for transfers between devices, exchange(): return lax.ppermute(array, 'dp', [(i, i ^ k) for i in range(self.count)])  73.6 us
    ppermute x26, starting transfers between devices, exchange(): return lax.ppermute(array, 'dp', [(i, i ^ k) for i in range(self.count)])  44.9 us
    pallas_call x1, Pallas kernels, attend_resident(): pl.pallas_call(functools.partial(resident_kernel, chunk, page_size), out_...  30.6 us
    pallas_call x2, Pallas kernels, gather_matmul(): pl.pallas_call(functools.partial(gather_matmul_kernel, chunk * columns, b...  10.1 us
    pallas_call x2, Pallas kernels, pack_pages(): pl.pallas_call(functools.partial(pack_kernel, tuple(peers), near, capacit...  8.74 us
    unnamed x33, local copies, waits for them, and re-layouts  7.9 us
    pallas_call x2, Pallas kernels, project(): pl.pallas_call(functools.partial(project_kernel, chunk * columns, tuple(p...  7.61 us
    pallas_call x1, Pallas kernels, attend_near(): pl.pallas_call(functools.partial(near_kernel, len(packed), place, page_si...  7.5 us
  transfers between devices with their start and end apart: 28, of which 20 were waited for; matrix products, arithmetic and copies ran while one was open for 3% of the time, Pallas kernels for 28%

profile of v3, /device:TPU:0, one launch (start us, length us, event | category | flops | bytes accessed | tf_op | source)
XLA Modules:
  0.0 224.3 jit_solution(10453074252700194217)
XLA Ops:
  0.0 0.7 copy-done.5
  0.7 0.7 copy-done.7
  1.4 4.4 %pack_far.1 = (bf16[5,288,128]{2,1,0:T(8,128)(2,1)}, bf16[5,288,128]{2,1,0:T(8,128)(2,1)}, bf16[5,288,128]{2,1,0:T(8,128)(2,1)}, bf16[5,288,128]{2,1,0:T(8,128)(2,1)}) custom-call(s32[1,192]{1,0:T(1,128)S(1)} %bitcast.39, s32[192]{0:T(256)S(1)} %copy-done.5, s32[1]{0:T(128)} %bitcast.1.rank_ref._, bf16[112,64,576]{2,1,0:T(8,128)(2,1)} %pool_ref.3, ...), custom_call_target="tpu_custom_call" | custom-call | tf_op jit(solution)/shard_map/pack_far/pallas_call | solution.py:80
  5.8 5.3 %collective-permute-start.1 = (bf16[5,288,128]{2,1,0:T(8,128)(2,1)}, bf16[5,288,128]{2,1,0:T(8,128)(2,1)S(1)}, u32[]{:S(2)}, u32[]{:S(2)}) collective-permute-start(bf16[5,288,128]{2,1,0:T(8,128)(2,1)} %get-tuple-element.52), channel_id=1, source_target_pairs={{0,20},{4,16},{8,28},{12,24},{16,4},{20,0},{24,12},{28,8},{1,21},{... | collective-permute-start | bytes 1105928 | tf_op jit(solution)/shard_map/ppermute | solution.py:711
  11.2 0.6 collective-permute-start.2
  11.8 3.3 %collective-permute-start.3 = (bf16[5,288,128]{2,1,0:T(8,128)(2,1)}, bf16[5,288,128]{2,1,0:T(8,128)(2,1)}, u32[]{:S(2)}, u32[]{:S(2)}) collective-permute-start(bf16[5,288,128]{2,1,0:T(8,128)(2,1)} %get-tuple-element.54), channel_id=1, source_target_pairs={{0,28},{4,24},{8,20},{12,16},{16,12},{20,8},{24,4},{28,0},{1,29},{... | collective-permute-start | bytes 1105928 | tf_op jit(solution)/shard_map/ppermute | solution.py:711
  15.0 4.3 %pack_near.1 = bf16[4,5,288,128]{3,2,1,0:T(8,128)(2,1)} custom-call(s32[1,192]{1,0:T(1,128)S(1)} %bitcast.40, s32[192]{0:T(256)S(1)} %copy-done.5, s32[1]{0:T(128)} %bitcast.1.rank_ref._, bf16[112,64,576]{2,1,0:T(8,128)(2,1)} %pool_ref.3, bf16[5,288,128]{2,1,0:T(8,128)(2,1)} %get-tuple-element.51._), custom_call_target="tpu_custom_call" | custom-call | tf_op jit(solution)/shard_map/pack_near/pallas_call | solution.py:80
  19.4 3.6 %all-to-all-start = ((bf16[4,5,288,128]{3,2,1,0:T(8,128)(2,1)}), bf16[4,5,288,128]{3,2,1,0:T(8,128)(2,1)S(1)}, u32[]{:S(2)}, u32[]{:S(2)}) async-start(bf16[4,5,288,128]{3,2,1,0:T(8,128)(2,1)} %pack_near.1), calls=%async_computation | async-start | bytes 2949120 | tf_op jit(solution)/shard_map/all_to_all | solution.py:716
  23.1 0.5 broadcast.99
  23.6 0.7 reduce.3
  24.8 0.7 compare_reduce_fusion
  25.7 2.1 copy.20
  27.8 0.7 select_n.39
  28.8 30.6 %attend_resident.1 = (f32[1024,128]{1,0:T(8,128)}, f32[1024,512]{1,0:T(8,128)}) custom-call(bf16[16,152]{1,0:T(8,128)(2,1)S(1)} %get-tuple-element.98.whole_ref.refs_0_, bf16[16,152]{1,0:T(8,128)(2,1)S(1)} %get-tuple-element.97.last_ref.refs_1_, s32[16,1]{1,0:T(8,128)S(1)} %copy.23.part_ref.refs_2_, bf16[1024,576]{1,0:T(8,128)(2,1)S(1)} %bitcast.32, ...), custom_call_target="tpu_custom_call" | custom-call | flops 99999997952 | bytes 100000000 | tf_op jit(solution)/shard_map/attend_resident/pallas_call | solution.py:232
  60.1 7.5 %attend_near.1 = (f32[1024,128]{1,0:T(8,128)}, f32[1024,512]{1,0:T(8,128)}) custom-call(bf16[16,152]{1,0:T(8,128)(2,1)S(1)} %get-tuple-element.98.whole_ref.refs_0_, bf16[16,152]{1,0:T(8,128)(2,1)S(1)} %get-tuple-element.97.last_ref.refs_1_, s32[16,1]{1,0:T(8,128)S(1)} %copy.23.part_ref.refs_2_, bf16[1024,576]{1,0:T(8,128)(2,1)S(1)} %bitcast.33, ...), custom_call_target="tpu_custom_call" | custom-call | flops 2852126720 | bytes 5668864 | tf_op jit(solution)/shard_map/attend_near/pallas_call | solution.py:279
  67.6 7.3 %collective-permute-done.refs_4_ = bf16[5,288,128]{2,1,0:T(8,128)(2,1)} collective-permute-done((bf16[5,288,128]{2,1,0:T(8,128)(2,1)}, bf16[5,288,128]{2,1,0:T(8,128)(2,1)}, u32[]{:S(2)}, u32[]{:S(2)}) %collective-permute-start) | collective-permute-done | bytes 368672 | tf_op jit(solution)/shard_map/ppermute | solution.py:711
  74.9 4.0 %latents_far.1 = (bf16[128,512]{1,0:T(8,128)(2,1)S(1)}, bf16[128,512]{1,0:T(8,128)(2,1)S(1)}, bf16[128,512]{1,0:T(8,128)(2,1)S(1)}, bf16[128,512]{1,0:T(8,128)(2...) custom-call(s32[1]{0:T(128)} %bitcast.1.rank_ref._, s32[1]{0:T(128)S(6)} %copy.24.limit_ref, ...), custom_call_target="tpu_custom_call" | custom-call | flops 1426063360 | bytes 2523136 | tf_op jit(solution)/shard_map/latents_far/pallas_call | solution.py:343
  78.9 4.4 %latents_near.1 = bf16[512,512]{1,0:T(8,128)(2,1)} custom-call(s32[1]{0:T(128)} %bitcast.1.rank_ref._, s32[1]{0:T(128)S(6)} %copy.24.limit_ref, bf16[1024,576]{1,0:T(8,128)(2,1)S(1)} %bitcast.35, bf16[1280,576]{1,0:T(8,128)(2,1)S(1)} %get-tuple-element.59.tokens_ref, f32[16,1280]{1,0:T(8,128)S(1)} %get-tuple-element.60.bias_ref, ...), custom_call_target="tpu_custom_call" | custom-call | flops 1426063360 | bytes 2523136 | tf_op jit(solution)/shard_map/latents_near/pallas_call | solution.py:364
  83.3 3.6 %all-to-all-start.1 = ((bf16[4,128,512]{2,1,0:T(8,128)(2,1)}), bf16[4,128,512]{2,1,0:T(8,128)(2,1)S(1)}, u32[]{:S(2)}, u32[]{:S(2)}) async-start(bf16[4,128,512]{2,1,0:T(8,128)(2,1)} %bitcast.42), calls=%async_computation.1 | async-start | bytes 1048576 | tf_op jit(solution)/shard_map/all_to_all | solution.py:716
  87.0 3.3 %collective-permute-start.5 = (bf16[128,512]{1,0:T(8,128)(2,1)S(1)}, bf16[128,512]{1,0:T(8,128)(2,1)S(1)}, u32[]{:S(2)}, u32[]{:S(2)}) collective-permute-start(bf16[128,512]{1,0:T(8,128)(2,1)S(1)} %get-tuple-element.62), channel_id=1, source_target_pairs={{0,20},{4,16},{8,28},{12,24},{16,4},{20,0},{24,12},{28,8},{1,21},{... | collective-permute-start | bytes 393224 | tf_op jit(solution)/shard_map/ppermute | solution.py:711
  90.2 1.8 collective-permute-start.6
  92.0 1.5 collective-permute-start.7
  93.6 3.3 %preload.2.refs_5_ = bf16[1024,3584]{1,0:T(8,128)(2,1)S(1)} custom-call(bf16[128,512]{1,0:T(8,128)(2,1)S(1)} %get-tuple-element.61._, bf16[1024,7168]{1,0:T(8,128)(2,1)} %weight_ref.5), custom_call_target="tpu_custom_call" | custom-call | flops 99999997952 | bytes 100000000 | tf_op jit(solution)/shard_map/preload/pallas_call | solution.py:438
  96.9 2.9 %copy-done = bf16[1024,3584]{1,0:T(8,128)(2,1)} copy-done((bf16[1024,3584]{1,0:T(8,128)(2,1)}, bf16[1024,3584]{1,0:T(8,128)(2,1)S(1)}, u32[]{:S(2)}) %copy-start) | copy-done | bytes 7340056
  99.8 3.7 %collective-permute-done.6.refs_2_ = bf16[128,512]{1,0:T(8,128)(2,1)S(1)} collective-permute-done((bf16[128,512]{1,0:T(8,128)(2,1)S(1)}, bf16[128,512]{1,0:T(8,128)(2,1)S(1)}, u32[]{:S(2)}, u32[]{:S(2)}) %collective-permute-start.6) | collective-permute-done | bytes 131104 | tf_op jit(solution)/shard_map/ppermute | solution.py:711
  103.5 3.6 %collective-permute-done.7.refs_3_ = bf16[128,512]{1,0:T(8,128)(2,1)S(1)} collective-permute-done((bf16[128,512]{1,0:T(8,128)(2,1)S(1)}, bf16[128,512]{1,0:T(8,128)(2,1)S(1)}, u32[]{:S(2)}, u32[]{:S(2)}) %collective-permute-start.7) | collective-permute-done | bytes 131104 | tf_op jit(solution)/shard_map/ppermute | solution.py:711
  107.0 6.7 %collective-permute-done.4.refs_0_ = bf16[128,512]{1,0:T(8,128)(2,1)S(1)} collective-permute-done((bf16[128,512]{1,0:T(8,128)(2,1)S(1)}, bf16[128,512]{1,0:T(8,128)(2,1)S(1)}, u32[]{:S(2)}, u32[]{:S(2)}) %collective-permute-start.4) | collective-permute-done | bytes 131104 | tf_op jit(solution)/shard_map/ppermute | solution.py:711
  113.7 3.1 %copy-done.1 = bf16[1024,3584]{1,0:T(8,128)(2,1)S(1)} copy-done((bf16[1024,3584]{1,0:T(8,128)(2,1)S(1)}, bf16[1024,3584]{1,0:T(8,128)(2,1)}, u32[]{:S(2)}) %copy-start.1) | copy-done | bytes 7340056
  116.8 1.4 project_first.1
  118.7 3.7 %project_out.1 = (bf16[64,3584]{1,0:T(8,128)(2,1)S(1)}, bf16[64,3584]{1,0:T(8,128)(2,1)S(1)}) custom-call(bf16[128,1024]{1,0:T(8,128)(2,1)S(1)} %get-tuple-element.72.rows_ref, bf16[1024,7168]{1,0:T(8,128)(2,1)} %weight_ref.5), custom_call_target="tpu_custom_call" | custom-call | flops 939524096 | bytes 8519680 | tf_op jit(solution)/shard_map/project_out/pallas_call | solution.py:536
  122.5 1.2 collective-permute-start.11
  123.7 6.0 %collective-permute-done.8.came_ref = bf16[64,3584]{1,0:T(8,128)(2,1)S(1)} collective-permute-done((bf16[64,3584]{1,0:T(8,128)(2,1)S(1)}, bf16[64,3584]{1,0:T(8,128)(2,1)S(1)}, u32[]{:S(2)}, u32[]{:S(2)}) %collective-permute-start.8) | collective-permute-done | bytes 458784 | tf_op jit(solution)/shard_map/ppermute | solution.py:711
  129.8 0.5 collective-permute-start.9
  130.3 5.7 %collective-permute-done.11.came_ref = bf16[64,3584]{1,0:T(8,128)(2,1)S(1)} collective-permute-done((bf16[64,3584]{1,0:T(8,128)(2,1)S(1)}, bf16[64,3584]{1,0:T(8,128)(2,1)S(1)}, u32[]{:S(2)}, u32[]{:S(2)}) %collective-permute-start.11) | collective-permute-done | bytes 458784 | tf_op jit(solution)/shard_map/ppermute | solution.py:711
  136.1 1.7 collective-permute-start.12
  137.8 0.8 collective-permute-done.9.came_ref
  138.7 3.4 %collective-permute-start.10 = (bf16[16,3584]{1,0:T(8,128)(2,1)S(1)}, bf16[16,3584]{1,0:T(8,128)(2,1)S(1)}, u32[]{:S(2)}, u32[]{:S(2)}) collective-permute-start(bf16[16,3584]{1,0:T(8,128)(2,1)S(1)} %get-tuple-element.70), channel_id=1, source_target_pairs={{0,16},{4,20},{8,24},{12,28},{16,0},{20,4},{24,8},{28,12},{1,17},{... | collective-permute-start | bytes 344072 | tf_op jit(solution)/shard_map/ppermute | solution.py:711
  142.2 2.6 %collective-permute-start.13 = (bf16[16,3584]{1,0:T(8,128)(2,1)S(1)}, bf16[16,3584]{1,0:T(8,128)(2,1)S(1)}, u32[]{:S(2)}, u32[]{:S(2)}) collective-permute-start(bf16[16,3584]{1,0:T(8,128)(2,1)S(1)} %get-tuple-element.78), channel_id=1, source_target_pairs={{0,16},{4,20},{8,24},{12,28},{16,0},{20,4},{24,8},{28,12},{1,17},{... | collective-permute-start | bytes 344072 | tf_op jit(solution)/shard_map/ppermute | solution.py:711
  144.8 5.2 %collective-permute-done.10.refs_0_ = bf16[16,3584]{1,0:T(8,128)(2,1)S(1)} collective-permute-done((bf16[16,3584]{1,0:T(8,128)(2,1)S(1)}, bf16[16,3584]{1,0:T(8,128)(2,1)S(1)}, u32[]{:S(2)}, u32[]{:S(2)}) %collective-permute-start.10) | collective-permute-done | bytes 114720 | tf_op jit(solution)/shard_map/ppermute | solution.py:711
  150.2 2.3 %collective-permute-done.13.refs_0_ = bf16[16,3584]{1,0:T(8,128)(2,1)S(1)} collective-permute-done((bf16[16,3584]{1,0:T(8,128)(2,1)S(1)}, bf16[16,3584]{1,0:T(8,128)(2,1)S(1)}, u32[]{:S(2)}, u32[]{:S(2)}) %collective-permute-start.13) | collective-permute-done | bytes 114720 | tf_op jit(solution)/shard_map/ppermute | solution.py:711
  152.5 0.7 collective-permute-start.14
  153.2 5.8 %collective-permute-done.17.refs_1_ = bf16[16,3584]{1,0:T(8,128)(2,1)S(1)} collective-permute-done((bf16[16,3584]{1,0:T(8,128)(2,1)S(1)}, bf16[16,3584]{1,0:T(8,128)(2,1)S(1)}, u32[]{:S(2)}, u32[]{:S(2)}) %collective-permute-start.17) | collective-permute-done | bytes 114720 | tf_op jit(solution)/shard_map/ppermute | solution.py:711
  159.0 1.7 collective-permute-start.18
  160.7 0.8 collective-permute-done.14.refs_1_
  161.7 4.2 %collective-permute-done.18.refs_2_ = bf16[32,3584]{1,0:T(8,128)(2,1)S(1)} collective-permute-done((bf16[32,3584]{1,0:T(8,128)(2,1)S(1)}, bf16[32,3584]{1,0:T(8,128)(2,1)S(1)}, u32[]{:S(2)}, u32[]{:S(2)}) %collective-permute-start.18) | collective-permute-done | bytes 229408 | tf_op jit(solution)/shard_map/ppermute | solution.py:711
  166.0 2.4 %collective-permute-done.15.refs_2_ = bf16[32,3584]{1,0:T(8,128)(2,1)S(1)} collective-permute-done((bf16[32,3584]{1,0:T(8,128)(2,1)S(1)}, bf16[32,3584]{1,0:T(8,128)(2,1)S(1)}, u32[]{:S(2)}, u32[]{:S(2)}) %collective-permute-start.15) | collective-permute-done | bytes 229408 | tf_op jit(solution)/shard_map/ppermute | solution.py:711
  168.4 3.1 %collective-permute-start.16 = (bf16[64,3584]{1,0:T(8,128)(2,1)S(1)}, bf16[64,3584]{1,0:T(8,128)(2,1)S(1)}, u32[]{:S(2)}, u32[]{:S(2)}) collective-permute-start(bf16[64,3584]{1,0:T(8,128)(2,1)S(1)} %pad_maximum_fusion), channel_id=1, source_target_pairs={{0,8},{4,12},{8,0},{12,4},{16,24},{20,28},{24,16},{28,20},{1,9},{5... | collective-permute-start | bytes 1376264 | tf_op jit(solution)/shard_map/ppermute | solution.py:711
  171.5 3.6 %preload.3.refs_7_.refs_10_.weight_ref = bf16[1152,3584]{1,0:T(8,128)(2,1)S(1)} custom-call(bf16[16,3584]{1,0:T(8,128)(2,1)S(1)} %get-tuple-element.79._.refs_0_, bf16[1152,7168]{1,0:T(8,128)(2,1)} %weight_ref.7), custom_call_target="tpu_custom_call" | custom-call | bytes 8257536 | tf_op jit(solution)/shard_map/preload/pallas_call | solution.py:438
  175.2 2.4 %collective-permute-done.19.refs_3_ = bf16[64,3584]{1,0:T(8,128)(2,1)S(1)} collective-permute-done((bf16[64,3584]{1,0:T(8,128)(2,1)S(1)}, bf16[64,3584]{1,0:T(8,128)(2,1)S(1)}, u32[]{:S(2)}, u32[]{:S(2)}) %collective-permute-start.19) | collective-permute-done | bytes 458784 | tf_op jit(solution)/shard_map/ppermute | solution.py:711
  177.5 5.1 %gate_up.2 = (f32[128,1152]{1,0:T(8,128)S(1)}, f32[128,1152]{1,0:T(8,128)S(1)}, f32[128,128]{1,0:T(8,128)S(1)}) custom-call(bf16[16,3584]{1,0:T(8,128)(2,1)S(1)} %get-tuple-element.80.refs_0_, bf16[16,3584]{1,0:T(8,128)(2,1)S(1)} %collective-permute-done.17.refs_1_, bf16[32,3584]{1,0:T(8,128)(2,1)S(1)} %collective-permute-done.18.refs_2_, ...), custom_call_target="tpu_custom_call" | custom-call | flops 2113929216 | bytes 17432576 | tf_op jit(solution)/shard_map/gate_up/pallas_call | solution.py:659
  182.6 5.1 %gate_up.3.rows_ref = bf16[128,1152]{1,0:T(8,128)(2,1)S(1)} custom-call(bf16[16,3584]{1,0:T(8,128)(2,1)S(1)} %get-tuple-element.79._.refs_0_, bf16[16,3584]{1,0:T(8,128)(2,1)S(1)} %collective-permute-done.14.refs_1_, bf16[32,3584]{1,0:T(8,128)(2,1)S(1)} %collective-permute-done.15.refs_2_, bf16[64,3584]{1,0:T(8,128)(2,1)S(1)} %collective-permute-done.16.refs_3_, ...), custom_call_target="tpu_custom_call" | custom-call | flops 2113929216 | bytes 17432576 | tf_op jit(solution)/shard_map/gate_up/pallas_call | solution.py:659
  187.7 1.4 project_down.2
  189.2 3.9 %project_down.3 = (bf16[64,3584]{1,0:T(8,128)(2,1)S(1)}, bf16[64,3584]{1,0:T(8,128)(2,1)S(1)}) custom-call(bf16[128,1152]{1,0:T(8,128)(2,1)S(1)} %gate_up.3.rows_ref, bf16[1152,7168]{1,0:T(8,128)(2,1)} %weight_ref.7), custom_call_target="tpu_custom_call" | custom-call | flops 1056964608 | bytes 9469952 | tf_op jit(solution)/shard_map/project_down/pallas_call | solution.py:536
  193.0 2.2 collective-permute-start.23
  195.2 4.5 %collective-permute-done.20.came_ref = bf16[64,3584]{1,0:T(8,128)(2,1)S(1)} collective-permute-done((bf16[64,3584]{1,0:T(8,128)(2,1)S(1)}, bf16[64,3584]{1,0:T(8,128)(2,1)S(1)}, u32[]{:S(2)}, u32[]{:S(2)}) %collective-permute-start.20) | collective-permute-done | bytes 458784 | tf_op jit(solution)/shard_map/ppermute | solution.py:711
  199.8 2.0 collective-permute-start.21
  201.8 4.8 %collective-permute-done.23.came_ref = bf16[64,3584]{1,0:T(8,128)(2,1)S(1)} collective-permute-done((bf16[64,3584]{1,0:T(8,128)(2,1)S(1)}, bf16[64,3584]{1,0:T(8,128)(2,1)S(1)}, u32[]{:S(2)}, u32[]{:S(2)}) %collective-permute-start.23) | collective-permute-done | bytes 458784 | tf_op jit(solution)/shard_map/ppermute | solution.py:711
  206.7 1.5 collective-permute-start.24
  208.2 1.2 collective-permute-done.21.came_ref
  209.4 5.0 %collective-permute-start.22 = (bf16[16,3584]{1,0:T(8,128)(2,1)S(1)}, bf16[16,3584]{1,0:T(8,128)(2,1)S(1)}, u32[]{:S(2)}, u32[]{:S(2)}) collective-permute-start(bf16[16,3584]{1,0:T(8,128)(2,1)S(1)} %get-tuple-element.89), channel_id=1, source_target_pairs={{0,16},{4,20},{8,24},{12,28},{16,0},{20,4},{24,8},{28,12},{1,17},{... | collective-permute-start | bytes 344072 | tf_op jit(solution)/shard_map/ppermute | solution.py:711
  214.4 2.9 %collective-permute-start.25 = (bf16[16,3584]{1,0:T(8,128)(2,1)S(1)}, bf16[16,3584]{1,0:T(8,128)(2,1)S(1)}, u32[]{:S(2)}, u32[]{:S(2)}) collective-permute-start(bf16[16,3584]{1,0:T(8,128)(2,1)S(1)} %get-tuple-element.96), channel_id=1, source_target_pairs={{0,16},{4,20},{8,24},{12,28},{16,0},{20,4},{24,8},{28,12},{1,17},{... | collective-permute-start | bytes 344072 | tf_op jit(solution)/shard_map/ppermute | solution.py:711
  217.3 4.8 %collective-permute-done.22 = bf16[16,3584]{1,0:T(8,128)(2,1)S(1)} collective-permute-done((bf16[16,3584]{1,0:T(8,128)(2,1)S(1)}, bf16[16,3584]{1,0:T(8,128)(2,1)S(1)}, u32[]{:S(2)}, u32[]{:S(2)}) %collective-permute-start.22) | collective-permute-done | bytes 114720 | tf_op jit(solution)/shard_map/ppermute | solution.py:711
  222.2 1.3 collective-permute-done.25
  223.6 0.7 pad_maximum_fusion.4
  (75 shorter events, 3.1 us)
Async XLA Ops:
  0.0 0.7 copy-start.5
  0.7 0.7 copy-start.7
  5.8 17.2 %copy-start.6 = (s32[192]{0:T(256)S(1)}, s32[192]{0:T(256)}, u32[]{:S(2)}) copy-start(s32[192]{0:T(256)} %page_ref.3) | copy-start | bytes 2308
  5.8 17.8 %copy-start.8 = (s32[192,1]{0,1:T(1,128)S(1)}, s32[192,1]{0,1:T(1,128)}, u32[]{:S(2)}) copy-start(s32[192,1]{0,1:T(1,128)} %param.16) | copy-start | bytes 2308
  5.8 18.4 %copy-start.11 = (s32[16]{0:T(128)S(1)}, s32[16]{0:T(128)}, u32[]{:S(2)}) copy-start(s32[16]{0:T(128)} %param.20) | copy-start | bytes 196
  5.8 18.5 %copy-start.10 = (s32[192]{0:T(256)S(1)}, s32[192]{0:T(256)}, u32[]{:S(2)}) copy-start(s32[192]{0:T(256)} %param.18) | copy-start | bytes 2308
  5.8 19.0 %copy-start.9 = (s32[16,32]{1,0:T(8,128)S(1)}, s32[16,32]{1,0:T(8,128)}, u32[]{:S(2)}) copy-start(s32[16,32]{1,0:T(8,128)} %param.21) | copy-start | bytes 6148
  5.8 61.8 %collective-permute-start.1 = (bf16[5,288,128]{2,1,0:T(8,128)(2,1)}, bf16[5,288,128]{2,1,0:T(8,128)(2,1)S(1)}, u32[]{:S(2)}, u32[]{:S(2)}) collective-permute-start(bf16[5,288,128]{2,1,0:T(8,128)(2,1)} %get-tuple-element.52), channel_id=1, source_target_pairs={{0,20},{4,16},{8,28},{12,24},{16,4},{20,0},{24,12},{28,8},{1,21},{... | collective-permute-start | bytes 1105928 | tf_op jit(solution)/shard_map/ppermute | solution.py:711
  11.2 56.5 %collective-permute-start.2 = (bf16[5,288,128]{2,1,0:T(8,128)(2,1)}, bf16[5,288,128]{2,1,0:T(8,128)(2,1)S(1)}, u32[]{:S(2)}, u32[]{:S(2)}) collective-permute-start(bf16[5,288,128]{2,1,0:T(8,128)(2,1)} %get-tuple-element.53), channel_id=1, source_target_pairs={{0,24},{4,28},{8,16},{12,20},{16,8},{20,12},{24,0},{28,4},{1,25},{... | collective-permute-start | bytes 1105928 | tf_op jit(solution)/shard_map/ppermute | solution.py:711
  11.8 55.9 %collective-permute-start.3 = (bf16[5,288,128]{2,1,0:T(8,128)(2,1)}, bf16[5,288,128]{2,1,0:T(8,128)(2,1)}, u32[]{:S(2)}, u32[]{:S(2)}) collective-permute-start(bf16[5,288,128]{2,1,0:T(8,128)(2,1)} %get-tuple-element.54), channel_id=1, source_target_pairs={{0,28},{4,24},{8,20},{12,16},{16,12},{20,8},{24,4},{28,0},{1,29},{... | collective-permute-start | bytes 1105928 | tf_op jit(solution)/shard_map/ppermute | solution.py:711
  15.0 59.9 %collective-permute-start = (bf16[5,288,128]{2,1,0:T(8,128)(2,1)}, bf16[5,288,128]{2,1,0:T(8,128)(2,1)}, u32[]{:S(2)}, u32[]{:S(2)}) collective-permute-start(bf16[5,288,128]{2,1,0:T(8,128)(2,1)} %get-tuple-element.51._), channel_id=1, source_target_pairs={{0,16},{4,20},{8,24},{12,28},{16,0},{20,4},{24,8},{28,12},{1,17},{... | collective-permute-start | bytes 1105928 | tf_op jit(solution)/shard_map/ppermute | solution.py:711
  19.4 40.7 %all-to-all-start = ((bf16[4,5,288,128]{3,2,1,0:T(8,128)(2,1)}), bf16[4,5,288,128]{3,2,1,0:T(8,128)(2,1)S(1)}, u32[]{:S(2)}, u32[]{:S(2)}) async-start(bf16[4,5,288,128]{3,2,1,0:T(8,128)(2,1)} %pack_near.1), calls=%async_computation | async-start | bytes 2949120 | tf_op jit(solution)/shard_map/all_to_all | solution.py:716
  83.3 30.4 %all-to-all-start.1 = ((bf16[4,128,512]{2,1,0:T(8,128)(2,1)}), bf16[4,128,512]{2,1,0:T(8,128)(2,1)S(1)}, u32[]{:S(2)}, u32[]{:S(2)}) async-start(bf16[4,128,512]{2,1,0:T(8,128)(2,1)} %bitcast.42), calls=%async_computation.1 | async-start | bytes 1048576 | tf_op jit(solution)/shard_map/all_to_all | solution.py:716
  87.0 12.8 %collective-permute-start.5 = (bf16[128,512]{1,0:T(8,128)(2,1)S(1)}, bf16[128,512]{1,0:T(8,128)(2,1)S(1)}, u32[]{:S(2)}, u32[]{:S(2)}) collective-permute-start(bf16[128,512]{1,0:T(8,128)(2,1)S(1)} %get-tuple-element.62), channel_id=1, source_target_pairs={{0,20},{4,16},{8,28},{12,24},{16,4},{20,0},{24,12},{28,8},{1,21},{... | collective-permute-start | bytes 393224 | tf_op jit(solution)/shard_map/ppermute | solution.py:711
  90.2 13.2 %collective-permute-start.6 = (bf16[128,512]{1,0:T(8,128)(2,1)S(1)}, bf16[128,512]{1,0:T(8,128)(2,1)S(1)}, u32[]{:S(2)}, u32[]{:S(2)}) collective-permute-start(bf16[128,512]{1,0:T(8,128)(2,1)S(1)} %get-tuple-element.63), channel_id=1, source_target_pairs={{0,24},{4,28},{8,16},{12,20},{16,8},{20,12},{24,0},{28,4},{1,25},{... | collective-permute-start | bytes 393224 | tf_op jit(solution)/shard_map/ppermute | solution.py:711
  92.0 15.0 %collective-permute-start.7 = (bf16[128,512]{1,0:T(8,128)(2,1)S(1)}, bf16[128,512]{1,0:T(8,128)(2,1)S(1)}, u32[]{:S(2)}, u32[]{:S(2)}) collective-permute-start(bf16[128,512]{1,0:T(8,128)(2,1)S(1)} %get-tuple-element.64), channel_id=1, source_target_pairs={{0,28},{4,24},{8,20},{12,16},{16,12},{20,8},{24,4},{28,0},{1,29},{... | collective-permute-start | bytes 393224 | tf_op jit(solution)/shard_map/ppermute | solution.py:711
  93.5 20.2 %copy-start.2 = (bf16[8,512,128]{2,1,0:T(8,128)(2,1)S(1)}, bf16[8,512,128]{2,1,0:T(8,128)(2,1)}, u32[]{:S(2)}) copy-start(bf16[8,512,128]{2,1,0:T(8,128)(2,1)} %refs_4_.1) | copy-start | bytes 3145732
  93.5 20.2 %collective-permute-start.4 = (bf16[128,512]{1,0:T(8,128)(2,1)S(1)}, bf16[128,512]{1,0:T(8,128)(2,1)S(1)}, u32[]{:S(2)}, u32[]{:S(2)}) collective-permute-start(bf16[128,512]{1,0:T(8,128)(2,1)S(1)} %get-tuple-element.61._), channel_id=1, source_target_pairs={{0,16},{4,20},{8,24},{12,28},{16,0},{20,4},{24,8},{28,12},{1,17},{... | collective-permute-start | bytes 393224 | tf_op jit(solution)/shard_map/ppermute | solution.py:711
  96.9 2.9 %copy-start = (bf16[1024,3584]{1,0:T(8,128)(2,1)}, bf16[1024,3584]{1,0:T(8,128)(2,1)S(1)}, u32[]{:S(2)}) copy-start(bf16[1024,3584]{1,0:T(8,128)(2,1)S(1)} %preload.2.refs_5_) | copy-start | bytes 22020100
  113.7 3.1 %copy-start.1 = (bf16[1024,3584]{1,0:T(8,128)(2,1)S(1)}, bf16[1024,3584]{1,0:T(8,128)(2,1)}, u32[]{:S(2)}) copy-start(bf16[1024,3584]{1,0:T(8,128)(2,1)} %copy-done) | copy-start | bytes 22020100
  118.2 11.5 %collective-permute-start.8 = (bf16[64,3584]{1,0:T(8,128)(2,1)S(1)}, bf16[64,3584]{1,0:T(8,128)(2,1)S(1)}, u32[]{:S(2)}, u32[]{:S(2)}) collective-permute-start(bf16[64,3584]{1,0:T(8,128)(2,1)S(1)} %get-tuple-element.66), channel_id=1, source_target_pairs={{0,4},{4,0},{8,12},{12,8},{16,20},{20,16},{24,28},{28,24},{1,5},{5... | collective-permute-start | bytes 1376264 | tf_op jit(solution)/shard_map/ppermute | solution.py:711
  118.7 31.3 %copy-start.3 = (bf16[16,7168]{1,0:T(8,128)(2,1)S(1)}, bf16[16,7168]{1,0:T(8,128)(2,1)}, u32[]{:S(2)}) copy-start(bf16[16,7168]{1,0:T(8,128)(2,1)} %residual_ref.3) | copy-start | bytes 688132
  118.7 31.3 %copy-start.4 = (f32[7168]{0:T(1024)S(1)}, f32[7168]{0:T(1024)}, u32[]{:S(2)}) copy-start(f32[7168]{0:T(1024)} %param.26) | copy-start | bytes 86020
  118.7 58.8 %slice-start = ((s8[16515072]{0:T(1024)(128)(4,1)}), s8[4194304]{0:T(1024)(128)(4,1)S(1)}, s32[]{:S(2)}) async-start(s8[16515072]{0:T(1024)(128)(4,1)} %bitcast.30), calls=%async_computation.2 | async-start | bytes 8388608
  118.7 58.8 %slice-start.1 = ((s8[16515072]{0:T(1024)(128)(4,1)}), s8[4194304]{0:T(1024)(128)(4,1)S(1)}, s32[]{:S(2)}) async-start(s8[16515072]{0:T(1024)(128)(4,1)} %bitcast.30), calls=%async_computation.3 | async-start | bytes 8388608
  122.5 13.5 %collective-permute-start.11 = (bf16[64,3584]{1,0:T(8,128)(2,1)S(1)}, bf16[64,3584]{1,0:T(8,128)(2,1)S(1)}, u32[]{:S(2)}, u32[]{:S(2)}) collective-permute-start(bf16[64,3584]{1,0:T(8,128)(2,1)S(1)} %get-tuple-element.74), channel_id=1, source_target_pairs={{0,8},{4,12},{8,0},{12,4},{16,24},{20,28},{24,16},{28,20},{1,9},{5... | collective-permute-start | bytes 1376264 | tf_op jit(solution)/shard_map/ppermute | solution.py:711
  129.8 8.8 %collective-permute-start.9 = (bf16[32,3584]{1,0:T(8,128)(2,1)S(1)}, bf16[32,3584]{1,0:T(8,128)(2,1)S(1)}, u32[]{:S(2)}, u32[]{:S(2)}) collective-permute-start(bf16[32,3584]{1,0:T(8,128)(2,1)S(1)} %get-tuple-element.68), channel_id=1, source_target_pairs={{0,8},{4,12},{8,0},{12,4},{16,24},{20,28},{24,16},{28,20},{1,9},{5... | collective-permute-start | bytes 688136 | tf_op jit(solution)/shard_map/ppermute | solution.py:711
  136.1 6.1 %collective-permute-start.12 = (bf16[32,3584]{1,0:T(8,128)(2,1)S(1)}, bf16[32,3584]{1,0:T(8,128)(2,1)S(1)}, u32[]{:S(2)}, u32[]{:S(2)}) collective-permute-start(bf16[32,3584]{1,0:T(8,128)(2,1)S(1)} %get-tuple-element.76), channel_id=1, source_target_pairs={{0,4},{4,0},{8,12},{12,8},{16,20},{20,16},{24,28},{28,24},{1,5},{5... | collective-permute-start | bytes 688136 | tf_op jit(solution)/shard_map/ppermute | solution.py:711
  138.7 11.4 %collective-permute-start.10 = (bf16[16,3584]{1,0:T(8,128)(2,1)S(1)}, bf16[16,3584]{1,0:T(8,128)(2,1)S(1)}, u32[]{:S(2)}, u32[]{:S(2)}) collective-permute-start(bf16[16,3584]{1,0:T(8,128)(2,1)S(1)} %get-tuple-element.70), channel_id=1, source_target_pairs={{0,16},{4,20},{8,24},{12,28},{16,0},{20,4},{24,8},{28,12},{1,17},{... | collective-permute-start | bytes 344072 | tf_op jit(solution)/shard_map/ppermute | solution.py:711
  142.2 10.2 %collective-permute-start.13 = (bf16[16,3584]{1,0:T(8,128)(2,1)S(1)}, bf16[16,3584]{1,0:T(8,128)(2,1)S(1)}, u32[]{:S(2)}, u32[]{:S(2)}) collective-permute-start(bf16[16,3584]{1,0:T(8,128)(2,1)S(1)} %get-tuple-element.78), channel_id=1, source_target_pairs={{0,16},{4,20},{8,24},{12,28},{16,0},{20,4},{24,8},{28,12},{1,17},{... | collective-permute-start | bytes 344072 | tf_op jit(solution)/shard_map/ppermute | solution.py:711
  150.1 8.9 %collective-permute-start.17 = (bf16[16,3584]{1,0:T(8,128)(2,1)S(1)}, bf16[16,3584]{1,0:T(8,128)(2,1)S(1)}, u32[]{:S(2)}, u32[]{:S(2)}) collective-permute-start(bf16[16,3584]{1,0:T(8,128)(2,1)S(1)} %get-tuple-element.80.refs_0_), channel_id=1, source_target_pairs={{0,16},{4,20},{8,24},{12,28},{16,0},{20,4},{24,8},{28,12},{1,17},{... | collective-permute-start | bytes 344072 | tf_op jit(solution)/shard_map/ppermute | solution.py:711
  152.5 9.1 %collective-permute-start.14 = (bf16[16,3584]{1,0:T(8,128)(2,1)S(1)}, bf16[16,3584]{1,0:T(8,128)(2,1)S(1)}, u32[]{:S(2)}, u32[]{:S(2)}) collective-permute-start(bf16[16,3584]{1,0:T(8,128)(2,1)S(1)} %get-tuple-element.79._.refs_0_), channel_id=1, source_target_pairs={{0,16},{4,20},{8,24},{12,28},{16,0},{20,4},{24,8},{28,12},{1,17},{... | collective-permute-start | bytes 344072 | tf_op jit(solution)/shard_map/ppermute | solution.py:711
  159.0 6.9 %collective-permute-start.18 = (bf16[32,3584]{1,0:T(8,128)(2,1)S(1)}, bf16[32,3584]{1,0:T(8,128)(2,1)S(1)}, u32[]{:S(2)}, u32[]{:S(2)}) collective-permute-start(bf16[32,3584]{1,0:T(8,128)(2,1)S(1)} %pad_maximum_fusion.3), channel_id=1, source_target_pairs={{0,8},{4,12},{8,0},{12,4},{16,24},{20,28},{24,16},{28,20},{1,9},{5... | collective-permute-start | bytes 688136 | tf_op jit(solution)/shard_map/ppermute | solution.py:711
  161.6 6.8 %collective-permute-start.15 = (bf16[32,3584]{1,0:T(8,128)(2,1)S(1)}, bf16[32,3584]{1,0:T(8,128)(2,1)S(1)}, u32[]{:S(2)}, u32[]{:S(2)}) collective-permute-start(bf16[32,3584]{1,0:T(8,128)(2,1)S(1)} %pad_maximum_fusion.2), channel_id=1, source_target_pairs={{0,4},{4,0},{8,12},{12,8},{16,20},{20,16},{24,28},{28,24},{1,5},{5... | collective-permute-start | bytes 688136 | tf_op jit(solution)/shard_map/ppermute | solution.py:711
  165.9 11.6 %collective-permute-start.19 = (bf16[64,3584]{1,0:T(8,128)(2,1)S(1)}, bf16[64,3584]{1,0:T(8,128)(2,1)S(1)}, u32[]{:S(2)}, u32[]{:S(2)}) collective-permute-start(bf16[64,3584]{1,0:T(8,128)(2,1)S(1)} %pad_maximum_fusion.1), channel_id=1, source_target_pairs={{0,4},{4,0},{8,12},{12,8},{16,20},{20,16},{24,28},{28,24},{1,5},{5... | collective-permute-start | bytes 1376264 | tf_op jit(solution)/shard_map/ppermute | solution.py:711
  168.4 14.2 %collective-permute-start.16 = (bf16[64,3584]{1,0:T(8,128)(2,1)S(1)}, bf16[64,3584]{1,0:T(8,128)(2,1)S(1)}, u32[]{:S(2)}, u32[]{:S(2)}) collective-permute-start(bf16[64,3584]{1,0:T(8,128)(2,1)S(1)} %pad_maximum_fusion), channel_id=1, source_target_pairs={{0,8},{4,12},{8,0},{12,4},{16,24},{20,28},{24,16},{28,20},{1,9},{5... | collective-permute-start | bytes 1376264 | tf_op jit(solution)/shard_map/ppermute | solution.py:711
  171.5 6.0 %slice-start.2 = ((s8[16515072]{0:T(1024)(128)(4,1)}), s8[4194304]{0:T(1024)(128)(4,1)S(1)}, s32[]{:S(2)}) async-start(s8[16515072]{0:T(1024)(128)(4,1)} %bitcast.30), calls=%async_computation.4 | async-start | bytes 8388608
  171.5 6.0 %slice-start.3 = ((s8[16515072]{0:T(1024)(128)(4,1)}), s8[3932160]{0:T(1024)(128)(4,1)S(1)}, s32[]{:S(2)}) async-start(s8[16515072]{0:T(1024)(128)(4,1)} %bitcast.30), calls=%async_computation.5 | async-start | bytes 7864320
  189.1 10.7 %collective-permute-start.20 = (bf16[64,3584]{1,0:T(8,128)(2,1)S(1)}, bf16[64,3584]{1,0:T(8,128)(2,1)S(1)}, u32[]{:S(2)}, u32[]{:S(2)}) collective-permute-start(bf16[64,3584]{1,0:T(8,128)(2,1)S(1)} %get-tuple-element.85), channel_id=1, source_target_pairs={{0,4},{4,0},{8,12},{12,8},{16,20},{20,16},{24,28},{28,24},{1,5},{5... | collective-permute-start | bytes 1376264 | tf_op jit(solution)/shard_map/ppermute | solution.py:711
  193.0 13.6 %collective-permute-start.23 = (bf16[64,3584]{1,0:T(8,128)(2,1)S(1)}, bf16[64,3584]{1,0:T(8,128)(2,1)S(1)}, u32[]{:S(2)}, u32[]{:S(2)}) collective-permute-start(bf16[64,3584]{1,0:T(8,128)(2,1)S(1)} %get-tuple-element.92), channel_id=1, source_target_pairs={{0,8},{4,12},{8,0},{12,4},{16,24},{20,28},{24,16},{28,20},{1,9},{5... | collective-permute-start | bytes 1376264 | tf_op jit(solution)/shard_map/ppermute | solution.py:711
  199.8 9.5 %collective-permute-start.21 = (bf16[32,3584]{1,0:T(8,128)(2,1)S(1)}, bf16[32,3584]{1,0:T(8,128)(2,1)S(1)}, u32[]{:S(2)}, u32[]{:S(2)}) collective-permute-start(bf16[32,3584]{1,0:T(8,128)(2,1)S(1)} %get-tuple-element.87), channel_id=1, source_target_pairs={{0,8},{4,12},{8,0},{12,4},{16,24},{20,28},{24,16},{28,20},{1,9},{5... | collective-permute-start | bytes 688136 | tf_op jit(solution)/shard_map/ppermute | solution.py:711
  206.7 7.6 %collective-permute-start.24 = (bf16[32,3584]{1,0:T(8,128)(2,1)S(1)}, bf16[32,3584]{1,0:T(8,128)(2,1)S(1)}, u32[]{:S(2)}, u32[]{:S(2)}) collective-permute-start(bf16[32,3584]{1,0:T(8,128)(2,1)S(1)} %get-tuple-element.94), channel_id=1, source_target_pairs={{0,4},{4,0},{8,12},{12,8},{16,20},{20,16},{24,28},{28,24},{1,5},{5... | collective-permute-start | bytes 688136 | tf_op jit(solution)/shard_map/ppermute | solution.py:711
  209.4 12.7 %collective-permute-start.22 = (bf16[16,3584]{1,0:T(8,128)(2,1)S(1)}, bf16[16,3584]{1,0:T(8,128)(2,1)S(1)}, u32[]{:S(2)}, u32[]{:S(2)}) collective-permute-start(bf16[16,3584]{1,0:T(8,128)(2,1)S(1)} %get-tuple-element.89), channel_id=1, source_target_pairs={{0,16},{4,20},{8,24},{12,28},{16,0},{20,4},{24,8},{28,12},{1,17},{... | collective-permute-start | bytes 344072 | tf_op jit(solution)/shard_map/ppermute | solution.py:711
  214.4 9.1 %collective-permute-start.25 = (bf16[16,3584]{1,0:T(8,128)(2,1)S(1)}, bf16[16,3584]{1,0:T(8,128)(2,1)S(1)}, u32[]{:S(2)}, u32[]{:S(2)}) collective-permute-start(bf16[16,3584]{1,0:T(8,128)(2,1)S(1)} %get-tuple-element.96), channel_id=1, source_target_pairs={{0,16},{4,20},{8,24},{12,28},{16,0},{20,4},{24,8},{28,12},{1,17},{... | collective-permute-start | bytes 344072 | tf_op jit(solution)/shard_map/ppermute | solution.py:711

commit v4 on v3

--- a/solution.py
+++ b/solution.py
@@ -474,22 +474,70 @@
     )(rows, in_vmem(weight))
 
 
-def project_first_kernel(order, rank_ref, near_ref, *refs):
+def head_values(parts, value_ref, slots, out):
+    heads = value_ref.shape[0] // LATENT
+    for h in range(heads):
+        rows = jnp.concatenate([part(pl.ds(h * slots, slots)) for part in parts], axis=0)
+        values = value_ref[pl.ds(h * LATENT, LATENT), :]
+        out(h, jnp.dot(rows, values, preferred_element_type=jnp.float32).astype(jnp.bfloat16))
+
+
+def value_near_kernel(rank_ref, near_ref, value_ref, out_ref):
+    split, width = near_ref.shape[0], value_ref.shape[1]
+    own, slots = rank_ref[0] & (split - 1), near_ref.shape[1] * LATENT // value_ref.shape[0]
+    parts = [lambda span, k=k: near_ref[own ^ k, span, :] for k in range(split)]
+
+    def out(h, rows):
+        out_ref[:, pl.ds(h * width, width)] = rows
+
+    head_values(parts, value_ref, slots, out)
+
+
+def value_near(rank, near, values):
+    heads = values.shape[0] // LATENT
+    shape = (near.shape[0] * near.shape[1] // heads, heads * values.shape[1])
+    vmem = pl.BlockSpec(memory_space=pltpu.VMEM)
+    return pl.pallas_call(
+        value_near_kernel,
+        out_shape=jax.ShapeDtypeStruct(shape, jnp.bfloat16),
+        in_specs=[pl.BlockSpec(memory_space=pltpu.SMEM), vmem, vmem],
+        compiler_params=pltpu.CompilerParams(vmem_limit_bytes=4 * MIB),
+        name="value_near",
+    )(rank, near, values)
+
+
+def project_first_kernel(order, near_ref, *refs):
     split = len(order) // 2
     far, refs = refs[:split], refs[split:]
-    value_ref, weight_ref, head_ref, keep_ref, send_ref = refs
-    heads, width = value_ref.shape[0], value_ref.shape[2]
-    own, slots = rank_ref[0] & (split - 1), near_ref.shape[1] // heads
-    for h in range(heads):
-        span = pl.ds(h * slots, slots)
-        rows = jnp.concatenate(
-            [near_ref[own ^ k, span, :] if k < split else far[k - split][span, :] for k in order],
-            axis=0,
-        )
-        head_ref[:, pl.ds(h * width, width)] = jnp.dot(
-            rows, value_ref[h], preferred_element_type=jnp.float32
-        ).astype(jnp.bfloat16)
-    multiply_tiles(range(len(order)), held(weight_ref), head_ref, keep_ref, send_ref)
+    value_ref, weight_ref, head_ref, keep_ref, send_ref, tiles_ref, sems = refs
+    tiles = stream(weight_ref, tiles_ref, sems, 0)
+    slots, width = near_ref.shape[0] // split, value_ref.shape[1]
+    place = {k: pl.ds(n * slots, slots) for n, k in enumerate(order)}
+    for k in range(split):
+        head_ref[place[k], :] = near_ref[pl.ds(k * slots, slots), :]
+
+    def out(h, rows):
+        for k in range(split):
+            head_ref[place[split + k], pl.ds(h * width, width)] = rows[
+                k * slots : (k + 1) * slots
+            ]
+
+    parts = [lambda span, ref=ref: ref[span, :] for ref in far]
+    head_values(parts, value_ref, slots, out)
+    multiply_tiles(range(len(order)), tiles, head_ref, keep_ref, send_ref)
+
+
+def project_first(order, near, far, values, weight, columns, tile=512):
+    depth, rows = weight.shape[0], 2 * near.shape[0]
+    half = jax.ShapeDtypeStruct((rows // 2, columns), jnp.bfloat16)
+    vmem = pl.BlockSpec(memory_space=pltpu.VMEM)
+    return pl.pallas_call(
+        functools.partial(project_first_kernel, order),
+        out_shape=(jax.ShapeDtypeStruct((rows, depth), jnp.bfloat16), half, half),
+        in_specs=[vmem] * (2 + len(far)) + [pl.BlockSpec(memory_space=pltpu.HBM)],
+        name="project_first",
+        **project_options(rows, depth, columns, tile),
+    )(near, *far, values, in_hbm(weight))
 
 
 def project_kernel(column, places, rows_ref, weight_ref, keep_ref, send_ref, tiles_ref, sems):
@@ -509,25 +557,6 @@
             transcendentals=0,
         ),
     )
-
-
-def project_first(order, rank, near, far, value_up, weight):
-    depth, columns = weight.shape
-    rows = len(order) * near.shape[1] // value_up.shape[0]
-    half = jax.ShapeDtypeStruct((rows // 2, columns), jnp.bfloat16)
-    vmem = pl.BlockSpec(memory_space=pltpu.VMEM)
-    return pl.pallas_call(
-        functools.partial(project_first_kernel, order),
-        out_shape=(jax.ShapeDtypeStruct((rows, depth), jnp.bfloat16), half, half),
-        in_specs=[pl.BlockSpec(memory_space=pltpu.SMEM)] + [vmem] * (3 + len(far)),
-        compiler_params=pltpu.CompilerParams(vmem_limit_bytes=6 * MIB),
-        cost_estimate=pl.CostEstimate(
-            flops=2 * rows * depth * columns,
-            bytes_accessed=2 * rows * (columns + depth),
-            transcendentals=0,
-        ),
-        name="project_first",
-    )(rank, near, *far, value_up, in_vmem(weight))
 
 
 def project(rows, weight, columns, chunk, places, name, tile=512):
@@ -817,9 +846,11 @@
     width = residual.shape[1]
     columns = width // CHUNKS
     places = [grid.places(c) for c in range(CHUNKS)]
-    out_first = preload(out_proj, 0, columns, ready, LARGE)
+    values = value_up.reshape(-1, value_up.shape[2])
+    values = preload(values, 0, values.shape[1], ready, LARGE, values.shape[1])
+    near_heads = value_near(rank, near_latents, values)
     head_out, *halves = project_first(
-        grid.order(0), rank, near_latents, far_latents, value_up, out_first
+        grid.order(0), near_heads, far_latents, values, out_proj, columns
     )
     projected = [halves] + [
         project(head_out, out_proj, columns, c, places[c], "project_out") for c in range(1, CHUNKS)

time: 224 us -> 219 us (0.978)
  local copies, waits for them, and re-layouts: 10.3 us -> 4.96 us
    ppermute x26, waiting for transfers between devices: 73.6 us -> 64.5 us  [exchange(): return lax.ppermute(array, 'dp', [(i, i ^ k) for i in range(self.count)])]
    all_to_all x2, waiting for transfers between devices: 0.01 us -> 7.01 us  [exchange_near(): lax.all_to_all(array, 'dp', split_axis=0, concat_axis=0, axis_index_group...]
    unnamed x33 -> x27, local copies, waits for them, and re-layouts: 7.9 us -> 1.94 us
    pallas_call x1, Pallas kernels: 1.39 us -> 3.75 us  [project_first(): pl.pallas_call(functools.partial(project_first_kernel, order), out_shape=...]
  transfers between devices with their start and end apart: 28 -> 28, of which waited for: 20 -> 19; matrix products, arithmetic and copies ran while one was open for 3% -> 3% of each run, Pallas kernels for 28% -> 28%
where the time goes in v4:
time: 219 us; the launch traced here: 218 us
  Pallas kernels  84.7 us (39%)
  waiting for transfers between devices  71.5 us (33%)
  starting transfers between devices  51.5 us (24%)
  local copies, waits for them, and re-layouts  4.96 us (2%)
  other arithmetic  4.35 us (2%)
    ppermute x26, waiting for transfers between devices, exchange(): return lax.ppermute(array, 'dp', [(i, i ^ k) for i in range(self.count)])  64.5 us
    ppermute x26, starting transfers between devices, exchange(): return lax.ppermute(array, 'dp', [(i, i ^ k) for i in range(self.count)])  43.6 us
    pallas_call x1, Pallas kernels, attend_resident(): pl.pallas_call(functools.partial(resident_kernel, chunk, page_size), out_...  30.6 us
    pallas_call x2, Pallas kernels, gather_matmul(): pl.pallas_call(functools.partial(gather_matmul_kernel, chunk * columns, b...  10.1 us
    pallas_call x2, Pallas kernels, pack_pages(): pl.pallas_call(functools.partial(pack_kernel, tuple(peers), near, capacit...  9.51 us
    all_to_all x2, starting transfers between devices, exchange_near(): lax.all_to_all(array, 'dp', split_axis=0, concat_axis=0, axis_index_group...  7.91 us
    pallas_call x2, Pallas kernels, project(): pl.pallas_call(functools.partial(project_kernel, chunk * columns, tuple(p...  7.58 us
    pallas_call x1, Pallas kernels, attend_near(): pl.pallas_call(functools.partial(near_kernel, len(packed), place, page_si...  7.53 us
  transfers between devices with their start and end apart: 28, of which 19 were waited for; matrix products, arithmetic and copies ran while one was open for 3% of the time, Pallas kernels for 28%

profile of v4, /device:TPU:0, one launch (start us, length us, event | category | flops | bytes accessed | tf_op | source)
XLA Modules:
  0.0 218.1 jit_solution(9857704437520643971)
XLA Ops:
  0.0 0.7 copy-done.2
  0.7 0.7 copy-done.4
  1.4 4.7 %pack_far.1 = (bf16[5,288,128]{2,1,0:T(8,128)(2,1)}, bf16[5,288,128]{2,1,0:T(8,128)(2,1)}, bf16[5,288,128]{2,1,0:T(8,128)(2,1)}, bf16[5,288,128]{2,1,0:T(8,128)(2,1)}) custom-call(s32[1,192]{1,0:T(1,128)S(1)} %bitcast.40, s32[192]{0:T(256)S(1)} %copy-done.2, s32[1]{0:T(128)} %bitcast.1.rank_ref._, bf16[112,64,576]{2,1,0:T(8,128)(2,1)} %pool_ref.3, ...), custom_call_target="tpu_custom_call" | custom-call | tf_op jit(solution)/shard_map/pack_far/pallas_call | solution.py:80
  6.1 3.4 %collective-permute-start = (bf16[5,288,128]{2,1,0:T(8,128)(2,1)}, bf16[5,288,128]{2,1,0:T(8,128)(2,1)S(1)}, u32[]{:S(2)}, u32[]{:S(2)}) collective-permute-start(bf16[5,288,128]{2,1,0:T(8,128)(2,1)} %get-tuple-element.51._), channel_id=1, source_target_pairs={{0,16},{4,20},{8,24},{12,28},{16,0},{20,4},{24,8},{28,12},{1,17},{... | collective-permute-start | bytes 1105928 | tf_op jit(solution)/shard_map/ppermute | solution.py:740
  9.5 4.8 %pack_near.1 = bf16[4,5,288,128]{3,2,1,0:T(8,128)(2,1)} custom-call(s32[1,192]{1,0:T(1,128)S(1)} %bitcast.41, s32[192]{0:T(256)S(1)} %copy-done.2, s32[1]{0:T(128)} %bitcast.1.rank_ref._, bf16[112,64,576]{2,1,0:T(8,128)(2,1)} %pool_ref.3, bf16[5,288,128]{2,1,0:T(8,128)(2,1)} %get-tuple-element.51._), custom_call_target="tpu_custom_call" | custom-call | tf_op jit(solution)/shard_map/pack_near/pallas_call | solution.py:80
  14.3 4.3 %all-to-all-start = ((bf16[4,5,288,128]{3,2,1,0:T(8,128)(2,1)}), bf16[4,5,288,128]{3,2,1,0:T(8,128)(2,1)S(1)}, u32[]{:S(2)}, u32[]{:S(2)}) async-start(bf16[4,5,288,128]{3,2,1,0:T(8,128)(2,1)} %pack_near.1), calls=%async_computation | async-start | bytes 2949120 | tf_op jit(solution)/shard_map/all_to_all | solution.py:745
  18.6 1.9 collective-permute-start.1
  20.5 3.4 %collective-permute-start.2 = (bf16[5,288,128]{2,1,0:T(8,128)(2,1)}, bf16[5,288,128]{2,1,0:T(8,128)(2,1)}, u32[]{:S(2)}, u32[]{:S(2)}) collective-permute-start(bf16[5,288,128]{2,1,0:T(8,128)(2,1)} %get-tuple-element.53), channel_id=1, source_target_pairs={{0,24},{4,28},{8,16},{12,20},{16,8},{20,12},{24,0},{28,4},{1,25},{... | collective-permute-start | bytes 1105928 | tf_op jit(solution)/shard_map/ppermute | solution.py:740
  24.0 0.5 broadcast.99
  24.5 0.7 reduce.3
  25.3 0.3 convert_reduce_fusion.2
  25.7 0.7 compare_reduce_fusion
  26.5 0.5 fusion.8
  27.1 2.1 copy.20
  29.2 0.7 copy.23.part_ref.refs_2_
  29.9 0.7 select_n.39
  30.6 0.4 convert_reduce_fusion
  30.9 30.6 %attend_resident.1 = (f32[1024,128]{1,0:T(8,128)}, f32[1024,512]{1,0:T(8,128)}) custom-call(bf16[16,152]{1,0:T(8,128)(2,1)S(1)} %get-tuple-element.98.whole_ref.refs_0_, bf16[16,152]{1,0:T(8,128)(2,1)S(1)} %get-tuple-element.97.last_ref.refs_1_, s32[16,1]{1,0:T(8,128)S(1)} %copy.23.part_ref.refs_2_, bf16[1024,576]{1,0:T(8,128)(2,1)S(1)} %bitcast.33, ...), custom_call_target="tpu_custom_call" | custom-call | flops 99999997952 | bytes 100000000 | tf_op jit(solution)/shard_map/attend_resident/pallas_call | solution.py:232
  62.2 3.8 %all-to-all-done = bf16[4,5,288,128]{3,2,1,0:T(8,128)(2,1)S(1)} async-done(((bf16[4,5,288,128]{3,2,1,0:T(8,128)(2,1)}), bf16[4,5,288,128]{3,2,1,0:T(8,128)(2,1)S(1)}, u32[]{:S(2)}, u32[]{:S(2)}) %all-to-all-start) | async-done | bytes 1474592 | tf_op jit(solution)/shard_map/all_to_all | solution.py:745
  66.0 7.5 %attend_near.1 = (f32[1024,128]{1,0:T(8,128)}, f32[1024,512]{1,0:T(8,128)}) custom-call(bf16[16,152]{1,0:T(8,128)(2,1)S(1)} %get-tuple-element.98.whole_ref.refs_0_, bf16[16,152]{1,0:T(8,128)(2,1)S(1)} %get-tuple-element.97.last_ref.refs_1_, s32[16,1]{1,0:T(8,128)S(1)} %copy.23.part_ref.refs_2_, bf16[1024,576]{1,0:T(8,128)(2,1)S(1)} %bitcast.34, ...), custom_call_target="tpu_custom_call" | custom-call | flops 2852126720 | bytes 5668864 | tf_op jit(solution)/shard_map/attend_near/pallas_call | solution.py:279
  73.6 4.0 %latents_far.1 = (bf16[128,512]{1,0:T(8,128)(2,1)S(1)}, bf16[128,512]{1,0:T(8,128)(2,1)S(1)}, bf16[128,512]{1,0:T(8,128)(2,1)S(1)}, bf16[128,512]{1,0:T(8,128)(2...) custom-call(s32[1]{0:T(128)} %bitcast.1.rank_ref._, s32[1]{0:T(128)S(6)} %copy.24.limit_ref, ...), custom_call_target="tpu_custom_call" | custom-call | flops 1426063360 | bytes 2523136 | tf_op jit(solution)/shard_map/latents_far/pallas_call | solution.py:343
  77.6 4.4 %latents_near.1 = bf16[512,512]{1,0:T(8,128)(2,1)} custom-call(s32[1]{0:T(128)} %bitcast.1.rank_ref._, s32[1]{0:T(128)S(6)} %copy.24.limit_ref, bf16[1024,576]{1,0:T(8,128)(2,1)S(1)} %bitcast.36, bf16[1280,576]{1,0:T(8,128)(2,1)S(1)} %get-tuple-element.59.tokens_ref, f32[16,1280]{1,0:T(8,128)S(1)} %get-tuple-element.60.bias_ref, ...), custom_call_target="tpu_custom_call" | custom-call | flops 1426063360 | bytes 2523136 | tf_op jit(solution)/shard_map/latents_near/pallas_call | solution.py:364
  82.0 3.6 %all-to-all-start.1 = ((bf16[4,128,512]{2,1,0:T(8,128)(2,1)}), bf16[4,128,512]{2,1,0:T(8,128)(2,1)S(1)}, u32[]{:S(2)}, u32[]{:S(2)}) async-start(bf16[4,128,512]{2,1,0:T(8,128)(2,1)} %bitcast.43), calls=%async_computation.1 | async-start | bytes 1048576 | tf_op jit(solution)/shard_map/all_to_all | solution.py:745
  85.6 4.0 %collective-permute-start.4 = (bf16[128,512]{1,0:T(8,128)(2,1)S(1)}, bf16[128,512]{1,0:T(8,128)(2,1)S(1)}, u32[]{:S(2)}, u32[]{:S(2)}) collective-permute-start(bf16[128,512]{1,0:T(8,128)(2,1)S(1)} %get-tuple-element.61._), channel_id=1, source_target_pairs={{0,16},{4,20},{8,24},{12,28},{16,0},{20,4},{24,8},{28,12},{1,17},{... | collective-permute-start | bytes 393224 | tf_op jit(solution)/shard_map/ppermute | solution.py:740
  89.6 1.2 collective-permute-start.5
  90.8 3.8 %collective-permute-start.6 = (bf16[128,512]{1,0:T(8,128)(2,1)S(1)}, bf16[128,512]{1,0:T(8,128)(2,1)S(1)}, u32[]{:S(2)}, u32[]{:S(2)}) collective-permute-start(bf16[128,512]{1,0:T(8,128)(2,1)S(1)} %get-tuple-element.63), channel_id=1, source_target_pairs={{0,24},{4,28},{8,16},{12,20},{16,8},{20,12},{24,0},{28,4},{1,25},{... | collective-permute-start | bytes 393224 | tf_op jit(solution)/shard_map/ppermute | solution.py:740
  94.6 1.2 preload.2.value_ref.refs_4_
  95.9 3.2 %all-to-all-done.1.near_ref = bf16[4,128,512]{2,1,0:T(8,128)(2,1)S(1)} async-done(((bf16[4,128,512]{2,1,0:T(8,128)(2,1)}), bf16[4,128,512]{2,1,0:T(8,128)(2,1)S(1)}, u32[]{:S(2)}, u32[]{:S(2)}) %all-to-all-start.1) | async-done | bytes 524320 | tf_op jit(solution)/shard_map/all_to_all | solution.py:745
  99.0 0.3 value_near.1.near_ref
  99.4 9.7 %collective-permute-done.5.refs_1_ = bf16[128,512]{1,0:T(8,128)(2,1)S(1)} collective-permute-done((bf16[128,512]{1,0:T(8,128)(2,1)S(1)}, bf16[128,512]{1,0:T(8,128)(2,1)S(1)}, u32[]{:S(2)}, u32[]{:S(2)}) %collective-permute-start.5) | collective-permute-done | bytes 131104 | tf_op jit(solution)/shard_map/ppermute | solution.py:740
  109.1 3.7 %project_first.1 = (bf16[128,1024]{1,0:T(8,128)(2,1)S(1)}, bf16[64,3584]{1,0:T(8,128)(2,1)S(1)}, bf16[64,3584]{1,0:T(8,128)(2,1)S(1)}) custom-call(bf16[64,1024]{1,0:T(8,128)(2,1)S(1)} %value_near.1.near_ref, bf16[128,512]{1,0:T(8,128)(2,1)S(1)} %collective-permute-done.4.refs_0_, bf16[128,512]{1,0:T(8,128)(2,1)S(1)} %collective-permute-done.5.refs_1_, ...), custom_call_target="tpu_custom_call" | custom-call | flops 939524096 | bytes 8519680 | tf_op jit(solution)/shard_map/project_first/pallas_call | solution.py:534
  112.8 1.7 collective-permute-start.8
  114.6 3.7 %project_out.1 = (bf16[64,3584]{1,0:T(8,128)(2,1)S(1)}, bf16[64,3584]{1,0:T(8,128)(2,1)S(1)}) custom-call(bf16[128,1024]{1,0:T(8,128)(2,1)S(1)} %get-tuple-element.72.rows_ref, bf16[1024,7168]{1,0:T(8,128)(2,1)} %weight_ref.3), custom_call_target="tpu_custom_call" | custom-call | flops 939524096 | bytes 8519680 | tf_op jit(solution)/shard_map/project_out/pallas_call | solution.py:565
  118.3 4.2 %collective-permute-start.11 = (bf16[64,3584]{1,0:T(8,128)(2,1)S(1)}, bf16[64,3584]{1,0:T(8,128)(2,1)S(1)}, u32[]{:S(2)}, u32[]{:S(2)}) collective-permute-start(bf16[64,3584]{1,0:T(8,128)(2,1)S(1)} %get-tuple-element.74), channel_id=1, source_target_pairs={{0,8},{4,12},{8,0},{12,4},{16,24},{20,28},{24,16},{28,20},{1,9},{5... | collective-permute-start | bytes 1376264 | tf_op jit(solution)/shard_map/ppermute | solution.py:740
  122.5 0.9 collective-permute-done.8.came_ref
  123.5 5.7 %collective-permute-start.9 = (bf16[32,3584]{1,0:T(8,128)(2,1)S(1)}, bf16[32,3584]{1,0:T(8,128)(2,1)S(1)}, u32[]{:S(2)}, u32[]{:S(2)}) collective-permute-start(bf16[32,3584]{1,0:T(8,128)(2,1)S(1)} %get-tuple-element.68), channel_id=1, source_target_pairs={{0,8},{4,12},{8,0},{12,4},{16,24},{20,28},{24,16},{28,20},{1,9},{5... | collective-permute-start | bytes 688136 | tf_op jit(solution)/shard_map/ppermute | solution.py:740
  129.2 4.4 %collective-permute-done.11.came_ref = bf16[64,3584]{1,0:T(8,128)(2,1)S(1)} collective-permute-done((bf16[64,3584]{1,0:T(8,128)(2,1)S(1)}, bf16[64,3584]{1,0:T(8,128)(2,1)S(1)}, u32[]{:S(2)}, u32[]{:S(2)}) %collective-permute-start.11) | collective-permute-done | bytes 458784 | tf_op jit(solution)/shard_map/ppermute | solution.py:740
  133.7 1.5 collective-permute-start.12
  135.2 0.8 collective-permute-done.9.came_ref
  136.1 4.0 %collective-permute-start.10 = (bf16[16,3584]{1,0:T(8,128)(2,1)S(1)}, bf16[16,3584]{1,0:T(8,128)(2,1)S(1)}, u32[]{:S(2)}, u32[]{:S(2)}) collective-permute-start(bf16[16,3584]{1,0:T(8,128)(2,1)S(1)} %get-tuple-element.70), channel_id=1, source_target_pairs={{0,16},{4,20},{8,24},{12,28},{16,0},{20,4},{24,8},{28,12},{1,17},{... | collective-permute-start | bytes 344072 | tf_op jit(solution)/shard_map/ppermute | solution.py:740
  140.1 2.9 %collective-permute-start.13 = (bf16[16,3584]{1,0:T(8,128)(2,1)S(1)}, bf16[16,3584]{1,0:T(8,128)(2,1)S(1)}, u32[]{:S(2)}, u32[]{:S(2)}) collective-permute-start(bf16[16,3584]{1,0:T(8,128)(2,1)S(1)} %get-tuple-element.78), channel_id=1, source_target_pairs={{0,16},{4,20},{8,24},{12,28},{16,0},{20,4},{24,8},{28,12},{1,17},{... | collective-permute-start | bytes 344072 | tf_op jit(solution)/shard_map/ppermute | solution.py:740
  143.1 4.8 %collective-permute-done.10.refs_0_ = bf16[16,3584]{1,0:T(8,128)(2,1)S(1)} collective-permute-done((bf16[16,3584]{1,0:T(8,128)(2,1)S(1)}, bf16[16,3584]{1,0:T(8,128)(2,1)S(1)}, u32[]{:S(2)}, u32[]{:S(2)}) %collective-permute-start.10) | collective-permute-done | bytes 114720 | tf_op jit(solution)/shard_map/ppermute | solution.py:740
  148.0 4.8 %collective-permute-done.13.refs_0_ = bf16[16,3584]{1,0:T(8,128)(2,1)S(1)} collective-permute-done((bf16[16,3584]{1,0:T(8,128)(2,1)S(1)}, bf16[16,3584]{1,0:T(8,128)(2,1)S(1)}, u32[]{:S(2)}, u32[]{:S(2)}) %collective-permute-start.13) | collective-permute-done | bytes 114720 | tf_op jit(solution)/shard_map/ppermute | solution.py:740
  153.0 1.8 collective-permute-done.17.refs_1_
  154.8 3.9 %collective-permute-done.14.refs_1_ = bf16[16,3584]{1,0:T(8,128)(2,1)S(1)} collective-permute-done((bf16[16,3584]{1,0:T(8,128)(2,1)S(1)}, bf16[16,3584]{1,0:T(8,128)(2,1)S(1)}, u32[]{:S(2)}, u32[]{:S(2)}) %collective-permute-start.14) | collective-permute-done | bytes 114720 | tf_op jit(solution)/shard_map/ppermute | solution.py:740
  158.8 1.0 collective-permute-start.15
  159.8 1.4 collective-permute-done.18.refs_2_
  161.2 2.7 %collective-permute-start.19 = (bf16[64,3584]{1,0:T(8,128)(2,1)S(1)}, bf16[64,3584]{1,0:T(8,128)(2,1)S(1)}, u32[]{:S(2)}, u32[]{:S(2)}) collective-permute-start(bf16[64,3584]{1,0:T(8,128)(2,1)S(1)} %pad_maximum_fusion.1), channel_id=1, source_target_pairs={{0,4},{4,0},{8,12},{12,8},{16,20},{20,16},{24,28},{28,24},{1,5},{5... | collective-permute-start | bytes 1376264 | tf_op jit(solution)/shard_map/ppermute | solution.py:740
  163.9 3.2 %collective-permute-done.15.refs_2_ = bf16[32,3584]{1,0:T(8,128)(2,1)S(1)} collective-permute-done((bf16[32,3584]{1,0:T(8,128)(2,1)S(1)}, bf16[32,3584]{1,0:T(8,128)(2,1)S(1)}, u32[]{:S(2)}, u32[]{:S(2)}) %collective-permute-start.15) | collective-permute-done | bytes 229408 | tf_op jit(solution)/shard_map/ppermute | solution.py:740
  167.3 3.6 %preload.3.refs_7_.refs_10_.weight_ref = bf16[1152,3584]{1,0:T(8,128)(2,1)S(1)} custom-call(bf16[16,3584]{1,0:T(8,128)(2,1)S(1)} %get-tuple-element.79._.refs_0_, bf16[1152,7168]{1,0:T(8,128)(2,1)} %weight_ref.5), custom_call_target="tpu_custom_call" | custom-call | bytes 8257536 | tf_op jit(solution)/shard_map/preload/pallas_call | solution.py:438
  170.9 3.8 %collective-permute-done.19.refs_3_ = bf16[64,3584]{1,0:T(8,128)(2,1)S(1)} collective-permute-done((bf16[64,3584]{1,0:T(8,128)(2,1)S(1)}, bf16[64,3584]{1,0:T(8,128)(2,1)S(1)}, u32[]{:S(2)}, u32[]{:S(2)}) %collective-permute-start.19) | collective-permute-done | bytes 458784 | tf_op jit(solution)/shard_map/ppermute | solution.py:740
  174.7 5.1 %gate_up.2 = (f32[128,1152]{1,0:T(8,128)S(1)}, f32[128,1152]{1,0:T(8,128)S(1)}, f32[128,128]{1,0:T(8,128)S(1)}) custom-call(bf16[16,3584]{1,0:T(8,128)(2,1)S(1)} %get-tuple-element.80.refs_0_, bf16[16,3584]{1,0:T(8,128)(2,1)S(1)} %collective-permute-done.17.refs_1_, bf16[32,3584]{1,0:T(8,128)(2,1)S(1)} %collective-permute-done.18.refs_2_, ...), custom_call_target="tpu_custom_call" | custom-call | flops 2113929216 | bytes 17432576 | tf_op jit(solution)/shard_map/gate_up/pallas_call | solution.py:688
  179.8 5.1 %gate_up.3.rows_ref = bf16[128,1152]{1,0:T(8,128)(2,1)S(1)} custom-call(bf16[16,3584]{1,0:T(8,128)(2,1)S(1)} %get-tuple-element.79._.refs_0_, bf16[16,3584]{1,0:T(8,128)(2,1)S(1)} %collective-permute-done.14.refs_1_, bf16[32,3584]{1,0:T(8,128)(2,1)S(1)} %collective-permute-done.15.refs_2_, bf16[64,3584]{1,0:T(8,128)(2,1)S(1)} %collective-permute-done.16.refs_3_, ...), custom_call_target="tpu_custom_call" | custom-call | flops 2113929216 | bytes 17432576 | tf_op jit(solution)/shard_map/gate_up/pallas_call | solution.py:688
  184.9 1.4 project_down.2
  186.3 1.0 collective-permute-start.20
  187.3 3.9 %project_down.3 = (bf16[64,3584]{1,0:T(8,128)(2,1)S(1)}, bf16[64,3584]{1,0:T(8,128)(2,1)S(1)}) custom-call(bf16[128,1152]{1,0:T(8,128)(2,1)S(1)} %gate_up.3.rows_ref, bf16[1152,7168]{1,0:T(8,128)(2,1)} %weight_ref.5), custom_call_target="tpu_custom_call" | custom-call | flops 1056964608 | bytes 9469952 | tf_op jit(solution)/shard_map/project_down/pallas_call | solution.py:565
  191.2 5.4 %collective-permute-done.20.came_ref = bf16[64,3584]{1,0:T(8,128)(2,1)S(1)} collective-permute-done((bf16[64,3584]{1,0:T(8,128)(2,1)S(1)}, bf16[64,3584]{1,0:T(8,128)(2,1)S(1)}, u32[]{:S(2)}, u32[]{:S(2)}) %collective-permute-start.20) | collective-permute-done | bytes 458784 | tf_op jit(solution)/shard_map/ppermute | solution.py:740
  196.8 7.4 %collective-permute-done.23.came_ref = bf16[64,3584]{1,0:T(8,128)(2,1)S(1)} collective-permute-done((bf16[64,3584]{1,0:T(8,128)(2,1)S(1)}, bf16[64,3584]{1,0:T(8,128)(2,1)S(1)}, u32[]{:S(2)}, u32[]{:S(2)}) %collective-permute-start.23) | collective-permute-done | bytes 458784 | tf_op jit(solution)/shard_map/ppermute | solution.py:740
  204.3 0.6 collective-permute-start.24
  204.9 1.8 collective-permute-done.21.came_ref
  206.8 3.6 %collective-permute-done.24.came_ref = bf16[32,3584]{1,0:T(8,128)(2,1)S(1)} collective-permute-done((bf16[32,3584]{1,0:T(8,128)(2,1)S(1)}, bf16[32,3584]{1,0:T(8,128)(2,1)S(1)}, u32[]{:S(2)}, u32[]{:S(2)}) %collective-permute-start.24) | collective-permute-done | bytes 229408 | tf_op jit(solution)/shard_map/ppermute | solution.py:740
  210.5 5.5 %collective-permute-done.22 = bf16[16,3584]{1,0:T(8,128)(2,1)S(1)} collective-permute-done((bf16[16,3584]{1,0:T(8,128)(2,1)S(1)}, bf16[16,3584]{1,0:T(8,128)(2,1)S(1)}, u32[]{:S(2)}, u32[]{:S(2)}) %collective-permute-start.22) | collective-permute-done | bytes 114720 | tf_op jit(solution)/shard_map/ppermute | solution.py:740
  216.1 1.2 collective-permute-done.25
  217.4 0.7 pad_maximum_fusion.4
  (70 shorter events, 2.0 us)
Async XLA Ops:
  0.0 0.7 copy-start.2
  0.7 0.7 copy-start.4
  6.1 67.4 %collective-permute-start = (bf16[5,288,128]{2,1,0:T(8,128)(2,1)}, bf16[5,288,128]{2,1,0:T(8,128)(2,1)S(1)}, u32[]{:S(2)}, u32[]{:S(2)}) collective-permute-start(bf16[5,288,128]{2,1,0:T(8,128)(2,1)} %get-tuple-element.51._), channel_id=1, source_target_pairs={{0,16},{4,20},{8,24},{12,28},{16,0},{20,4},{24,8},{28,12},{1,17},{... | collective-permute-start | bytes 1105928 | tf_op jit(solution)/shard_map/ppermute | solution.py:740
  14.3 9.6 %copy-start.3 = (s32[192]{0:T(256)S(1)}, s32[192]{0:T(256)}, u32[]{:S(2)}) copy-start(s32[192]{0:T(256)} %page_ref.3) | copy-start | bytes 2308
  14.3 10.2 %copy-start.5 = (s32[192,1]{0,1:T(1,128)S(1)}, s32[192,1]{0,1:T(1,128)}, u32[]{:S(2)}) copy-start(s32[192,1]{0,1:T(1,128)} %param.16) | copy-start | bytes 2308
  14.3 10.9 %copy-start.7 = (s32[192]{0:T(256)S(1)}, s32[192]{0:T(256)}, u32[]{:S(2)}) copy-start(s32[192]{0:T(256)} %param.18) | copy-start | bytes 2308
  14.3 11.4 %copy-start.6 = (s32[16,32]{1,0:T(8,128)S(1)}, s32[16,32]{1,0:T(8,128)}, u32[]{:S(2)}) copy-start(s32[16,32]{1,0:T(8,128)} %param.21) | copy-start | bytes 6148
  14.3 12.2 %copy-start.8 = (s32[16]{0:T(128)S(1)}, s32[16]{0:T(128)}, u32[]{:S(2)}) copy-start(s32[16]{0:T(128)} %param.20) | copy-start | bytes 196
  14.3 51.7 %all-to-all-start = ((bf16[4,5,288,128]{3,2,1,0:T(8,128)(2,1)}), bf16[4,5,288,128]{3,2,1,0:T(8,128)(2,1)S(1)}, u32[]{:S(2)}, u32[]{:S(2)}) async-start(bf16[4,5,288,128]{3,2,1,0:T(8,128)(2,1)} %pack_near.1), calls=%async_computation | async-start | bytes 2949120 | tf_op jit(solution)/shard_map/all_to_all | solution.py:745
  18.6 54.9 %collective-permute-start.1 = (bf16[5,288,128]{2,1,0:T(8,128)(2,1)}, bf16[5,288,128]{2,1,0:T(8,128)(2,1)S(1)}, u32[]{:S(2)}, u32[]{:S(2)}) collective-permute-start(bf16[5,288,128]{2,1,0:T(8,128)(2,1)} %get-tuple-element.52), channel_id=1, source_target_pairs={{0,20},{4,16},{8,28},{12,24},{16,4},{20,0},{24,12},{28,8},{1,21},{... | collective-permute-start | bytes 1105928 | tf_op jit(solution)/shard_map/ppermute | solution.py:740
  20.5 53.1 %collective-permute-start.2 = (bf16[5,288,128]{2,1,0:T(8,128)(2,1)}, bf16[5,288,128]{2,1,0:T(8,128)(2,1)}, u32[]{:S(2)}, u32[]{:S(2)}) collective-permute-start(bf16[5,288,128]{2,1,0:T(8,128)(2,1)} %get-tuple-element.53), channel_id=1, source_target_pairs={{0,24},{4,28},{8,16},{12,20},{16,8},{20,12},{24,0},{28,4},{1,25},{... | collective-permute-start | bytes 1105928 | tf_op jit(solution)/shard_map/ppermute | solution.py:740
  23.9 49.7 %collective-permute-start.3 = (bf16[5,288,128]{2,1,0:T(8,128)(2,1)}, bf16[5,288,128]{2,1,0:T(8,128)(2,1)}, u32[]{:S(2)}, u32[]{:S(2)}) collective-permute-start(bf16[5,288,128]{2,1,0:T(8,128)(2,1)} %get-tuple-element.54), channel_id=1, source_target_pairs={{0,28},{4,24},{8,20},{12,16},{16,12},{20,8},{24,4},{28,0},{1,29},{... | collective-permute-start | bytes 1105928 | tf_op jit(solution)/shard_map/ppermute | solution.py:740
  82.0 17.1 %all-to-all-start.1 = ((bf16[4,128,512]{2,1,0:T(8,128)(2,1)}), bf16[4,128,512]{2,1,0:T(8,128)(2,1)S(1)}, u32[]{:S(2)}, u32[]{:S(2)}) async-start(bf16[4,128,512]{2,1,0:T(8,128)(2,1)} %bitcast.43), calls=%async_computation.1 | async-start | bytes 1048576 | tf_op jit(solution)/shard_map/all_to_all | solution.py:745
  85.6 13.7 %collective-permute-start.4 = (bf16[128,512]{1,0:T(8,128)(2,1)S(1)}, bf16[128,512]{1,0:T(8,128)(2,1)S(1)}, u32[]{:S(2)}, u32[]{:S(2)}) collective-permute-start(bf16[128,512]{1,0:T(8,128)(2,1)S(1)} %get-tuple-element.61._), channel_id=1, source_target_pairs={{0,16},{4,20},{8,24},{12,28},{16,0},{20,4},{24,8},{28,12},{1,17},{... | collective-permute-start | bytes 393224 | tf_op jit(solution)/shard_map/ppermute | solution.py:740
  89.6 19.5 %collective-permute-start.5 = (bf16[128,512]{1,0:T(8,128)(2,1)S(1)}, bf16[128,512]{1,0:T(8,128)(2,1)S(1)}, u32[]{:S(2)}, u32[]{:S(2)}) collective-permute-start(bf16[128,512]{1,0:T(8,128)(2,1)S(1)} %get-tuple-element.62), channel_id=1, source_target_pairs={{0,20},{4,16},{8,28},{12,24},{16,4},{20,0},{24,12},{28,8},{1,21},{... | collective-permute-start | bytes 393224 | tf_op jit(solution)/shard_map/ppermute | solution.py:740
  90.8 18.3 %collective-permute-start.6 = (bf16[128,512]{1,0:T(8,128)(2,1)S(1)}, bf16[128,512]{1,0:T(8,128)(2,1)S(1)}, u32[]{:S(2)}, u32[]{:S(2)}) collective-permute-start(bf16[128,512]{1,0:T(8,128)(2,1)S(1)} %get-tuple-element.63), channel_id=1, source_target_pairs={{0,24},{4,28},{8,16},{12,20},{16,8},{20,12},{24,0},{28,4},{1,25},{... | collective-permute-start | bytes 393224 | tf_op jit(solution)/shard_map/ppermute | solution.py:740
  94.6 14.5 %collective-permute-start.7 = (bf16[128,512]{1,0:T(8,128)(2,1)S(1)}, bf16[128,512]{1,0:T(8,128)(2,1)S(1)}, u32[]{:S(2)}, u32[]{:S(2)}) collective-permute-start(bf16[128,512]{1,0:T(8,128)(2,1)S(1)} %get-tuple-element.64), channel_id=1, source_target_pairs={{0,28},{4,24},{8,20},{12,16},{16,12},{20,8},{24,4},{28,0},{1,29},{... | collective-permute-start | bytes 393224 | tf_op jit(solution)/shard_map/ppermute | solution.py:740
  112.8 10.5 %collective-permute-start.8 = (bf16[64,3584]{1,0:T(8,128)(2,1)S(1)}, bf16[64,3584]{1,0:T(8,128)(2,1)S(1)}, u32[]{:S(2)}, u32[]{:S(2)}) collective-permute-start(bf16[64,3584]{1,0:T(8,128)(2,1)S(1)} %get-tuple-element.66), channel_id=1, source_target_pairs={{0,4},{4,0},{8,12},{12,8},{16,20},{20,16},{24,28},{28,24},{1,5},{5... | collective-permute-start | bytes 1376264 | tf_op jit(solution)/shard_map/ppermute | solution.py:740
  114.6 60.2 %slice-start = ((s8[16515072]{0:T(1024)(128)(4,1)}), s8[4194304]{0:T(1024)(128)(4,1)S(1)}, s32[]{:S(2)}) async-start(s8[16515072]{0:T(1024)(128)(4,1)} %bitcast.31), calls=%async_computation.2 | async-start | bytes 8388608
  114.6 60.2 %slice-start.1 = ((s8[16515072]{0:T(1024)(128)(4,1)}), s8[4194304]{0:T(1024)(128)(4,1)S(1)}, s32[]{:S(2)}) async-start(s8[16515072]{0:T(1024)(128)(4,1)} %bitcast.31), calls=%async_computation.3 | async-start | bytes 8388608
  118.3 29.6 %copy-start = (bf16[16,7168]{1,0:T(8,128)(2,1)S(1)}, bf16[16,7168]{1,0:T(8,128)(2,1)}, u32[]{:S(2)}) copy-start(bf16[16,7168]{1,0:T(8,128)(2,1)} %residual_ref.3) | copy-start | bytes 688132
  118.3 29.6 %copy-start.1 = (f32[7168]{0:T(1024)S(1)}, f32[7168]{0:T(1024)}, u32[]{:S(2)}) copy-start(f32[7168]{0:T(1024)} %param.26) | copy-start | bytes 86020
  118.3 15.3 %collective-permute-start.11 = (bf16[64,3584]{1,0:T(8,128)(2,1)S(1)}, bf16[64,3584]{1,0:T(8,128)(2,1)S(1)}, u32[]{:S(2)}, u32[]{:S(2)}) collective-permute-start(bf16[64,3584]{1,0:T(8,128)(2,1)S(1)} %get-tuple-element.74), channel_id=1, source_target_pairs={{0,8},{4,12},{8,0},{12,4},{16,24},{20,28},{24,16},{28,20},{1,9},{5... | collective-permute-start | bytes 1376264 | tf_op jit(solution)/shard_map/ppermute | solution.py:740
  123.5 12.5 %collective-permute-start.9 = (bf16[32,3584]{1,0:T(8,128)(2,1)S(1)}, bf16[32,3584]{1,0:T(8,128)(2,1)S(1)}, u32[]{:S(2)}, u32[]{:S(2)}) collective-permute-start(bf16[32,3584]{1,0:T(8,128)(2,1)S(1)} %get-tuple-element.68), channel_id=1, source_target_pairs={{0,8},{4,12},{8,0},{12,4},{16,24},{20,28},{24,16},{28,20},{1,9},{5... | collective-permute-start | bytes 688136 | tf_op jit(solution)/shard_map/ppermute | solution.py:740
  133.7 6.4 %collective-permute-start.12 = (bf16[32,3584]{1,0:T(8,128)(2,1)S(1)}, bf16[32,3584]{1,0:T(8,128)(2,1)S(1)}, u32[]{:S(2)}, u32[]{:S(2)}) collective-permute-start(bf16[32,3584]{1,0:T(8,128)(2,1)S(1)} %get-tuple-element.76), channel_id=1, source_target_pairs={{0,4},{4,0},{8,12},{12,8},{16,20},{20,16},{24,28},{28,24},{1,5},{5... | collective-permute-start | bytes 688136 | tf_op jit(solution)/shard_map/ppermute | solution.py:740
  136.1 11.8 %collective-permute-start.10 = (bf16[16,3584]{1,0:T(8,128)(2,1)S(1)}, bf16[16,3584]{1,0:T(8,128)(2,1)S(1)}, u32[]{:S(2)}, u32[]{:S(2)}) collective-permute-start(bf16[16,3584]{1,0:T(8,128)(2,1)S(1)} %get-tuple-element.70), channel_id=1, source_target_pairs={{0,16},{4,20},{8,24},{12,28},{16,0},{20,4},{24,8},{28,12},{1,17},{... | collective-permute-start | bytes 344072 | tf_op jit(solution)/shard_map/ppermute | solution.py:740
  140.1 12.7 %collective-permute-start.13 = (bf16[16,3584]{1,0:T(8,128)(2,1)S(1)}, bf16[16,3584]{1,0:T(8,128)(2,1)S(1)}, u32[]{:S(2)}, u32[]{:S(2)}) collective-permute-start(bf16[16,3584]{1,0:T(8,128)(2,1)S(1)} %get-tuple-element.78), channel_id=1, source_target_pairs={{0,16},{4,20},{8,24},{12,28},{16,0},{20,4},{24,8},{28,12},{1,17},{... | collective-permute-start | bytes 344072 | tf_op jit(solution)/shard_map/ppermute | solution.py:740
  147.9 6.8 %collective-permute-start.17 = (bf16[16,3584]{1,0:T(8,128)(2,1)S(1)}, bf16[16,3584]{1,0:T(8,128)(2,1)S(1)}, u32[]{:S(2)}, u32[]{:S(2)}) collective-permute-start(bf16[16,3584]{1,0:T(8,128)(2,1)S(1)} %get-tuple-element.80.refs_0_), channel_id=1, source_target_pairs={{0,16},{4,20},{8,24},{12,28},{16,0},{20,4},{24,8},{28,12},{1,17},{... | collective-permute-start | bytes 344072 | tf_op jit(solution)/shard_map/ppermute | solution.py:740
  152.9 5.9 %collective-permute-start.14 = (bf16[16,3584]{1,0:T(8,128)(2,1)S(1)}, bf16[16,3584]{1,0:T(8,128)(2,1)S(1)}, u32[]{:S(2)}, u32[]{:S(2)}) collective-permute-start(bf16[16,3584]{1,0:T(8,128)(2,1)S(1)} %get-tuple-element.79._.refs_0_), channel_id=1, source_target_pairs={{0,16},{4,20},{8,24},{12,28},{16,0},{20,4},{24,8},{28,12},{1,17},{... | collective-permute-start | bytes 344072 | tf_op jit(solution)/shard_map/ppermute | solution.py:740
  154.8 6.4 %collective-permute-start.18 = (bf16[32,3584]{1,0:T(8,128)(2,1)S(1)}, bf16[32,3584]{1,0:T(8,128)(2,1)S(1)}, u32[]{:S(2)}, u32[]{:S(2)}) collective-permute-start(bf16[32,3584]{1,0:T(8,128)(2,1)S(1)} %pad_maximum_fusion.3), channel_id=1, source_target_pairs={{0,8},{4,12},{8,0},{12,4},{16,24},{20,28},{24,16},{28,20},{1,9},{5... | collective-permute-start | bytes 688136 | tf_op jit(solution)/shard_map/ppermute | solution.py:740
  158.8 8.3 %collective-permute-start.15 = (bf16[32,3584]{1,0:T(8,128)(2,1)S(1)}, bf16[32,3584]{1,0:T(8,128)(2,1)S(1)}, u32[]{:S(2)}, u32[]{:S(2)}) collective-permute-start(bf16[32,3584]{1,0:T(8,128)(2,1)S(1)} %pad_maximum_fusion.2), channel_id=1, source_target_pairs={{0,4},{4,0},{8,12},{12,8},{16,20},{20,16},{24,28},{28,24},{1,5},{5... | collective-permute-start | bytes 688136 | tf_op jit(solution)/shard_map/ppermute | solution.py:740
  161.2 13.5 %collective-permute-start.19 = (bf16[64,3584]{1,0:T(8,128)(2,1)S(1)}, bf16[64,3584]{1,0:T(8,128)(2,1)S(1)}, u32[]{:S(2)}, u32[]{:S(2)}) collective-permute-start(bf16[64,3584]{1,0:T(8,128)(2,1)S(1)} %pad_maximum_fusion.1), channel_id=1, source_target_pairs={{0,4},{4,0},{8,12},{12,8},{16,20},{20,16},{24,28},{28,24},{1,5},{5... | collective-permute-start | bytes 1376264 | tf_op jit(solution)/shard_map/ppermute | solution.py:740
  167.2 12.7 %collective-permute-start.16 = (bf16[64,3584]{1,0:T(8,128)(2,1)S(1)}, bf16[64,3584]{1,0:T(8,128)(2,1)S(1)}, u32[]{:S(2)}, u32[]{:S(2)}) collective-permute-start(bf16[64,3584]{1,0:T(8,128)(2,1)S(1)} %pad_maximum_fusion), channel_id=1, source_target_pairs={{0,8},{4,12},{8,0},{12,4},{16,24},{20,28},{24,16},{28,20},{1,9},{5... | collective-permute-start | bytes 1376264 | tf_op jit(solution)/shard_map/ppermute | solution.py:740
  167.3 7.5 %slice-start.2 = ((s8[16515072]{0:T(1024)(128)(4,1)}), s8[4194304]{0:T(1024)(128)(4,1)S(1)}, s32[]{:S(2)}) async-start(s8[16515072]{0:T(1024)(128)(4,1)} %bitcast.31), calls=%async_computation.4 | async-start | bytes 8388608
  167.3 7.4 %slice-start.3 = ((s8[16515072]{0:T(1024)(128)(4,1)}), s8[3932160]{0:T(1024)(128)(4,1)S(1)}, s32[]{:S(2)}) async-start(s8[16515072]{0:T(1024)(128)(4,1)} %bitcast.31), calls=%async_computation.5 | async-start | bytes 7864320
  186.3 10.3 %collective-permute-start.20 = (bf16[64,3584]{1,0:T(8,128)(2,1)S(1)}, bf16[64,3584]{1,0:T(8,128)(2,1)S(1)}, u32[]{:S(2)}, u32[]{:S(2)}) collective-permute-start(bf16[64,3584]{1,0:T(8,128)(2,1)S(1)} %get-tuple-element.85), channel_id=1, source_target_pairs={{0,4},{4,0},{8,12},{12,8},{16,20},{20,16},{24,28},{28,24},{1,5},{5... | collective-permute-start | bytes 1376264 | tf_op jit(solution)/shard_map/ppermute | solution.py:740
  191.2 13.1 %collective-permute-start.23 = (bf16[64,3584]{1,0:T(8,128)(2,1)S(1)}, bf16[64,3584]{1,0:T(8,128)(2,1)S(1)}, u32[]{:S(2)}, u32[]{:S(2)}) collective-permute-start(bf16[64,3584]{1,0:T(8,128)(2,1)S(1)} %get-tuple-element.92), channel_id=1, source_target_pairs={{0,8},{4,12},{8,0},{12,4},{16,24},{20,28},{24,16},{28,20},{1,9},{5... | collective-permute-start | bytes 1376264 | tf_op jit(solution)/shard_map/ppermute | solution.py:740
  196.7 10.0 %collective-permute-start.21 = (bf16[32,3584]{1,0:T(8,128)(2,1)S(1)}, bf16[32,3584]{1,0:T(8,128)(2,1)S(1)}, u32[]{:S(2)}, u32[]{:S(2)}) collective-permute-start(bf16[32,3584]{1,0:T(8,128)(2,1)S(1)} %get-tuple-element.87), channel_id=1, source_target_pairs={{0,8},{4,12},{8,0},{12,4},{16,24},{20,28},{24,16},{28,20},{1,9},{5... | collective-permute-start | bytes 688136 | tf_op jit(solution)/shard_map/ppermute | solution.py:740
  204.3 6.1 %collective-permute-start.24 = (bf16[32,3584]{1,0:T(8,128)(2,1)S(1)}, bf16[32,3584]{1,0:T(8,128)(2,1)S(1)}, u32[]{:S(2)}, u32[]{:S(2)}) collective-permute-start(bf16[32,3584]{1,0:T(8,128)(2,1)S(1)} %get-tuple-element.94), channel_id=1, source_target_pairs={{0,4},{4,0},{8,12},{12,8},{16,20},{20,16},{24,28},{28,24},{1,5},{5... | collective-permute-start | bytes 688136 | tf_op jit(solution)/shard_map/ppermute | solution.py:740
  206.7 9.4 %collective-permute-start.22 = (bf16[16,3584]{1,0:T(8,128)(2,1)S(1)}, bf16[16,3584]{1,0:T(8,128)(2,1)S(1)}, u32[]{:S(2)}, u32[]{:S(2)}) collective-permute-start(bf16[16,3584]{1,0:T(8,128)(2,1)S(1)} %get-tuple-element.89), channel_id=1, source_target_pairs={{0,16},{4,20},{8,24},{12,28},{16,0},{20,4},{24,8},{28,12},{1,17},{... | collective-permute-start | bytes 344072 | tf_op jit(solution)/shard_map/ppermute | solution.py:740
  210.5 6.9 %collective-permute-start.25 = (bf16[16,3584]{1,0:T(8,128)(2,1)S(1)}, bf16[16,3584]{1,0:T(8,128)(2,1)S(1)}, u32[]{:S(2)}, u32[]{:S(2)}) collective-permute-start(bf16[16,3584]{1,0:T(8,128)(2,1)S(1)} %get-tuple-element.96), channel_id=1, source_target_pairs={{0,16},{4,20},{8,24},{12,28},{16,0},{20,4},{24,8},{28,12},{1,17},{... | collective-permute-start | bytes 344072 | tf_op jit(solution)/shard_map/ppermute | solution.py:740
